TPU v7x, 32 devices: a whole 2x2x4 slice. The times are simulated.
32 devices in a mesh: dp: 2 (over x), ctx: 16 (over z, y, core).
Axes of the slice: x: 2, y: 2, z: 4, core: 2. Of those that a mesh axis runs over, the one named last changes fastest.
Arguments:
- tokens: bfloat16 [2, 2048, 1152], P('dp', 'ctx'), may hold values from -50 to 50
- cotangent: bfloat16 [2, 2048, 1152], P('dp', 'ctx'), may hold values from -45 to 45
- clip_frames: int32 [2, 8], P('dp'), may hold values from 1 to 8, as said below
- clip_offsets: int32 [2, 8], P('dp'), may hold values from 0 to 1920, as said below
- clip_heights: int32 [2, 8], P('dp'), may hold values from 8 to 16, as said below
- clip_widths: int32 [2, 8], P('dp'), may hold values from 4 to 8
- spatial_gain: float32 [1152], replicated, may hold values from 0.1 to 1.9
- spatial_qkv: bfloat16 [1728, 1152], P('ctx'), may hold values from -0.1875 to 0.1875
- spatial_out: bfloat16 [576, 1152], P('ctx'), may hold values from -0.25 to 0.25
- temporal_gain: float32 [1152], replicated, may hold values from 0.1 to 1.9
- temporal_qkv: bfloat16 [1728, 1152], P('ctx'), may hold values from -0.1875 to 0.1875
- temporal_out: bfloat16 [576, 1152], P('ctx'), may hold values from -0.25 to 0.25
Outputs:
- output: bfloat16 [2, 2048, 1152], P('dp', 'ctx')
- tokens_grad: bfloat16 [2, 2048, 1152], P('dp', 'ctx')
- gain_grads: float32 [2, 1152], replicated
Inputs may be any that keep to these rules, and one draw needn't show every extreme that they name: `clip_frames`: clip 0 of every bin starts at offset 0 and has exactly 8 frame tiles; every later clip starts after the one before it ends, and the last ends by tile 16. `clip_offsets`: offsets are multiples of 128 and rise from clip to clip; the last clip of every bin starts at tile 16 - 1. `clip_heights`: clip 0 of every bin has 16 rows and 8 columns; heights times widths never exceed 128.
All inputs are finite; a program needn't handle non-finite values.
Results may differ from a plain program's by a relative error of at most 0.024.
Values may be sent and summed in bfloat16 or wider, within the bound.
No kernel may reach another device: no remote copies, remote signals or barrier semaphores. Data moves between devices by JAX's collectives and lax.ppermute only.
A program may use at most 64 MiB of HBM per device.

v0:
```python
import functools
import math

import jax
import jax.numpy as jnp
from jax import lax
from jax.experimental import pallas as pl
from jax.experimental.pallas import tpu as pltpu
from jax.sharding import PartitionSpec as P

HEADS = 8
FRAME = 128
EPSILON = 1e-06
ROPE_BASE = 10000.0
MASKED = -1e30
F32 = jnp.float32
BF16 = jnp.bfloat16
VMEM_LIMIT = 12 * 1024 * 1024


def nn(a, b):
    return lax.dot_general(a, b, (((1,), (0,)), ((), ())), preferred_element_type=F32)


def nt(a, b):
    return lax.dot_general(a, b, (((1,), (1,)), ((), ())), preferred_element_type=F32)


def tn(a, b):
    return lax.dot_general(a, b, (((0,), (0,)), ((), ())), preferred_element_type=F32)


class Rows:
    def __init__(self, qkv_rows, out_rows, size):
        self.qkv, self.out = qkv_rows, out_rows
        self.shard = qkv_rows + out_rows
        self.total = self.shard * size
        self.inner = out_rows * size
        self.head = self.inner // HEADS
        cut = self.shard % 16 == 0
        self.qkv_cut = -(-qkv_rows // 16) * 16 if cut else self.shard
        self.out_cut = qkv_rows // 16 * 16 if cut else 0
        self.qkv_total = self.qkv_cut * size
        self.out_total = (self.shard - self.out_cut) * size

    def spans(self, first, count, per_shard, stride, shift):
        found = []
        row = first
        while row < first + count:
            block, inside = divmod(row, per_shard)
            length = min(per_shard - inside, first + count - row)
            place = block * stride + shift + inside
            if found and found[-1][0] + found[-1][1] == place:
                found[-1] = (found[-1][0], found[-1][1] + length)
            else:
                found.append((place, length))
            row += length
        return found

    def qkv_spans(self, which, head, stride):
        return self.spans(which * self.inner + head * self.head, self.head, self.qkv, stride, 0)

    def out_spans(self, head, cut):
        stride = self.shard - cut
        return self.spans(head * self.head, self.head, self.out, stride, self.qkv - cut)

    def qkv_weight(self, ref):
        if self.qkv_cut == self.shard:
            return ref[...].reshape(self.total, -1)
        return ref[:, : self.qkv_cut, :].reshape(self.qkv_total, -1)

    def out_weight(self, ref):
        if self.out_cut == 0:
            return ref[...].reshape(self.total, -1)
        return ref[:, self.out_cut :, :].reshape(self.out_total, -1)


def read_rows(ref, spans):
    parts = [ref[place : place + length, :] for place, length in spans]
    return parts[0] if len(parts) == 1 else jnp.concatenate(parts, axis=0)


def write_rows(ref, spans, value):
    done = 0
    for place, length in spans:
        ref[place : place + length, :] = value[done : done + length, :]
        done += length


def inverse_size(values):
    return lax.rsqrt(jnp.mean(values * values, axis=-1, keepdims=True) + EPSILON)


def norm_back(values, inverse, gain, grad):
    scaled = grad * gain
    middle = jnp.mean(scaled * values, axis=-1, keepdims=True)
    grad_values = inverse * scaled - values * (inverse * inverse * inverse * middle)
    grad_gain = jnp.sum(grad * (values * inverse), axis=0, keepdims=True)
    return grad_values, grad_gain


def shares_of(queries, keys, allowed, live, scale):
    scores = [tn(key, query) for key, query in zip(keys, queries)]
    weights = [jnp.exp(jnp.where(allowed, score * scale, MASKED)) for score in scores]
    totals = [jnp.sum(weight, axis=0, keepdims=True) + (1.0 - live) for weight in weights]
    return [weight * (1.0 / total) for weight, total in zip(weights, totals)]


def attend_back(queries, keys, values, shares, shares_low, grads, scale):
    grad_shares = [tn(value, grad) for value, grad in zip(values, grads)]
    middles = [jnp.sum(a * b, axis=0, keepdims=True) for a, b in zip(shares, grad_shares)]
    grad_scores = [
        (share * (grad_share - middle) * scale).astype(BF16)
        for share, grad_share, middle in zip(shares, grad_shares, middles)
    ]
    return (
        [nn(key, grad_score) for key, grad_score in zip(keys, grad_scores)],
        [nt(query, grad_score) for query, grad_score in zip(queries, grad_scores)],
        [nt(grad, share) for grad, share in zip(grads, shares_low)],
    )


def clips_at(clips, frames):
    counts, times, numbers = (jnp.zeros_like(frames) for _ in range(3))
    for clip in range(clips.shape[1]):
        start = clips[1, clip] // FRAME
        member = (frames >= start) & (frames < start + clips[0, clip])
        counts = jnp.where(member, clips[2, clip] * clips[3, clip], counts)
        times = jnp.where(member, frames - start, times)
        numbers = jnp.where(member, clip + 1, numbers)
    return counts, times, numbers


def ids(shape, dim):
    return lax.broadcasted_iota(jnp.int32, shape, dim)


def space_masks(clips):
    count = clips_at(clips, lax.axis_index("ctx").astype(jnp.int32))[0]
    return ids((FRAME, FRAME), 0) < count, (ids((1, FRAME), 1) < count).astype(F32)


def time_masks(clips, near, slots):
    rank = lax.axis_index("ctx")
    token = ids((1, FRAME), 1)
    slot = lax.rem(token, slots)
    counts, times, numbers = clips_at(clips, (rank // near) * near + token // slots)
    alive = lax.rem(rank, near) * slots + slot < counts
    group = (numbers * FRAME + slot).astype(F32)
    keys = jnp.where(alive, group, -1.0)
    allowed = jnp.broadcast_to(keys, (FRAME, FRAME)).T == group
    return allowed, alive.astype(F32), times.astype(F32)


def turn_tables(times, half):
    frequency = jnp.exp(ids((half, FRAME), 0).astype(F32) * (-math.log(ROPE_BASE) / half))
    angles = frequency * times
    cosine, sine = jnp.cos(angles), jnp.sin(angles)
    return jnp.concatenate([cosine, cosine], axis=0), jnp.concatenate([-sine, sine], axis=0)


def out_columns(rows):
    return lax.rem(ids((1, rows.total), 1), rows.shard) >= rows.qkv


def weight_copies(layout, order, pieces, target, sems, which):
    count = target.shape[1]
    return [
        pltpu.make_async_copy(
            pieces[piece].at[pl.ds(first, count)], target.at[order[index]], sems.at[which, index]
        )
        for index, (piece, first) in enumerate(layout)
    ]


def gate(rows, *events, others=()):
    anywhere = pl.BlockSpec(memory_space=pl.ANY)
    arrays = (rows, *others)
    count = len(arrays)
    results = pl.pallas_call(
        lambda *refs: None,
        out_shape=tuple(jax.ShapeDtypeStruct(array.shape, array.dtype) for array in arrays),
        in_specs=[anywhere] * (count + len(events)),
        out_specs=(anywhere,) * count,
        input_output_aliases={index: index for index in range(count)},
        compiler_params=pltpu.CompilerParams(vmem_limit_bytes=1024 * 1024),
    )(*arrays, *events)
    return results if others else results[0]


def start_weights(layouts, order, pieces, space, time, sems):
    def start(first, second):
        for copy in weight_copies(first, order, pieces, space, sems, 0):
            copy.start()
        for copy in weight_copies(second, order, pieces, time, sems, 1):
            copy.start()

    plane = order[len(layouts[0])]

    @pl.when(plane == 0)
    def _():
        start(layouts[0], layouts[1])

    @pl.when(plane != 0)
    def _():
        start(layouts[1], layouts[0])


def wait_weights(layouts, order, pieces, target, sems, which):
    for copy in weight_copies(layouts[0], order, pieces, target, sems, which):
        copy.wait()


def give(direct, stage, outs):
    if not direct:
        outs[0][...] = stage[...]
        return
    core = lax.rem(lax.axis_index("ctx"), 2)
    length = FRAME // (2 * direct)
    for chip in range(direct):
        for out, to in zip(outs, (core, 1 - core)):
            source = pl.ds(pl.multiple_of((2 * chip + to) * length, 16), length)
            out[chip * length : (chip + 1) * length, :] = stage[source, :]


def join(direct, own, from_twin, *outs):
    rank = lax.axis_index("ctx")
    core, chip = lax.rem(rank, 2), lax.rem(rank // 2, direct)
    length = own.shape[0] // direct
    for distance, out in enumerate(outs):
        source = pl.ds(pl.multiple_of((chip ^ distance) * length, 16), length)
        out[pl.ds(pl.multiple_of(core * length, 16), length), :] = own[source, :]
        out[pl.ds(pl.multiple_of((1 - core) * length, 16), length), :] = from_twin[source, :]


def collect(direct, arrived, stage):
    if not direct:
        return arrived[0]
    chip = lax.rem(lax.axis_index("ctx") // 2, direct)
    length = arrived[0].shape[0]
    for distance, part in enumerate(arrived):
        target = pl.ds(pl.multiple_of((chip ^ distance) * length, 16), length)
        stage[target, :] = part[...]
    return stage


def front(rows, layouts, order_of, direct, clips, tokens, gains, *refs):
    sends = 2 if direct else 1
    pieces, refs = refs[: -9 - sends], refs[-9 - sends :]
    hidden, saved, shares_out, space, time = refs[:5]
    project, mixed, stage, sems = refs[-4:]
    order = order_of()
    start_weights(layouts, order, pieces, space, time, sems)
    allowed, live = space_masks(clips)
    values = tokens[0].astype(F32)
    normed = (values * inverse_size(values) * gains[:1]).astype(BF16)
    mixed[...] = jnp.zeros_like(mixed)
    stride = rows.qkv_cut
    length = stride if len(layouts[0]) > 1 else rows.total

    def project_from(layout):
        for index, (piece, first) in enumerate(layout):
            target = pl.ds(pl.multiple_of(order[index] * length, 16), length)
            project[target, :] = nt(pieces[piece][first : first + length, :], normed)

    pl.when(order[-1] == 0)(lambda: project_from(layouts[0]))
    pl.when(order[-1] != 0)(lambda: project_from(layouts[1]))
    saved[...] = project[...].astype(BF16)
    scale = rows.head ** (-0.5)
    queries, keys, values_in = (
        [read_rows(project, rows.qkv_spans(which, head, stride)).astype(BF16) for head in range(HEADS)]
        for which in range(3)
    )
    shares = [share.astype(BF16) for share in shares_of(queries, keys, allowed, live, scale)]
    blended = [nn(value, share) * live for value, share in zip(values_in, shares)]
    for head in range(HEADS):
        shares_out[head] = shares[head]
        write_rows(mixed, rows.out_spans(head, rows.out_cut), blended[head])
    wait_weights(layouts, order, pieces, space, sems, 0)
    update = tn(mixed[...].astype(BF16), rows.out_weight(space))
    low = (values + update).astype(BF16)
    hidden[...] = low
    values = low.astype(F32)
    normed = (values * inverse_size(values) * gains[1:]).astype(BF16)
    wait_weights(layouts, order, pieces, time, sems, 1)
    both = nt(jnp.concatenate([normed, tokens[1]], axis=0), time[...].reshape(rows.total, -1))
    count = values.shape[0]
    stage[...] = jnp.where(out_columns(rows), both[count:], both[:count]).astype(BF16)
    give(direct, stage, refs[5:-4])


def time_core(rows, near, slots, direct, clips, *refs):
    project, result, stage = refs[-3:]
    arrived = collect(direct, refs[: direct or 1], stage)
    allowed, live, times = time_masks(clips, near, slots)
    for first in range(0, rows.total, FRAME):
        project[first : first + FRAME, :] = arrived[:, first : first + FRAME].astype(F32).T
    scale = rows.head ** (-0.5)
    half = rows.head // 2
    cosine, sine = turn_tables(times, half)

    def swapped(vectors):
        return jnp.concatenate([vectors[half:], vectors[:half]], axis=0)

    heads = range(HEADS)
    turned = []
    for which in range(2):
        vectors = [read_rows(project, rows.qkv_spans(which, head, rows.shard)) for head in heads]
        turned.append([(part * cosine + swapped(part) * sine).astype(BF16) for part in vectors])
    queries, keys = turned
    values = [read_rows(project, rows.qkv_spans(2, head, rows.shard)).astype(BF16) for head in heads]
    grads = [(read_rows(project, rows.out_spans(head, 0)) * live).astype(BF16) for head in heads]
    shares = shares_of(queries, keys, allowed, live, scale)
    shares_low = [share.astype(BF16) for share in shares]
    blended = [nn(value, share) * live for value, share in zip(values, shares_low)]
    parts = attend_back(queries, keys, values, shares, shares_low, grads, scale)
    for head in heads:
        write_rows(result, rows.out_spans(head, 0), blended[head])
        for which in range(2):
            turned_grad = parts[which][head].astype(BF16).astype(F32)
            write_rows(
                result,
                rows.qkv_spans(which, head, rows.shard),
                turned_grad * cosine - swapped(turned_grad) * sine,
            )
        write_rows(result, rows.qkv_spans(2, head, rows.shard), parts[2][head])
    for first in range(0, rows.total, FRAME):
        stage[:, first : first + FRAME] = result[first : first + FRAME, :].T.astype(BF16)
    give(direct, stage, refs[direct or 1 : -3])


def time_back(rows, direct, clips, *refs):
    arrived, refs = refs[: direct or 1], refs[direct or 1 :]
    tokens, gains, time, space, hidden, saved, shares_in = refs[:7]
    grad_hidden_out, grad_normed_out, gain_parts, project, grad_project, stage = refs[7:]
    arrived = collect(direct, arrived, stage)
    live = space_masks(clips)[1]
    received = arrived[...]
    mask = jnp.broadcast_to(out_columns(rows), received.shape)
    left = jnp.where(mask, jnp.zeros_like(received), received)
    grad_normed = nn(left, time[...].reshape(rows.total, -1)).astype(BF16).astype(F32)
    values = hidden[...].astype(F32)
    grad_front, grad_time_gain = norm_back(values, inverse_size(values), gains[1:], grad_normed)
    grad_hidden = (tokens[1].astype(F32) + grad_front).astype(BF16)
    grad_hidden_out[...] = grad_hidden

    project[...] = nt(rows.out_weight(space), grad_hidden)
    grad_project[...] = jnp.zeros_like(grad_project)
    scale = rows.head ** (-0.5)
    heads = range(HEADS)
    spans = [[rows.qkv_spans(which, head, rows.qkv_cut) for head in heads] for which in range(3)]
    queries, keys, values_in = (
        [read_rows(saved, where).astype(BF16) for where in places] for places in spans
    )
    grads = [
        (read_rows(project, rows.out_spans(head, rows.out_cut)) * live).astype(BF16) for head in heads
    ]
    shares_low = [shares_in[head] for head in heads]
    shares = [share.astype(F32) for share in shares_low]
    parts = attend_back(queries, keys, values_in, shares, shares_low, grads, scale)
    for places, found in zip(spans, parts):
        for where, part in zip(places, found):
            write_rows(grad_project, where, part)
    grad_normed = tn(grad_project[...].astype(BF16), rows.qkv_weight(space)).astype(BF16)
    grad_normed_out[...] = grad_normed
    values = tokens[0].astype(F32)
    normed = values * inverse_size(values)
    grad_space_gain = jnp.sum(grad_normed.astype(F32) * normed, axis=0, keepdims=True)
    both_gains = jnp.concatenate([grad_space_gain, grad_time_gain], axis=0).astype(gain_parts.dtype)
    gain_parts[...] = jnp.broadcast_to(both_gains[None], gain_parts.shape)


def finish(rows, direct, *refs):
    arrived, refs = refs[: direct or 1], refs[direct or 1 :]
    tokens, gains, time, hidden, grad_hidden, grad_normed, output, grad_tokens, stage = refs
    received = collect(direct, arrived, stage)[...]
    mask = jnp.broadcast_to(out_columns(rows), received.shape)
    left = jnp.where(mask, received, jnp.zeros_like(received))
    update = nn(left, time[...].reshape(rows.total, -1))
    output[...] = (hidden[...].astype(F32) + update).astype(BF16)
    values = tokens[0].astype(F32)
    grad = grad_normed[...].astype(F32)
    grad_values, _ = norm_back(values, inverse_size(values), gains[:1], grad)
    grad_tokens[...] = (grad_hidden[...].astype(F32) + grad_values).astype(BF16)


def call(body, out_shapes, scratch, clips, operands):
    clips = () if clips is None else (clips,)
    whole = pl.BlockSpec(memory_space=pltpu.VMEM)
    scalars = pl.BlockSpec(memory_space=pltpu.SMEM)
    return pl.pallas_call(
        body,
        out_shape=out_shapes,
        in_specs=[scalars] * len(clips) + [whole] * len(operands),
        out_specs=jax.tree.map(lambda _: whole, out_shapes),
        scratch_shapes=scratch,
        compiler_params=pltpu.CompilerParams(vmem_limit_bytes=VMEM_LIMIT),
    )(*clips, *operands)


def gather_ring(space_rows, time_rows, size, others):
    chips = size // 2
    chain = chips // 2
    shard = space_rows.shape[0]

    def chip_at(place):
        place = place % chips
        return 2 * place if place < chain else 2 * (chips - 1 - place) + 1

    ring_pairs = []
    for place in range(chips):
        ring_pairs.append((2 * chip_at(place), 2 * chip_at(place + 1)))
        ring_pairs.append((2 * chip_at(place) + 1, 2 * chip_at(place - 1) + 1))
    planes = lax.axis_size("dp")
    plane = lax.rem(lax.axis_index("dp"), 2)

    def ring(rows):
        return lax.ppermute(rows, "ctx", ring_pairs)

    def across(rows):
        return lax.ppermute(rows, "dp", [(index, index ^ 1) for index in range(planes)])

    def twin(rows):
        return lax.ppermute(rows, "ctx", [(index, index ^ 1) for index in range(size)])

    own = jnp.where(plane == 0, space_rows, time_rows)
    own_other = jnp.where(plane == 0, time_rows, space_rows)
    t0 = twin(own)
    o1 = ring(own)
    t1 = ring(t0)
    t0_other = twin(own_other)
    o2 = ring(o1)
    x_o1 = across(o1)
    o1_twin = twin(o1)
    o2 = gate(o2, t1, o1_twin, t0_other)
    t2 = ring(t1)
    x_o1_twin = twin(x_o1)
    x_t1 = across(t1)
    t1_twin = twin(t1)
    t2 = gate(t2, o2, t1_twin)
    o3 = ring(o2)
    o3 = gate(o3, t2, x_o1)
    o2_twin = twin(o2)
    t3 = ring(t2)
    t2_twin = twin(t2)
    x_t1, *others = gate(x_t1, t3, x_o1_twin, t2_twin, others=others)
    o4 = ring(o3)
    o4 = gate(o4, x_t1, t3)
    x_o3 = across(o3)
    o3_twin = twin(o3)
    x_o2 = ring(x_o1)
    t3_twin = twin(t3)
    x_t1_twin = twin(x_t1)
    x_t2 = ring(x_t1)
    x_o4 = across(o4)
    o4_twin = twin(o4)
    x_t2 = gate(x_t2, o4_twin, t3_twin, x_o3, x_o2)
    x_t3 = ring(x_t2)
    x_o2_twin = twin(x_o2)
    x_t2_twin = twin(x_t2)
    x_o3_twin = twin(x_o3)
    x_o4_twin = twin(x_o4)
    x_t3_twin = twin(x_t3)
    mine = {"o0": (own, 0), "t0": (t0, 0)}
    other = {"o0": (own_other, 0), "t0": (t0_other, 0)}
    mine |= {"o1": (o1, 0), "o1_twin": (o1_twin, 0)}
    other |= {"o1": (x_o1, 0), "o1_twin": (x_o1_twin, 0)}
    mine |= {"t1": (t1, 0), "t1_twin": (t1_twin, 0)}
    other |= {"t1": (x_t1, 0), "t1_twin": (x_t1_twin, 0)}
    mine |= {"o2": (o2, 0), "o2_twin": (o2_twin, 0)}
    other |= {"o2": (x_o2, 0), "o2_twin": (x_o2_twin, 0)}
    mine |= {"t2": (t2, 0), "t2_twin": (t2_twin, 0)}
    other |= {"t2": (x_t2, 0), "t2_twin": (x_t2_twin, 0)}
    mine |= {"o3": (o3, 0), "o3_twin": (o3_twin, 0)}
    other |= {"o3": (x_o3, 0), "o3_twin": (x_o3_twin, 0)}
    mine |= {"t3": (t3, 0), "t3_twin": (t3_twin, 0)}
    other |= {"t3": (x_t3, 0), "t3_twin": (x_t3_twin, 0)}
    mine |= {"o4": (o4, 0), "o4_twin": (o4_twin, 0)}
    other |= {"o4": (x_o4, 0), "o4_twin": (x_o4_twin, 0)}
    names = ["o0", "t0", "o1", "o2", "o3", "o4", "t1", "t2", "t3"]
    twins = names[2:]

    def order_of():
        rank = lax.axis_index("ctx")
        chip, core = rank // 2, lax.rem(rank, 2)
        column, level = lax.rem(chip, 2), chip // 2
        place = jnp.where(column == 0, level, chips - 1 - level)

        def came(carrier, name):
            steps, shard_core = int(name[1]), carrier if name[0] == "o" else 1 - carrier
            at = lax.rem(place + steps * (2 * carrier - 1) + chips, chips)
            return 2 * jnp.where(at < chain, 2 * at, 2 * (chips - 1 - at) + 1) + shard_core

        order = [came(core, name) for name in names] + [came(1 - core, name) for name in twins]
        return order + [lax.rem(lax.axis_index("dp"), 2)]

    pieces, layouts = [], ([], [])
    for half, found in enumerate((mine, other)):
        for name in names + [name + "_twin" for name in twins]:
            array, first = found[name]
            place_in = [index for index, piece in enumerate(pieces) if piece is array]
            if not place_in:
                place_in = [len(pieces)]
                pieces.append(array)
            layouts[half].append((place_in[0], first * shard))
    return pieces, layouts, order_of, others


def gather_weights(space_rows, time_rows, size, others):
    if size == 16 and lax.axis_size("dp") % 2 == 0:
        return gather_ring(space_rows, time_rows, size, others)
    shard, features = space_rows.shape
    gathered = lax.all_gather(jnp.concatenate([space_rows, time_rows], axis=0), "ctx", axis=0)
    gathered = gathered.reshape(size, 2, shard, features)
    halves = [gathered[:, half].reshape(size * shard, features) for half in range(2)]
    return halves, ([(0, 0)], [(1, 0)]), lambda: [0, 0], others


def shards(
    tokens,
    cotangent,
    clip_frames,
    clip_offsets,
    clip_heights,
    clip_widths,
    spatial_gain,
    spatial_qkv,
    spatial_out,
    temporal_gain,
    temporal_qkv,
    temporal_out,
):
    size = lax.axis_size("ctx")
    everyone = lax.axis_size("dp") * size
    count, features = tokens.shape[1], tokens.shape[2]
    assert count == FRAME and FRAME % size == 0
    near = size // 2
    slots = FRAME // near
    rows = Rows(spatial_qkv.shape[0], spatial_out.shape[0], size)
    both_tokens = jnp.concatenate([tokens, cotangent], axis=0)
    both_gains = jnp.stack([spatial_gain, temporal_gain])
    clips = jnp.concatenate([clip_frames, clip_offsets, clip_heights, clip_widths], axis=0)
    pieces, layouts, order_of, others = gather_weights(
        jnp.concatenate([spatial_qkv, spatial_out], axis=0),
        jnp.concatenate([temporal_qkv, temporal_out], axis=0),
        size,
        (both_tokens, both_gains, clips),
    )
    both_tokens, both_gains, clips = others
    wide = pltpu.VMEM((rows.total, FRAME), F32)
    qkv_wide = pltpu.VMEM((rows.qkv_total, FRAME), F32)
    out_wide = pltpu.VMEM((rows.out_total, FRAME), F32)
    blocks = len(layouts[0])
    sems = pltpu.SemaphoreType.DMA((2, blocks))
    weight_shape = jax.ShapeDtypeStruct((blocks, rows.total // blocks, features), BF16)
    groups = [list(range(first, first + near)) for first in range(0, size, near)]

    direct = 4 if near == 8 and slots % 16 == 0 else 0
    part = jax.ShapeDtypeStruct((FRAME // 2 if direct else FRAME, rows.total), BF16)
    parts = (part,) * (2 if direct else 1)
    stage = pltpu.VMEM((FRAME, rows.total), BF16)

    def exchange(sent):
        if not direct:
            arrived = lax.all_to_all(
                sent[0].reshape(near, slots, rows.total),
                "ctx",
                split_axis=0,
                concat_axis=0,
                axis_index_groups=groups,
                tiled=True,
            )
            return [arrived.reshape(FRAME, rows.total)]
        own, to_twin = sent
        from_twin = lax.ppermute(to_twin, "ctx", [(index, index ^ 1) for index in range(size)])
        joined = jax.ShapeDtypeStruct((2 * slots, rows.total), BF16)
        here, *away = call(
            functools.partial(join, direct), (joined,) * direct, [], None, (own, from_twin)
        )
        return [here] + [
            lax.ppermute(rows_away, "ctx", [(index, index ^ (2 * distance)) for index in range(size)])
            for distance, rows_away in list(enumerate(away, 1))[::-1]
        ][::-1]

    hidden, saved, shares, space_weights, time_weights, *sent = call(
        functools.partial(front, rows, layouts, order_of, direct),
        (
            jax.ShapeDtypeStruct((FRAME, features), BF16),
            jax.ShapeDtypeStruct((rows.qkv_total, FRAME), BF16),
            jax.ShapeDtypeStruct((HEADS, FRAME, FRAME), BF16),
            weight_shape,
            weight_shape,
            *parts,
        ),
        [qkv_wide, out_wide, stage, sems],
        clips,
        (both_tokens, both_gains, *pieces),
    )
    arrived = exchange(sent)
    sent = call(
        functools.partial(time_core, rows, near, slots, direct),
        parts,
        [wide, wide, stage],
        clips,
        arrived,
    )
    arrived = exchange(sent)
    whole = jax.ShapeDtypeStruct((FRAME, features), BF16)
    grad_hidden, grad_normed, gains = call(
        functools.partial(time_back, rows, direct),
        (whole, whole, jax.ShapeDtypeStruct((everyone, 2, features), BF16)),
        [out_wide, qkv_wide, stage],
        clips,
        (*arrived, both_tokens, both_gains, time_weights, space_weights, hidden, saved, shares),
    )
    gains = lax.all_to_all(gains, ("dp", "ctx"), split_axis=0, concat_axis=0, tiled=True)
    result, grad_tokens = call(
        functools.partial(finish, rows, direct),
        (whole, whole),
        [stage],
        None,
        (*arrived, both_tokens, both_gains, time_weights, hidden, grad_hidden, grad_normed),
    )
    gain_grads = jnp.sum(gains.astype(F32), axis=0) * (1.0 / math.sqrt(everyone * FRAME))
    return result[None], grad_tokens[None], gain_grads


def solution(mesh):
    return jax.shard_map(
        shards,
        mesh=mesh,
        in_specs=(
            P("dp", "ctx", None),
            P("dp", "ctx", None),
            P("dp", None),
            P("dp", None),
            P("dp", None),
            P("dp", None),
            P(),
            P("ctx", None),
            P("ctx", None),
            P(),
            P("ctx", None),
            P("ctx", None),
        ),
        out_specs=(P("dp", "ctx", None), P("dp", "ctx", None), P()),
        check_vma=False,
    )
```

profile of v0, /device:TPU:0, one launch (start us, length us, event | category | flops | bytes accessed | tf_op | source)
XLA Modules:
  0.0 106.9 jit_solution(12225356914135767980)
XLA Ops:
  2.6 2.6 %collective-permute-start.4 = (bf16[144,1152]{1,0:T(8,128)(2,1)S(1)}, bf16[144,1152]{1,0:T(8,128)(2,1)S(1)}, u32[]{:S(2)}, u32[]{:S(2)}) collective-permute-start(bf16[144,1152]{1,0:T(8,128)(2,1)S(1)} %get-tuple-element.56.refs_0_), channel_id=1, source_target_pairs={{0,4},{1,3},{4,8},{5,1},{8,12},{9,5},{12,14},{13,9},{14,10},{15,13... | collective-permute-start | bytes 995336 | tf_op jit(solution)/shard_map/ppermute | solution.py:418
  5.2 1.6 %collective-permute-start.1 = (bf16[144,1152]{1,0:T(8,128)(2,1)S(1)}, bf16[144,1152]{1,0:T(8,128)(2,1)S(1)}, u32[]{:S(2)}, u32[]{:S(2)}) collective-permute-start(bf16[144,1152]{1,0:T(8,128)(2,1)S(1)} %collective-permute-done.refs_1_), channel_id=1, source_target_pairs={{0,4},{1,3},{4,8},{5,1},{8,12},{9,5},{12,14},{13,9},{14,10},{15,13... | collective-permute-start | bytes 995336 | tf_op jit(solution)/shard_map/ppermute | solution.py:418
  6.8 3.5 %collective-permute-done.4.refs_2_ = bf16[144,1152]{1,0:T(8,128)(2,1)S(1)} collective-permute-done((bf16[144,1152]{1,0:T(8,128)(2,1)S(1)}, bf16[144,1152]{1,0:T(8,128)(2,1)S(1)}, u32[]{:S(2)}, u32[]{:S(2)}) %collective-permute-start.4) | collective-permute-done | bytes 331808 | tf_op jit(solution)/shard_map/ppermute | solution.py:418
  10.3 2.1 %collective-permute-start.5 = (bf16[144,1152]{1,0:T(8,128)(2,1)S(1)}, bf16[144,1152]{1,0:T(8,128)(2,1)S(1)}, u32[]{:S(2)}, u32[]{:S(2)}) collective-permute-start(bf16[144,1152]{1,0:T(8,128)(2,1)S(1)} %collective-permute-done.4.refs_2_), channel_id=1, source_target_pairs={{0,4},{1,3},{4,8},{5,1},{8,12},{9,5},{12,14},{13,9},{14,10},{15,13... | collective-permute-start | bytes 995336 | tf_op jit(solution)/shard_map/ppermute | solution.py:418
  13.9 2.1 %collective-permute-start.3 = (bf16[144,1152]{1,0:T(8,128)(2,1)S(1)}, bf16[144,1152]{1,0:T(8,128)(2,1)S(1)}, u32[]{:S(2)}, u32[]{:S(2)}) collective-permute-start(bf16[144,1152]{1,0:T(8,128)(2,1)S(1)} %collective-permute-done.1.refs_1_.refs_6_), channel_id=1, source_target_pairs={{0,4},{1,3},{4,8},{5,1},{8,12},{9,5},{12,14},{13,9},{14,10},{15,13... | collective-permute-start | bytes 995336 | tf_op jit(solution)/shard_map/ppermute | solution.py:418
  17.4 2.1 %collective-permute-start.13 = (bf16[144,1152]{1,0:T(8,128)(2,1)S(1)}, bf16[144,1152]{1,0:T(8,128)(2,1)S(1)}, u32[]{:S(2)}, u32[]{:S(2)}) collective-permute-start(bf16[144,1152]{1,0:T(8,128)(2,1)S(1)} %shard_map.139.refs_1_.refs_3_), channel_id=1, source_target_pairs={{0,4},{1,3},{4,8},{5,1},{8,12},{9,5},{12,14},{13,9},{14,10},{15,13... | collective-permute-start | bytes 995336 | tf_op jit(solution)/shard_map/ppermute | solution.py:418
  20.9 1.6 %collective-permute-start.2 = (bf16[144,1152]{1,0:T(8,128)(2,1)S(1)}, bf16[144,1152]{1,0:T(8,128)(2,1)S(1)}, u32[]{:S(2)}, u32[]{:S(2)}) collective-permute-start(bf16[144,1152]{1,0:T(8,128)(2,1)S(1)} %collective-permute-done.1.refs_1_.refs_6_), channel_id=1, source_target_pairs={{0,16},{16,0},{1,17},{17,1},{2,18},{18,2},{3,19},{19,3},{4,20},{20... | collective-permute-start | bytes 995336 | tf_op jit(solution)/shard_map/ppermute | solution.py:421
  23.0 1.6 %collective-permute-start.9 = (bf16[144,1152]{1,0:T(8,128)(2,1)S(1)}, bf16[144,1152]{1,0:T(8,128)(2,1)S(1)}, u32[]{:S(2)}, u32[]{:S(2)}) collective-permute-start(bf16[144,1152]{1,0:T(8,128)(2,1)S(1)} %shard_map.140.refs_1_.refs_7_), channel_id=1, source_target_pairs={{0,4},{1,3},{4,8},{5,1},{8,12},{9,5},{12,14},{13,9},{14,10},{15,13... | collective-permute-start | bytes 995336 | tf_op jit(solution)/shard_map/ppermute | solution.py:418
  24.6 2.0 %collective-permute-start.14 = (bf16[144,1152]{1,0:T(8,128)(2,1)S(1)}, bf16[144,1152]{1,0:T(8,128)(2,1)S(1)}, u32[]{:S(2)}, u32[]{:S(2)}) collective-permute-start(bf16[144,1152]{1,0:T(8,128)(2,1)S(1)} %shard_map.142.refs_4_), channel_id=1, source_target_pairs={{0,4},{1,3},{4,8},{5,1},{8,12},{9,5},{12,14},{13,9},{14,10},{15,13... | collective-permute-start | bytes 995336 | tf_op jit(solution)/shard_map/ppermute | solution.py:418
  26.7 1.6 %collective-permute-start.19 = (bf16[144,1152]{1,0:T(8,128)(2,1)S(1)}, bf16[144,1152]{1,0:T(8,128)(2,1)S(1)}, u32[]{:S(2)}, u32[]{:S(2)}) collective-permute-start(bf16[144,1152]{1,0:T(8,128)(2,1)S(1)} %collective-permute-done.10.refs_2_.refs_18_), channel_id=1, source_target_pairs={{0,4},{1,3},{4,8},{5,1},{8,12},{9,5},{12,14},{13,9},{14,10},{15,13... | collective-permute-start | bytes 995336 | tf_op jit(solution)/shard_map/ppermute | solution.py:418
  28.4 1.6 %collective-permute-done.2.refs_0_ = bf16[144,1152]{1,0:T(8,128)(2,1)S(1)} collective-permute-done((bf16[144,1152]{1,0:T(8,128)(2,1)S(1)}, bf16[144,1152]{1,0:T(8,128)(2,1)S(1)}, u32[]{:S(2)}, u32[]{:S(2)}) %collective-permute-start.2) | collective-permute-done | bytes 331808 | tf_op jit(solution)/shard_map/ppermute | solution.py:421
  31.5 2.2 %collective-permute-done.14.refs_0_ = bf16[144,1152]{1,0:T(8,128)(2,1)S(1)} collective-permute-done((bf16[144,1152]{1,0:T(8,128)(2,1)S(1)}, bf16[144,1152]{1,0:T(8,128)(2,1)S(1)}, u32[]{:S(2)}, u32[]{:S(2)}) %collective-permute-start.14) | collective-permute-done | bytes 331808 | tf_op jit(solution)/shard_map/ppermute | solution.py:418
  33.6 1.6 %collective-permute-start.22 = (bf16[144,1152]{1,0:T(8,128)(2,1)S(1)}, bf16[144,1152]{1,0:T(8,128)(2,1)S(1)}, u32[]{:S(2)}, u32[]{:S(2)}) collective-permute-start(bf16[144,1152]{1,0:T(8,128)(2,1)S(1)} %get-tuple-element.32.refs_1_.refs_22_), channel_id=1, source_target_pairs={{0,4},{1,3},{4,8},{5,1},{8,12},{9,5},{12,14},{13,9},{14,10},{15,13... | collective-permute-start | bytes 995336 | tf_op jit(solution)/shard_map/ppermute | solution.py:418
  35.2 2.0 %collective-permute-done.19.refs_4_.refs_19_ = bf16[144,1152]{1,0:T(8,128)(2,1)S(1)} collective-permute-done((bf16[144,1152]{1,0:T(8,128)(2,1)S(1)}, bf16[144,1152]{1,0:T(8,128)(2,1)S(1)}, u32[]{:S(2)}, u32[]{:S(2)}) %collective-permute-start.19) | collective-permute-done | bytes 331808 | tf_op jit(solution)/shard_map/ppermute | solution.py:418
  40.8 1.6 %collective-permute-start.23 = (bf16[144,1152]{1,0:T(8,128)(2,1)S(1)}, bf16[144,1152]{1,0:T(8,128)(2,1)S(1)}, u32[]{:S(2)}, u32[]{:S(2)}) collective-permute-start(bf16[144,1152]{1,0:T(8,128)(2,1)S(1)} %shard_map.144.refs_23_), channel_id=1, source_target_pairs={{0,4},{1,3},{4,8},{5,1},{8,12},{9,5},{12,14},{13,9},{14,10},{15,13... | collective-permute-start | bytes 995336 | tf_op jit(solution)/shard_map/ppermute | solution.py:418
  43.0 5.4 %collective-permute-done.21.refs_21_ = bf16[144,1152]{1,0:T(8,128)(2,1)S(1)} collective-permute-done((bf16[144,1152]{1,0:T(8,128)(2,1)S(1)}, bf16[144,1152]{1,0:T(8,128)(2,1)S(1)}, u32[]{:S(2)}, u32[]{:S(2)}) %collective-permute-start.21) | collective-permute-done | bytes 331808 | tf_op jit(solution)/shard_map/ppermute | solution.py:421
  50.5 9.9 %shard_map.145 = (bf16[128,1152]{1,0:T(8,128)(2,1)S(1)}, bf16[1792,128]{1,0:T(8,128)(2,1)S(1)}, bf16[8,128,128]{2,1,0:T(8,128)(2,1)S(1)}, bf16[16,144,1152]{2,1,...) custom-call(s32[4,8]{1,0:T(4,128)S(1)} %get-tuple-element.29.clips, ...), custom_call_target="tpu_custom_call" | custom-call | tf_op jit(solution)/shard_map/pallas_call | solution.py:391
  62.1 3.3 %collective-permute-start.31 = (bf16[32,2304]{1,0:T(8,128)(2,1)S(1)}, bf16[32,2304]{1,0:T(8,128)(2,1)S(1)}, u32[]{:S(2)}, u32[]{:S(2)}) collective-permute-start(bf16[32,2304]{1,0:T(8,128)(2,1)S(1)} %get-tuple-element.36), channel_id=1, source_target_pairs={{0,2},{1,3},{2,0},{3,1},{4,6},{5,7},{6,4},{7,5},{8,10},{9,11},{10,... | collective-permute-start | bytes 442376 | tf_op jit(solution)/shard_map/ppermute | solution.py:581
  67.0 2.6 %collective-permute-done.31.refs_1_ = bf16[32,2304]{1,0:T(8,128)(2,1)S(1)} collective-permute-done((bf16[32,2304]{1,0:T(8,128)(2,1)S(1)}, bf16[32,2304]{1,0:T(8,128)(2,1)S(1)}, u32[]{:S(2)}, u32[]{:S(2)}) %collective-permute-start.31) | collective-permute-done | bytes 147488 | tf_op jit(solution)/shard_map/ppermute | solution.py:581
  69.6 2.6 %collective-permute-done.32.refs_2_ = bf16[32,2304]{1,0:T(8,128)(2,1)S(1)} collective-permute-done((bf16[32,2304]{1,0:T(8,128)(2,1)S(1)}, bf16[32,2304]{1,0:T(8,128)(2,1)S(1)}, u32[]{:S(2)}, u32[]{:S(2)}) %collective-permute-start.32) | collective-permute-done | bytes 147488 | tf_op jit(solution)/shard_map/ppermute | solution.py:581
  72.2 1.8 %collective-permute-done.33.refs_3_ = bf16[32,2304]{1,0:T(8,128)(2,1)S(1)} collective-permute-done((bf16[32,2304]{1,0:T(8,128)(2,1)S(1)}, bf16[32,2304]{1,0:T(8,128)(2,1)S(1)}, u32[]{:S(2)}, u32[]{:S(2)}) %collective-permute-start.33) | collective-permute-done | bytes 147488 | tf_op jit(solution)/shard_map/ppermute | solution.py:581
  74.0 2.2 %shard_map.147 = (bf16[64,2304]{1,0:T(8,128)(2,1)S(1)}, bf16[64,2304]{1,0:T(8,128)(2,1)S(1)}) custom-call(s32[4,8]{1,0:T(4,128)S(1)} %get-tuple-element.29.clips, bf16[32,2304]{1,0:T(8,128)(2,1)S(1)} %get-tuple-element.35.refs_0_, bf16[32,2304]{1,0:T(8,128)(2,1)S(1)} %collective-permute-done.31.refs_1_, ...), custom_call_target="tpu_custom_call" | custom-call | tf_op jit(solution)/shard_map/pallas_call | solution.py:391
  76.3 1.6 %collective-permute-done.34.from_twin = bf16[64,2304]{1,0:T(8,128)(2,1)S(1)} collective-permute-done((bf16[64,2304]{1,0:T(8,128)(2,1)S(1)}, bf16[64,2304]{1,0:T(8,128)(2,1)S(1)}, u32[]{:S(2)}, u32[]{:S(2)}) %collective-permute-start.34) | collective-permute-done | bytes 294944 | tf_op jit(solution)/shard_map/ppermute | solution.py:575
  77.9 1.7 %collective-permute-start.35 = (bf16[32,2304]{1,0:T(8,128)(2,1)S(1)}, bf16[32,2304]{1,0:T(8,128)(2,1)S(1)}, u32[]{:S(2)}, u32[]{:S(2)}) collective-permute-start(bf16[32,2304]{1,0:T(8,128)(2,1)S(1)} %get-tuple-element.42), channel_id=1, source_target_pairs={{0,2},{1,3},{2,0},{3,1},{4,6},{5,7},{6,4},{7,5},{8,10},{9,11},{10,... | collective-permute-start | bytes 442376 | tf_op jit(solution)/shard_map/ppermute | solution.py:581
  81.4 2.4 %collective-permute-done.35.refs_1_ = bf16[32,2304]{1,0:T(8,128)(2,1)S(1)} collective-permute-done((bf16[32,2304]{1,0:T(8,128)(2,1)S(1)}, bf16[32,2304]{1,0:T(8,128)(2,1)S(1)}, u32[]{:S(2)}, u32[]{:S(2)}) %collective-permute-start.35) | collective-permute-done | bytes 147488 | tf_op jit(solution)/shard_map/ppermute | solution.py:581
  83.8 2.5 %collective-permute-done.36.refs_2_ = bf16[32,2304]{1,0:T(8,128)(2,1)S(1)} collective-permute-done((bf16[32,2304]{1,0:T(8,128)(2,1)S(1)}, bf16[32,2304]{1,0:T(8,128)(2,1)S(1)}, u32[]{:S(2)}, u32[]{:S(2)}) %collective-permute-start.36) | collective-permute-done | bytes 147488 | tf_op jit(solution)/shard_map/ppermute | solution.py:581
  86.3 1.8 %collective-permute-done.37.refs_3_ = bf16[32,2304]{1,0:T(8,128)(2,1)S(1)} collective-permute-done((bf16[32,2304]{1,0:T(8,128)(2,1)S(1)}, bf16[32,2304]{1,0:T(8,128)(2,1)S(1)}, u32[]{:S(2)}, u32[]{:S(2)}) %collective-permute-start.37) | collective-permute-done | bytes 147488 | tf_op jit(solution)/shard_map/ppermute | solution.py:581
  88.2 4.9 %shard_map.149 = (bf16[128,1152]{1,0:T(8,128)(2,1)S(1)}, bf16[128,1152]{1,0:T(8,128)(2,1)S(1)}, bf16[32,2,1152]{2,1,0:T(2,128)(2,1)}) custom-call(s32[4,8]{1,0:T(4,128)S(1)} %get-tuple-element.29.clips, bf16[32,2304]{1,0:T(8,128)(2,1)S(1)} %get-tuple-element.41.refs_0_, bf16[32,2304]{1,0:T(8,128)(2,1)S(1)} %collective-permute-done.35.refs_1_, ...), custom_call_target="tpu_custom_call" | custom-call | tf_op jit(solution)/shard_map/pallas_call | solution.py:391
  93.1 4.7 %all-to-all-start = ((bf16[32,2,1152]{2,1,0:T(2,128)(2,1)}), bf16[32,2,1152]{2,1,0:T(2,128)(2,1)S(1)}, u32[]{:S(2)}, u32[]{:S(2)}) async-start(bf16[32,2,1152]{2,1,0:T(2,128)(2,1)} %get-tuple-element.54), calls=%async_computation | async-start | bytes 294912 | tf_op jit(solution)/shard_map/all_to_all | solution.py:616
  97.8 2.5 %copy-done.1 = bf16[16,144,1152]{2,1,0:T(8,128)(2,1)S(1)} copy-done((bf16[16,144,1152]{2,1,0:T(8,128)(2,1)S(1)}, bf16[16,144,1152]{2,1,0:T(8,128)(2,1)}, u32[]{:S(2)}) %copy-start.1) | copy-done | bytes 5308440
  100.3 1.9 %shard_map.150 = (bf16[128,1152]{1,0:T(8,128)(2,1)}, bf16[128,1152]{1,0:T(8,128)(2,1)}) custom-call(bf16[32,2304]{1,0:T(8,128)(2,1)S(1)} %get-tuple-element.41.refs_0_, bf16[32,2304]{1,0:T(8,128)(2,1)S(1)} %collective-permute-done.35.refs_1_, bf16[32,2304]{1,0:T(8,128)(2,1)S(1)} %collective-permute-done.36.refs_2_, ...), custom_call_target="tpu_custom_call" | custom-call | tf_op jit(solution)/shard_map/pallas_call | solution.py:391
  102.2 4.0 %all-to-all-done = bf16[32,2,1152]{2,1,0:T(2,128)(2,1)S(1)} async-done(((bf16[32,2,1152]{2,1,0:T(2,128)(2,1)}), bf16[32,2,1152]{2,1,0:T(2,128)(2,1)S(1)}, u32[]{:S(2)}, u32[]{:S(2)}) %all-to-all-start) | async-done | bytes 147488 | tf_op jit(solution)/shard_map/all_to_all | solution.py:616
  (82 shorter events, 20.6 us)
Async XLA Ops:
  2.6 7.7 %collective-permute-start.4 = (bf16[144,1152]{1,0:T(8,128)(2,1)S(1)}, bf16[144,1152]{1,0:T(8,128)(2,1)S(1)}, u32[]{:S(2)}, u32[]{:S(2)}) collective-permute-start(bf16[144,1152]{1,0:T(8,128)(2,1)S(1)} %get-tuple-element.56.refs_0_), channel_id=1, source_target_pairs={{0,4},{1,3},{4,8},{5,1},{8,12},{9,5},{12,14},{13,9},{14,10},{15,13... | collective-permute-start | bytes 995336 | tf_op jit(solution)/shard_map/ppermute | solution.py:418
  5.2 8.6 %collective-permute-start.1 = (bf16[144,1152]{1,0:T(8,128)(2,1)S(1)}, bf16[144,1152]{1,0:T(8,128)(2,1)S(1)}, u32[]{:S(2)}, u32[]{:S(2)}) collective-permute-start(bf16[144,1152]{1,0:T(8,128)(2,1)S(1)} %collective-permute-done.refs_1_), channel_id=1, source_target_pairs={{0,4},{1,3},{4,8},{5,1},{8,12},{9,5},{12,14},{13,9},{14,10},{15,13... | collective-permute-start | bytes 995336 | tf_op jit(solution)/shard_map/ppermute | solution.py:418
  6.8 7.0 %collective-permute-start.7 = (bf16[144,1152]{1,0:T(8,128)(2,1)S(1)}, bf16[144,1152]{1,0:T(8,128)(2,1)S(1)}, u32[]{:S(2)}, u32[]{:S(2)}) collective-permute-start(bf16[144,1152]{1,0:T(8,128)(2,1)S(1)} %get-tuple-element.55.refs_16_), channel_id=1, source_target_pairs={{0,1},{1,0},{2,3},{3,2},{4,5},{5,4},{6,7},{7,6},{8,9},{9,8},{10,11... | collective-permute-start | bytes 995336 | tf_op jit(solution)/shard_map/ppermute | solution.py:424
  10.3 5.6 %collective-permute-start.6 = (bf16[144,1152]{1,0:T(8,128)(2,1)S(1)}, bf16[144,1152]{1,0:T(8,128)(2,1)S(1)}, u32[]{:S(2)}, u32[]{:S(2)}) collective-permute-start(bf16[144,1152]{1,0:T(8,128)(2,1)S(1)} %collective-permute-done.4.refs_2_), channel_id=1, source_target_pairs={{0,1},{1,0},{2,3},{3,2},{4,5},{5,4},{6,7},{7,6},{8,9},{9,8},{10,11... | collective-permute-start | bytes 995336 | tf_op jit(solution)/shard_map/ppermute | solution.py:424
  10.3 7.1 %collective-permute-start.5 = (bf16[144,1152]{1,0:T(8,128)(2,1)S(1)}, bf16[144,1152]{1,0:T(8,128)(2,1)S(1)}, u32[]{:S(2)}, u32[]{:S(2)}) collective-permute-start(bf16[144,1152]{1,0:T(8,128)(2,1)S(1)} %collective-permute-done.4.refs_2_), channel_id=1, source_target_pairs={{0,4},{1,3},{4,8},{5,1},{8,12},{9,5},{12,14},{13,9},{14,10},{15,13... | collective-permute-start | bytes 995336 | tf_op jit(solution)/shard_map/ppermute | solution.py:418
  12.4 10.1 %collective-permute-start.10 = (bf16[144,1152]{1,0:T(8,128)(2,1)S(1)}, bf16[144,1152]{1,0:T(8,128)(2,1)S(1)}, u32[]{:S(2)}, u32[]{:S(2)}) collective-permute-start(bf16[144,1152]{1,0:T(8,128)(2,1)S(1)} %collective-permute-done.4.refs_2_), channel_id=1, source_target_pairs={{0,16},{16,0},{1,17},{17,1},{2,18},{18,2},{3,19},{19,3},{4,20},{20... | collective-permute-start | bytes 995336 | tf_op jit(solution)/shard_map/ppermute | solution.py:421
  13.8 8.6 %collective-permute-start.8 = (bf16[144,1152]{1,0:T(8,128)(2,1)S(1)}, bf16[144,1152]{1,0:T(8,128)(2,1)S(1)}, u32[]{:S(2)}, u32[]{:S(2)}) collective-permute-start(bf16[144,1152]{1,0:T(8,128)(2,1)S(1)} %collective-permute-done.1.refs_1_.refs_6_), channel_id=1, source_target_pairs={{0,1},{1,0},{2,3},{3,2},{4,5},{5,4},{6,7},{7,6},{8,9},{9,8},{10,11... | collective-permute-start | bytes 995336 | tf_op jit(solution)/shard_map/ppermute | solution.py:424
  13.9 8.6 %collective-permute-start.3 = (bf16[144,1152]{1,0:T(8,128)(2,1)S(1)}, bf16[144,1152]{1,0:T(8,128)(2,1)S(1)}, u32[]{:S(2)}, u32[]{:S(2)}) collective-permute-start(bf16[144,1152]{1,0:T(8,128)(2,1)S(1)} %collective-permute-done.1.refs_1_.refs_6_), channel_id=1, source_target_pairs={{0,4},{1,3},{4,8},{5,1},{8,12},{9,5},{12,14},{13,9},{14,10},{15,13... | collective-permute-start | bytes 995336 | tf_op jit(solution)/shard_map/ppermute | solution.py:418
  17.4 7.2 %collective-permute-start.13 = (bf16[144,1152]{1,0:T(8,128)(2,1)S(1)}, bf16[144,1152]{1,0:T(8,128)(2,1)S(1)}, u32[]{:S(2)}, u32[]{:S(2)}) collective-permute-start(bf16[144,1152]{1,0:T(8,128)(2,1)S(1)} %shard_map.139.refs_1_.refs_3_), channel_id=1, source_target_pairs={{0,4},{1,3},{4,8},{5,1},{8,12},{9,5},{12,14},{13,9},{14,10},{15,13... | collective-permute-start | bytes 995336 | tf_op jit(solution)/shard_map/ppermute | solution.py:418
  20.9 9.1 %collective-permute-start.2 = (bf16[144,1152]{1,0:T(8,128)(2,1)S(1)}, bf16[144,1152]{1,0:T(8,128)(2,1)S(1)}, u32[]{:S(2)}, u32[]{:S(2)}) collective-permute-start(bf16[144,1152]{1,0:T(8,128)(2,1)S(1)} %collective-permute-done.1.refs_1_.refs_6_), channel_id=1, source_target_pairs={{0,16},{16,0},{1,17},{17,1},{2,18},{18,2},{3,19},{19,3},{4,20},{20... | collective-permute-start | bytes 995336 | tf_op jit(solution)/shard_map/ppermute | solution.py:421
  22.5 9.0 %collective-permute-start.12 = (bf16[144,1152]{1,0:T(8,128)(2,1)S(1)}, bf16[144,1152]{1,0:T(8,128)(2,1)S(1)}, u32[]{:S(2)}, u32[]{:S(2)}) collective-permute-start(bf16[144,1152]{1,0:T(8,128)(2,1)S(1)} %shard_map.140.refs_1_.refs_7_), channel_id=1, source_target_pairs={{0,1},{1,0},{2,3},{3,2},{4,5},{5,4},{6,7},{7,6},{8,9},{9,8},{10,11... | collective-permute-start | bytes 995336 | tf_op jit(solution)/shard_map/ppermute | solution.py:424
  23.0 8.5 %collective-permute-start.9 = (bf16[144,1152]{1,0:T(8,128)(2,1)S(1)}, bf16[144,1152]{1,0:T(8,128)(2,1)S(1)}, u32[]{:S(2)}, u32[]{:S(2)}) collective-permute-start(bf16[144,1152]{1,0:T(8,128)(2,1)S(1)} %shard_map.140.refs_1_.refs_7_), channel_id=1, source_target_pairs={{0,4},{1,3},{4,8},{5,1},{8,12},{9,5},{12,14},{13,9},{14,10},{15,13... | collective-permute-start | bytes 995336 | tf_op jit(solution)/shard_map/ppermute | solution.py:418
  24.6 9.1 %collective-permute-start.14 = (bf16[144,1152]{1,0:T(8,128)(2,1)S(1)}, bf16[144,1152]{1,0:T(8,128)(2,1)S(1)}, u32[]{:S(2)}, u32[]{:S(2)}) collective-permute-start(bf16[144,1152]{1,0:T(8,128)(2,1)S(1)} %shard_map.142.refs_4_), channel_id=1, source_target_pairs={{0,4},{1,3},{4,8},{5,1},{8,12},{9,5},{12,14},{13,9},{14,10},{15,13... | collective-permute-start | bytes 995336 | tf_op jit(solution)/shard_map/ppermute | solution.py:418
  26.7 10.5 %collective-permute-start.19 = (bf16[144,1152]{1,0:T(8,128)(2,1)S(1)}, bf16[144,1152]{1,0:T(8,128)(2,1)S(1)}, u32[]{:S(2)}, u32[]{:S(2)}) collective-permute-start(bf16[144,1152]{1,0:T(8,128)(2,1)S(1)} %collective-permute-done.10.refs_2_.refs_18_), channel_id=1, source_target_pairs={{0,4},{1,3},{4,8},{5,1},{8,12},{9,5},{12,14},{13,9},{14,10},{15,13... | collective-permute-start | bytes 995336 | tf_op jit(solution)/shard_map/ppermute | solution.py:418
  30.0 8.1 %collective-permute-start.20 = (bf16[144,1152]{1,0:T(8,128)(2,1)S(1)}, bf16[144,1152]{1,0:T(8,128)(2,1)S(1)}, u32[]{:S(2)}, u32[]{:S(2)}) collective-permute-start(bf16[144,1152]{1,0:T(8,128)(2,1)S(1)} %shard_map.142.refs_4_), channel_id=1, source_target_pairs={{0,16},{16,0},{1,17},{17,1},{2,18},{18,2},{3,19},{19,3},{4,20},{20... | collective-permute-start | bytes 995336 | tf_op jit(solution)/shard_map/ppermute | solution.py:421
  31.5 6.6 %collective-permute-start.18 = (bf16[144,1152]{1,0:T(8,128)(2,1)S(1)}, bf16[144,1152]{1,0:T(8,128)(2,1)S(1)}, u32[]{:S(2)}, u32[]{:S(2)}) collective-permute-start(bf16[144,1152]{1,0:T(8,128)(2,1)S(1)} %collective-permute-done.9.refs_4_.refs_2_.refs_8_), channel_id=1, source_target_pairs={{0,1},{1,0},{2,3},{3,2},{4,5},{5,4},{6,7},{7,6},{8,9},{9,8},{10,11... | collective-permute-start | bytes 995336 | tf_op jit(solution)/shard_map/ppermute | solution.py:424
  33.6 4.9 %collective-permute-start.17 = (bf16[144,1152]{1,0:T(8,128)(2,1)S(1)}, bf16[144,1152]{1,0:T(8,128)(2,1)S(1)}, u32[]{:S(2)}, u32[]{:S(2)}) collective-permute-start(bf16[144,1152]{1,0:T(8,128)(2,1)S(1)} %shard_map.143.refs_5_), channel_id=1, source_target_pairs={{0,1},{1,0},{2,3},{3,2},{4,5},{5,4},{6,7},{7,6},{8,9},{9,8},{10,11... | collective-permute-start | bytes 995336 | tf_op jit(solution)/shard_map/ppermute | solution.py:424
  33.6 7.1 %collective-permute-start.22 = (bf16[144,1152]{1,0:T(8,128)(2,1)S(1)}, bf16[144,1152]{1,0:T(8,128)(2,1)S(1)}, u32[]{:S(2)}, u32[]{:S(2)}) collective-permute-start(bf16[144,1152]{1,0:T(8,128)(2,1)S(1)} %get-tuple-element.32.refs_1_.refs_22_), channel_id=1, source_target_pairs={{0,4},{1,3},{4,8},{5,1},{8,12},{9,5},{12,14},{13,9},{14,10},{15,13... | collective-permute-start | bytes 995336 | tf_op jit(solution)/shard_map/ppermute | solution.py:418
  37.2 5.1 %collective-permute-start.15 = (bf16[144,1152]{1,0:T(8,128)(2,1)S(1)}, bf16[144,1152]{1,0:T(8,128)(2,1)S(1)}, u32[]{:S(2)}, u32[]{:S(2)}) collective-permute-start(bf16[144,1152]{1,0:T(8,128)(2,1)S(1)} %shard_map.139.refs_1_.refs_3_), channel_id=1, source_target_pairs={{0,1},{1,0},{2,3},{3,2},{4,5},{5,4},{6,7},{7,6},{8,9},{9,8},{10,11... | collective-permute-start | bytes 995336 | tf_op jit(solution)/shard_map/ppermute | solution.py:424
  38.1 4.8 %collective-permute-start.16 = (bf16[144,1152]{1,0:T(8,128)(2,1)S(1)}, bf16[144,1152]{1,0:T(8,128)(2,1)S(1)}, u32[]{:S(2)}, u32[]{:S(2)}) collective-permute-start(bf16[144,1152]{1,0:T(8,128)(2,1)S(1)} %shard_map.142.refs_4_), channel_id=1, source_target_pairs={{0,1},{1,0},{2,3},{3,2},{4,5},{5,4},{6,7},{7,6},{8,9},{9,8},{10,11... | collective-permute-start | bytes 995336 | tf_op jit(solution)/shard_map/ppermute | solution.py:424
  38.6 9.8 %collective-permute-start.21 = (bf16[144,1152]{1,0:T(8,128)(2,1)S(1)}, bf16[144,1152]{1,0:T(8,128)(2,1)S(1)}, u32[]{:S(2)}, u32[]{:S(2)}) collective-permute-start(bf16[144,1152]{1,0:T(8,128)(2,1)S(1)} %shard_map.143.refs_5_), channel_id=1, source_target_pairs={{0,16},{16,0},{1,17},{17,1},{2,18},{18,2},{3,19},{19,3},{4,20},{20... | collective-permute-start | bytes 995336 | tf_op jit(solution)/shard_map/ppermute | solution.py:421
  40.8 7.6 %collective-permute-start.23 = (bf16[144,1152]{1,0:T(8,128)(2,1)S(1)}, bf16[144,1152]{1,0:T(8,128)(2,1)S(1)}, u32[]{:S(2)}, u32[]{:S(2)}) collective-permute-start(bf16[144,1152]{1,0:T(8,128)(2,1)S(1)} %shard_map.144.refs_23_), channel_id=1, source_target_pairs={{0,4},{1,3},{4,8},{5,1},{8,12},{9,5},{12,14},{13,9},{14,10},{15,13... | collective-permute-start | bytes 995336 | tf_op jit(solution)/shard_map/ppermute | solution.py:418
  42.3 6.5 %collective-permute-start.27 = (bf16[144,1152]{1,0:T(8,128)(2,1)S(1)}, bf16[144,1152]{1,0:T(8,128)(2,1)S(1)}, u32[]{:S(2)}, u32[]{:S(2)}) collective-permute-start(bf16[144,1152]{1,0:T(8,128)(2,1)S(1)} %get-tuple-element.32.refs_1_.refs_22_), channel_id=1, source_target_pairs={{0,1},{1,0},{2,3},{3,2},{4,5},{5,4},{6,7},{7,6},{8,9},{9,8},{10,11... | collective-permute-start | bytes 995336 | tf_op jit(solution)/shard_map/ppermute | solution.py:424
  42.4 6.4 %collective-permute-start.25 = (bf16[144,1152]{1,0:T(8,128)(2,1)S(1)}, bf16[144,1152]{1,0:T(8,128)(2,1)S(1)}, u32[]{:S(2)}, u32[]{:S(2)}) collective-permute-start(bf16[144,1152]{1,0:T(8,128)(2,1)S(1)} %collective-permute-done.20.refs_3_.refs_20_), channel_id=1, source_target_pairs={{0,1},{1,0},{2,3},{3,2},{4,5},{5,4},{6,7},{7,6},{8,9},{9,8},{10,11... | collective-permute-start | bytes 995336 | tf_op jit(solution)/shard_map/ppermute | solution.py:424
  42.9 7.1 %collective-permute-start.28 = (bf16[144,1152]{1,0:T(8,128)(2,1)S(1)}, bf16[144,1152]{1,0:T(8,128)(2,1)S(1)}, u32[]{:S(2)}, u32[]{:S(2)}) collective-permute-start(bf16[144,1152]{1,0:T(8,128)(2,1)S(1)} %shard_map.144.refs_23_), channel_id=1, source_target_pairs={{0,1},{1,0},{2,3},{3,2},{4,5},{5,4},{6,7},{7,6},{8,9},{9,8},{10,11... | collective-permute-start | bytes 995336 | tf_op jit(solution)/shard_map/ppermute | solution.py:424
  62.1 7.5 %collective-permute-start.31 = (bf16[32,2304]{1,0:T(8,128)(2,1)S(1)}, bf16[32,2304]{1,0:T(8,128)(2,1)S(1)}, u32[]{:S(2)}, u32[]{:S(2)}) collective-permute-start(bf16[32,2304]{1,0:T(8,128)(2,1)S(1)} %get-tuple-element.36), channel_id=1, source_target_pairs={{0,2},{1,3},{2,0},{3,1},{4,6},{5,7},{6,4},{7,5},{8,10},{9,11},{10,... | collective-permute-start | bytes 442376 | tf_op jit(solution)/shard_map/ppermute | solution.py:581
  65.4 6.7 %collective-permute-start.32 = (bf16[32,2304]{1,0:T(8,128)(2,1)S(1)}, bf16[32,2304]{1,0:T(8,128)(2,1)S(1)}, u32[]{:S(2)}, u32[]{:S(2)}) collective-permute-start(bf16[32,2304]{1,0:T(8,128)(2,1)S(1)} %get-tuple-element.37), channel_id=1, source_target_pairs={{0,4},{1,5},{2,6},{3,7},{4,0},{5,1},{6,2},{7,3},{8,12},{9,13},{10,... | collective-permute-start | bytes 442376 | tf_op jit(solution)/shard_map/ppermute | solution.py:581
  66.6 7.4 %collective-permute-start.33 = (bf16[32,2304]{1,0:T(8,128)(2,1)S(1)}, bf16[32,2304]{1,0:T(8,128)(2,1)S(1)}, u32[]{:S(2)}, u32[]{:S(2)}) collective-permute-start(bf16[32,2304]{1,0:T(8,128)(2,1)S(1)} %get-tuple-element.38), channel_id=1, source_target_pairs={{0,6},{1,7},{2,4},{3,5},{4,2},{5,3},{6,0},{7,1},{8,14},{9,15},{10,... | collective-permute-start | bytes 442376 | tf_op jit(solution)/shard_map/ppermute | solution.py:581
  77.9 6.0 %collective-permute-start.35 = (bf16[32,2304]{1,0:T(8,128)(2,1)S(1)}, bf16[32,2304]{1,0:T(8,128)(2,1)S(1)}, u32[]{:S(2)}, u32[]{:S(2)}) collective-permute-start(bf16[32,2304]{1,0:T(8,128)(2,1)S(1)} %get-tuple-element.42), channel_id=1, source_target_pairs={{0,2},{1,3},{2,0},{3,1},{4,6},{5,7},{6,4},{7,5},{8,10},{9,11},{10,... | collective-permute-start | bytes 442376 | tf_op jit(solution)/shard_map/ppermute | solution.py:581
  79.6 6.7 %collective-permute-start.36 = (bf16[32,2304]{1,0:T(8,128)(2,1)S(1)}, bf16[32,2304]{1,0:T(8,128)(2,1)S(1)}, u32[]{:S(2)}, u32[]{:S(2)}) collective-permute-start(bf16[32,2304]{1,0:T(8,128)(2,1)S(1)} %get-tuple-element.43), channel_id=1, source_target_pairs={{0,4},{1,5},{2,6},{3,7},{4,0},{5,1},{6,2},{7,3},{8,12},{9,13},{10,... | collective-permute-start | bytes 442376 | tf_op jit(solution)/shard_map/ppermute | solution.py:581
  80.8 7.3 %collective-permute-start.37 = (bf16[32,2304]{1,0:T(8,128)(2,1)S(1)}, bf16[32,2304]{1,0:T(8,128)(2,1)S(1)}, u32[]{:S(2)}, u32[]{:S(2)}) collective-permute-start(bf16[32,2304]{1,0:T(8,128)(2,1)S(1)} %get-tuple-element.44), channel_id=1, source_target_pairs={{0,6},{1,7},{2,4},{3,5},{4,2},{5,3},{6,0},{7,1},{8,14},{9,15},{10,... | collective-permute-start | bytes 442376 | tf_op jit(solution)/shard_map/ppermute | solution.py:581
  93.1 13.1 %all-to-all-start = ((bf16[32,2,1152]{2,1,0:T(2,128)(2,1)}), bf16[32,2,1152]{2,1,0:T(2,128)(2,1)S(1)}, u32[]{:S(2)}, u32[]{:S(2)}) async-start(bf16[32,2,1152]{2,1,0:T(2,128)(2,1)} %get-tuple-element.54), calls=%async_computation | async-start | bytes 294912 | tf_op jit(solution)/shard_map/all_to_all | solution.py:616
  (15 other events, 209.7 us)
where the time goes:
time: 107 us
  starting transfers between devices  40.8 us (38%)
  waiting for transfers between devices  40.1 us (37%)
  Pallas kernels  19 us (18%)
  local copies, waits for them, and re-layouts  3.93 us (4%)
  other arithmetic  2.2 us (2%)
    pallas_call x6, Pallas kernels, call(): pl.pallas_call(body, out_shape=out_shapes, in_specs=[scalars] * len(clips...  19 us
    ppermute x10, starting transfers between devices, ring(): return lax.ppermute(rows, 'ctx', ring_pairs)  18.8 us
    ppermute x6, waiting for transfers between devices, exchange(): lax.ppermute(rows_away, 'ctx', [(index, index ^ 2 * distance) for index i...  13.8 us
    ppermute x10, waiting for transfers between devices, ring(): return lax.ppermute(rows, 'ctx', ring_pairs)  9.79 us
    ppermute x6, starting transfers between devices, exchange(): lax.ppermute(rows_away, 'ctx', [(index, index ^ 2 * distance) for index i...  8.43 us
    ppermute x4, waiting for transfers between devices, across(): lax.ppermute(rows, 'dp', [(index, index ^ 1) for index in range(planes)])  7.9 us
    ppermute x4, starting transfers between devices, across(): lax.ppermute(rows, 'dp', [(index, index ^ 1) for index in range(planes)])  6.03 us
    all_to_all x1, starting transfers between devices, shards(): lax.all_to_all(gains, ('dp', 'ctx'), split_axis=0, concat_axis=0, tiled=T...  4.67 us
  transfers between devices with their start and end apart: 39, of which 19 were waited for; matrix products, arithmetic and copies ran while one was open for 1% of the time, Pallas kernels for 2%

commit v1 on v0

--- a/solution.py
+++ b/solution.py
@@ -366,8 +366,12 @@
     values = tokens[0].astype(F32)
     normed = values * inverse_size(values)
     grad_space_gain = jnp.sum(grad_normed.astype(F32) * normed, axis=0, keepdims=True)
-    both_gains = jnp.concatenate([grad_space_gain, grad_time_gain], axis=0).astype(gain_parts.dtype)
-    gain_parts[...] = jnp.broadcast_to(both_gains[None], gain_parts.shape)
+    gain_parts[...] = jnp.concatenate([grad_space_gain, grad_time_gain], axis=0)
+
+
+def spread(parts, from_twin, outs):
+    chip_sum = (parts[...] + from_twin[...]).astype(outs.dtype)
+    outs[...] = jnp.broadcast_to(chip_sum[None], outs.shape)
 
 
 def finish(rows, direct, *refs):
@@ -459,8 +463,8 @@
     x_o2_twin = twin(x_o2)
     x_t2_twin = twin(x_t2)
     x_o3_twin = twin(x_o3)
+    x_t3_twin = twin(x_t3)
     x_o4_twin = twin(x_o4)
-    x_t3_twin = twin(x_t3)
     mine = {"o0": (own, 0), "t0": (t0, 0)}
     other = {"o0": (own_other, 0), "t0": (t0_other, 0)}
     mine |= {"o1": (o1, 0), "o1_twin": (o1_twin, 0)}
@@ -608,12 +612,26 @@
     whole = jax.ShapeDtypeStruct((FRAME, features), BF16)
     grad_hidden, grad_normed, gains = call(
         functools.partial(time_back, rows, direct),
-        (whole, whole, jax.ShapeDtypeStruct((everyone, 2, features), BF16)),
+        (whole, whole, jax.ShapeDtypeStruct((2, features), F32)),
         [out_wide, qkv_wide, stage],
         clips,
         (*arrived, both_tokens, both_gains, time_weights, space_weights, hidden, saved, shares),
     )
-    gains = lax.all_to_all(gains, ("dp", "ctx"), split_axis=0, concat_axis=0, tiled=True)
+    gains = call(
+        spread,
+        jax.ShapeDtypeStruct((everyone // 2, 2, features), BF16),
+        [],
+        None,
+        (gains, lax.ppermute(gains, "ctx", [(index, index ^ 1) for index in range(size)])),
+    )
+    gains = lax.all_to_all(
+        gains,
+        ("dp", "ctx"),
+        split_axis=0,
+        concat_axis=0,
+        axis_index_groups=[list(range(core, everyone, 2)) for core in range(2)],
+        tiled=True,
+    )
     result, grad_tokens = call(
         functools.partial(finish, rows, direct),
         (whole, whole),

time: 107 us -> 109 us (1.019)
  starting transfers between devices: 40.8 us -> 41.9 us
    ppermute x0 -> x1, waiting for transfers between devices: none -> 1.16 us  [shards(): lax.ppermute(gains, 'ctx', [(index, index ^ 1) for index in range(size)])]
    pallas_call x6 -> x7, Pallas kernels: 19 us -> 19 us  [call(): pl.pallas_call(body, out_shape=out_shapes, in_specs=[scalars] * len(clips...]
  transfers between devices with their start and end apart: 39 -> 40, of which waited for: 19 -> 20; matrix products, arithmetic and copies ran while one was open for 1% -> 1% of each run, Pallas kernels for 2% -> 2%
where the time goes in v1:
time: 109 us; the launch traced here: 108 us
  starting transfers between devices  41.9 us (38%)
  waiting for transfers between devices  40.4 us (37%)
  Pallas kernels  19 us (17%)
  local copies, waits for them, and re-layouts  3.93 us (4%)
  other arithmetic  2.14 us (2%)
    pallas_call x7, Pallas kernels, call(): pl.pallas_call(body, out_shape=out_shapes, in_specs=[scalars] * len(clips...  19 us
    ppermute x10, starting transfers between devices, ring(): return lax.ppermute(rows, 'ctx', ring_pairs)  18.8 us
    ppermute x6, waiting for transfers between devices, exchange(): lax.ppermute(rows_away, 'ctx', [(index, index ^ 2 * distance) for index i...  13.8 us
    ppermute x10, waiting for transfers between devices, ring(): return lax.ppermute(rows, 'ctx', ring_pairs)  9.79 us
    ppermute x6, starting transfers between devices, exchange(): lax.ppermute(rows_away, 'ctx', [(index, index ^ 2 * distance) for index i...  8.43 us
    ppermute x4, waiting for transfers between devices, across(): lax.ppermute(rows, 'dp', [(index, index ^ 1) for index in range(planes)])  7.9 us
    ppermute x4, starting transfers between devices, across(): lax.ppermute(rows, 'dp', [(index, index ^ 1) for index in range(planes)])  6.03 us
    all_to_all x1, starting transfers between devices, shards(): lax.all_to_all(gains, ('dp', 'ctx'), split_axis=0, concat_axis=0, axis_in...  5.69 us
  transfers between devices with their start and end apart: 40, of which 20 were waited for; matrix products, arithmetic and copies ran while one was open for 1% of the time, Pallas kernels for 2%

profile of v1, /device:TPU:0, one launch (start us, length us, event | category | flops | bytes accessed | tf_op | source)
XLA Modules:
  0.0 108.2 jit_solution(17954602117011489701)
XLA Ops:
  2.6 2.6 %collective-permute-start.4 = (bf16[144,1152]{1,0:T(8,128)(2,1)S(1)}, bf16[144,1152]{1,0:T(8,128)(2,1)S(1)}, u32[]{:S(2)}, u32[]{:S(2)}) collective-permute-start(bf16[144,1152]{1,0:T(8,128)(2,1)S(1)} %get-tuple-element.56.refs_0_), channel_id=1, source_target_pairs={{0,4},{1,3},{4,8},{5,1},{8,12},{9,5},{12,14},{13,9},{14,10},{15,13... | collective-permute-start | bytes 995336 | tf_op jit(solution)/shard_map/ppermute | solution.py:422
  5.2 1.6 %collective-permute-start.1 = (bf16[144,1152]{1,0:T(8,128)(2,1)S(1)}, bf16[144,1152]{1,0:T(8,128)(2,1)S(1)}, u32[]{:S(2)}, u32[]{:S(2)}) collective-permute-start(bf16[144,1152]{1,0:T(8,128)(2,1)S(1)} %collective-permute-done.refs_1_), channel_id=1, source_target_pairs={{0,4},{1,3},{4,8},{5,1},{8,12},{9,5},{12,14},{13,9},{14,10},{15,13... | collective-permute-start | bytes 995336 | tf_op jit(solution)/shard_map/ppermute | solution.py:422
  6.8 3.5 %collective-permute-done.4.refs_2_ = bf16[144,1152]{1,0:T(8,128)(2,1)S(1)} collective-permute-done((bf16[144,1152]{1,0:T(8,128)(2,1)S(1)}, bf16[144,1152]{1,0:T(8,128)(2,1)S(1)}, u32[]{:S(2)}, u32[]{:S(2)}) %collective-permute-start.4) | collective-permute-done | bytes 331808 | tf_op jit(solution)/shard_map/ppermute | solution.py:422
  10.3 2.1 %collective-permute-start.5 = (bf16[144,1152]{1,0:T(8,128)(2,1)S(1)}, bf16[144,1152]{1,0:T(8,128)(2,1)S(1)}, u32[]{:S(2)}, u32[]{:S(2)}) collective-permute-start(bf16[144,1152]{1,0:T(8,128)(2,1)S(1)} %collective-permute-done.4.refs_2_), channel_id=1, source_target_pairs={{0,4},{1,3},{4,8},{5,1},{8,12},{9,5},{12,14},{13,9},{14,10},{15,13... | collective-permute-start | bytes 995336 | tf_op jit(solution)/shard_map/ppermute | solution.py:422
  13.9 2.1 %collective-permute-start.3 = (bf16[144,1152]{1,0:T(8,128)(2,1)S(1)}, bf16[144,1152]{1,0:T(8,128)(2,1)S(1)}, u32[]{:S(2)}, u32[]{:S(2)}) collective-permute-start(bf16[144,1152]{1,0:T(8,128)(2,1)S(1)} %collective-permute-done.1.refs_1_.refs_6_), channel_id=1, source_target_pairs={{0,4},{1,3},{4,8},{5,1},{8,12},{9,5},{12,14},{13,9},{14,10},{15,13... | collective-permute-start | bytes 995336 | tf_op jit(solution)/shard_map/ppermute | solution.py:422
  17.4 2.1 %collective-permute-start.13 = (bf16[144,1152]{1,0:T(8,128)(2,1)S(1)}, bf16[144,1152]{1,0:T(8,128)(2,1)S(1)}, u32[]{:S(2)}, u32[]{:S(2)}) collective-permute-start(bf16[144,1152]{1,0:T(8,128)(2,1)S(1)} %shard_map.139.refs_1_.refs_3_), channel_id=1, source_target_pairs={{0,4},{1,3},{4,8},{5,1},{8,12},{9,5},{12,14},{13,9},{14,10},{15,13... | collective-permute-start | bytes 995336 | tf_op jit(solution)/shard_map/ppermute | solution.py:422
  20.9 1.6 %collective-permute-start.2 = (bf16[144,1152]{1,0:T(8,128)(2,1)S(1)}, bf16[144,1152]{1,0:T(8,128)(2,1)S(1)}, u32[]{:S(2)}, u32[]{:S(2)}) collective-permute-start(bf16[144,1152]{1,0:T(8,128)(2,1)S(1)} %collective-permute-done.1.refs_1_.refs_6_), channel_id=1, source_target_pairs={{0,16},{16,0},{1,17},{17,1},{2,18},{18,2},{3,19},{19,3},{4,20},{20... | collective-permute-start | bytes 995336 | tf_op jit(solution)/shard_map/ppermute | solution.py:425
  23.0 1.6 %collective-permute-start.9 = (bf16[144,1152]{1,0:T(8,128)(2,1)S(1)}, bf16[144,1152]{1,0:T(8,128)(2,1)S(1)}, u32[]{:S(2)}, u32[]{:S(2)}) collective-permute-start(bf16[144,1152]{1,0:T(8,128)(2,1)S(1)} %shard_map.140.refs_1_.refs_7_), channel_id=1, source_target_pairs={{0,4},{1,3},{4,8},{5,1},{8,12},{9,5},{12,14},{13,9},{14,10},{15,13... | collective-permute-start | bytes 995336 | tf_op jit(solution)/shard_map/ppermute | solution.py:422
  24.6 2.0 %collective-permute-start.14 = (bf16[144,1152]{1,0:T(8,128)(2,1)S(1)}, bf16[144,1152]{1,0:T(8,128)(2,1)S(1)}, u32[]{:S(2)}, u32[]{:S(2)}) collective-permute-start(bf16[144,1152]{1,0:T(8,128)(2,1)S(1)} %shard_map.142.refs_4_), channel_id=1, source_target_pairs={{0,4},{1,3},{4,8},{5,1},{8,12},{9,5},{12,14},{13,9},{14,10},{15,13... | collective-permute-start | bytes 995336 | tf_op jit(solution)/shard_map/ppermute | solution.py:422
  26.7 1.6 %collective-permute-start.19 = (bf16[144,1152]{1,0:T(8,128)(2,1)S(1)}, bf16[144,1152]{1,0:T(8,128)(2,1)S(1)}, u32[]{:S(2)}, u32[]{:S(2)}) collective-permute-start(bf16[144,1152]{1,0:T(8,128)(2,1)S(1)} %collective-permute-done.10.refs_2_.refs_18_), channel_id=1, source_target_pairs={{0,4},{1,3},{4,8},{5,1},{8,12},{9,5},{12,14},{13,9},{14,10},{15,13... | collective-permute-start | bytes 995336 | tf_op jit(solution)/shard_map/ppermute | solution.py:422
  28.4 1.6 %collective-permute-done.2.refs_0_ = bf16[144,1152]{1,0:T(8,128)(2,1)S(1)} collective-permute-done((bf16[144,1152]{1,0:T(8,128)(2,1)S(1)}, bf16[144,1152]{1,0:T(8,128)(2,1)S(1)}, u32[]{:S(2)}, u32[]{:S(2)}) %collective-permute-start.2) | collective-permute-done | bytes 331808 | tf_op jit(solution)/shard_map/ppermute | solution.py:425
  31.5 2.2 %collective-permute-done.14.refs_0_ = bf16[144,1152]{1,0:T(8,128)(2,1)S(1)} collective-permute-done((bf16[144,1152]{1,0:T(8,128)(2,1)S(1)}, bf16[144,1152]{1,0:T(8,128)(2,1)S(1)}, u32[]{:S(2)}, u32[]{:S(2)}) %collective-permute-start.14) | collective-permute-done | bytes 331808 | tf_op jit(solution)/shard_map/ppermute | solution.py:422
  33.6 1.6 %collective-permute-start.22 = (bf16[144,1152]{1,0:T(8,128)(2,1)S(1)}, bf16[144,1152]{1,0:T(8,128)(2,1)S(1)}, u32[]{:S(2)}, u32[]{:S(2)}) collective-permute-start(bf16[144,1152]{1,0:T(8,128)(2,1)S(1)} %get-tuple-element.32.refs_1_.refs_22_), channel_id=1, source_target_pairs={{0,4},{1,3},{4,8},{5,1},{8,12},{9,5},{12,14},{13,9},{14,10},{15,13... | collective-permute-start | bytes 995336 | tf_op jit(solution)/shard_map/ppermute | solution.py:422
  35.2 2.0 %collective-permute-done.19.refs_4_.refs_19_ = bf16[144,1152]{1,0:T(8,128)(2,1)S(1)} collective-permute-done((bf16[144,1152]{1,0:T(8,128)(2,1)S(1)}, bf16[144,1152]{1,0:T(8,128)(2,1)S(1)}, u32[]{:S(2)}, u32[]{:S(2)}) %collective-permute-start.19) | collective-permute-done | bytes 331808 | tf_op jit(solution)/shard_map/ppermute | solution.py:422
  40.8 1.6 %collective-permute-start.23 = (bf16[144,1152]{1,0:T(8,128)(2,1)S(1)}, bf16[144,1152]{1,0:T(8,128)(2,1)S(1)}, u32[]{:S(2)}, u32[]{:S(2)}) collective-permute-start(bf16[144,1152]{1,0:T(8,128)(2,1)S(1)} %shard_map.144.refs_23_), channel_id=1, source_target_pairs={{0,4},{1,3},{4,8},{5,1},{8,12},{9,5},{12,14},{13,9},{14,10},{15,13... | collective-permute-start | bytes 995336 | tf_op jit(solution)/shard_map/ppermute | solution.py:422
  43.0 5.4 %collective-permute-done.21.refs_21_ = bf16[144,1152]{1,0:T(8,128)(2,1)S(1)} collective-permute-done((bf16[144,1152]{1,0:T(8,128)(2,1)S(1)}, bf16[144,1152]{1,0:T(8,128)(2,1)S(1)}, u32[]{:S(2)}, u32[]{:S(2)}) %collective-permute-start.21) | collective-permute-done | bytes 331808 | tf_op jit(solution)/shard_map/ppermute | solution.py:425
  50.5 9.9 %shard_map.145 = (bf16[128,1152]{1,0:T(8,128)(2,1)S(1)}, bf16[1792,128]{1,0:T(8,128)(2,1)S(1)}, bf16[8,128,128]{2,1,0:T(8,128)(2,1)S(1)}, bf16[16,144,1152]{2,1,...) custom-call(s32[4,8]{1,0:T(4,128)S(1)} %get-tuple-element.29.clips, ...), custom_call_target="tpu_custom_call" | custom-call | tf_op jit(solution)/shard_map/pallas_call | solution.py:395
  62.1 3.3 %collective-permute-start.31 = (bf16[32,2304]{1,0:T(8,128)(2,1)S(1)}, bf16[32,2304]{1,0:T(8,128)(2,1)S(1)}, u32[]{:S(2)}, u32[]{:S(2)}) collective-permute-start(bf16[32,2304]{1,0:T(8,128)(2,1)S(1)} %get-tuple-element.36), channel_id=1, source_target_pairs={{0,2},{1,3},{2,0},{3,1},{4,6},{5,7},{6,4},{7,5},{8,10},{9,11},{10,... | collective-permute-start | bytes 442376 | tf_op jit(solution)/shard_map/ppermute | solution.py:585
  67.0 2.6 %collective-permute-done.31.refs_1_ = bf16[32,2304]{1,0:T(8,128)(2,1)S(1)} collective-permute-done((bf16[32,2304]{1,0:T(8,128)(2,1)S(1)}, bf16[32,2304]{1,0:T(8,128)(2,1)S(1)}, u32[]{:S(2)}, u32[]{:S(2)}) %collective-permute-start.31) | collective-permute-done | bytes 147488 | tf_op jit(solution)/shard_map/ppermute | solution.py:585
  69.6 2.6 %collective-permute-done.32.refs_2_ = bf16[32,2304]{1,0:T(8,128)(2,1)S(1)} collective-permute-done((bf16[32,2304]{1,0:T(8,128)(2,1)S(1)}, bf16[32,2304]{1,0:T(8,128)(2,1)S(1)}, u32[]{:S(2)}, u32[]{:S(2)}) %collective-permute-start.32) | collective-permute-done | bytes 147488 | tf_op jit(solution)/shard_map/ppermute | solution.py:585
  72.2 1.8 %collective-permute-done.33.refs_3_ = bf16[32,2304]{1,0:T(8,128)(2,1)S(1)} collective-permute-done((bf16[32,2304]{1,0:T(8,128)(2,1)S(1)}, bf16[32,2304]{1,0:T(8,128)(2,1)S(1)}, u32[]{:S(2)}, u32[]{:S(2)}) %collective-permute-start.33) | collective-permute-done | bytes 147488 | tf_op jit(solution)/shard_map/ppermute | solution.py:585
  74.0 2.2 %shard_map.147 = (bf16[64,2304]{1,0:T(8,128)(2,1)S(1)}, bf16[64,2304]{1,0:T(8,128)(2,1)S(1)}) custom-call(s32[4,8]{1,0:T(4,128)S(1)} %get-tuple-element.29.clips, bf16[32,2304]{1,0:T(8,128)(2,1)S(1)} %get-tuple-element.35.refs_0_, bf16[32,2304]{1,0:T(8,128)(2,1)S(1)} %collective-permute-done.31.refs_1_, ...), custom_call_target="tpu_custom_call" | custom-call | tf_op jit(solution)/shard_map/pallas_call | solution.py:395
  76.3 1.6 %collective-permute-done.34.from_twin = bf16[64,2304]{1,0:T(8,128)(2,1)S(1)} collective-permute-done((bf16[64,2304]{1,0:T(8,128)(2,1)S(1)}, bf16[64,2304]{1,0:T(8,128)(2,1)S(1)}, u32[]{:S(2)}, u32[]{:S(2)}) %collective-permute-start.34) | collective-permute-done | bytes 294944 | tf_op jit(solution)/shard_map/ppermute | solution.py:579
  77.9 1.7 %collective-permute-start.35 = (bf16[32,2304]{1,0:T(8,128)(2,1)S(1)}, bf16[32,2304]{1,0:T(8,128)(2,1)S(1)}, u32[]{:S(2)}, u32[]{:S(2)}) collective-permute-start(bf16[32,2304]{1,0:T(8,128)(2,1)S(1)} %get-tuple-element.42), channel_id=1, source_target_pairs={{0,2},{1,3},{2,0},{3,1},{4,6},{5,7},{6,4},{7,5},{8,10},{9,11},{10,... | collective-permute-start | bytes 442376 | tf_op jit(solution)/shard_map/ppermute | solution.py:585
  81.4 2.4 %collective-permute-done.35.refs_1_ = bf16[32,2304]{1,0:T(8,128)(2,1)S(1)} collective-permute-done((bf16[32,2304]{1,0:T(8,128)(2,1)S(1)}, bf16[32,2304]{1,0:T(8,128)(2,1)S(1)}, u32[]{:S(2)}, u32[]{:S(2)}) %collective-permute-start.35) | collective-permute-done | bytes 147488 | tf_op jit(solution)/shard_map/ppermute | solution.py:585
  83.8 2.5 %collective-permute-done.36.refs_2_ = bf16[32,2304]{1,0:T(8,128)(2,1)S(1)} collective-permute-done((bf16[32,2304]{1,0:T(8,128)(2,1)S(1)}, bf16[32,2304]{1,0:T(8,128)(2,1)S(1)}, u32[]{:S(2)}, u32[]{:S(2)}) %collective-permute-start.36) | collective-permute-done | bytes 147488 | tf_op jit(solution)/shard_map/ppermute | solution.py:585
  86.3 1.8 %collective-permute-done.37.refs_3_ = bf16[32,2304]{1,0:T(8,128)(2,1)S(1)} collective-permute-done((bf16[32,2304]{1,0:T(8,128)(2,1)S(1)}, bf16[32,2304]{1,0:T(8,128)(2,1)S(1)}, u32[]{:S(2)}, u32[]{:S(2)}) %collective-permute-start.37) | collective-permute-done | bytes 147488 | tf_op jit(solution)/shard_map/ppermute | solution.py:585
  88.2 4.2 %shard_map.149 = (bf16[128,1152]{1,0:T(8,128)(2,1)S(1)}, bf16[128,1152]{1,0:T(8,128)(2,1)S(1)}, f32[2,1152]{1,0:T(2,128)S(1)}) custom-call(s32[4,8]{1,0:T(4,128)S(1)} %get-tuple-element.29.clips, bf16[32,2304]{1,0:T(8,128)(2,1)S(1)} %get-tuple-element.41.refs_0_, bf16[32,2304]{1,0:T(8,128)(2,1)S(1)} %collective-permute-done.35.refs_1_, ...), custom_call_target="tpu_custom_call" | custom-call | tf_op jit(solution)/shard_map/pallas_call | solution.py:395
  94.3 5.7 %all-to-all-start = ((bf16[16,2,1152]{2,1,0:T(2,128)(2,1)}), bf16[16,2,1152]{2,1,0:T(2,128)(2,1)S(1)}, u32[]{:S(2)}, u32[]{:S(2)}) async-start(bf16[16,2,1152]{2,1,0:T(2,128)(2,1)} %shard_map.151), calls=%async_computation | async-start | bytes 147456 | tf_op jit(solution)/shard_map/all_to_all | solution.py:627
  100.0 2.5 %copy-done.1 = bf16[16,144,1152]{2,1,0:T(8,128)(2,1)S(1)} copy-done((bf16[16,144,1152]{2,1,0:T(8,128)(2,1)S(1)}, bf16[16,144,1152]{2,1,0:T(8,128)(2,1)}, u32[]{:S(2)}) %copy-start.1) | copy-done | bytes 5308440
  102.5 1.9 %shard_map.150 = (bf16[128,1152]{1,0:T(8,128)(2,1)}, bf16[128,1152]{1,0:T(8,128)(2,1)}) custom-call(bf16[32,2304]{1,0:T(8,128)(2,1)S(1)} %get-tuple-element.41.refs_0_, bf16[32,2304]{1,0:T(8,128)(2,1)S(1)} %collective-permute-done.35.refs_1_, bf16[32,2304]{1,0:T(8,128)(2,1)S(1)} %collective-permute-done.36.refs_2_, ...), custom_call_target="tpu_custom_call" | custom-call | tf_op jit(solution)/shard_map/pallas_call | solution.py:395
  104.4 3.1 %all-to-all-done = bf16[16,2,1152]{2,1,0:T(2,128)(2,1)S(1)} async-done(((bf16[16,2,1152]{2,1,0:T(2,128)(2,1)}), bf16[16,2,1152]{2,1,0:T(2,128)(2,1)S(1)}, u32[]{:S(2)}, u32[]{:S(2)}) %all-to-all-start) | async-done | bytes 73760 | tf_op jit(solution)/shard_map/all_to_all | solution.py:627
  (85 shorter events, 22.4 us)
Async XLA Ops:
  2.6 7.7 %collective-permute-start.4 = (bf16[144,1152]{1,0:T(8,128)(2,1)S(1)}, bf16[144,1152]{1,0:T(8,128)(2,1)S(1)}, u32[]{:S(2)}, u32[]{:S(2)}) collective-permute-start(bf16[144,1152]{1,0:T(8,128)(2,1)S(1)} %get-tuple-element.56.refs_0_), channel_id=1, source_target_pairs={{0,4},{1,3},{4,8},{5,1},{8,12},{9,5},{12,14},{13,9},{14,10},{15,13... | collective-permute-start | bytes 995336 | tf_op jit(solution)/shard_map/ppermute | solution.py:422
  5.2 8.6 %collective-permute-start.1 = (bf16[144,1152]{1,0:T(8,128)(2,1)S(1)}, bf16[144,1152]{1,0:T(8,128)(2,1)S(1)}, u32[]{:S(2)}, u32[]{:S(2)}) collective-permute-start(bf16[144,1152]{1,0:T(8,128)(2,1)S(1)} %collective-permute-done.refs_1_), channel_id=1, source_target_pairs={{0,4},{1,3},{4,8},{5,1},{8,12},{9,5},{12,14},{13,9},{14,10},{15,13... | collective-permute-start | bytes 995336 | tf_op jit(solution)/shard_map/ppermute | solution.py:422
  6.8 7.0 %collective-permute-start.7 = (bf16[144,1152]{1,0:T(8,128)(2,1)S(1)}, bf16[144,1152]{1,0:T(8,128)(2,1)S(1)}, u32[]{:S(2)}, u32[]{:S(2)}) collective-permute-start(bf16[144,1152]{1,0:T(8,128)(2,1)S(1)} %get-tuple-element.55.refs_16_), channel_id=1, source_target_pairs={{0,1},{1,0},{2,3},{3,2},{4,5},{5,4},{6,7},{7,6},{8,9},{9,8},{10,11... | collective-permute-start | bytes 995336 | tf_op jit(solution)/shard_map/ppermute | solution.py:428
  10.3 5.6 %collective-permute-start.6 = (bf16[144,1152]{1,0:T(8,128)(2,1)S(1)}, bf16[144,1152]{1,0:T(8,128)(2,1)S(1)}, u32[]{:S(2)}, u32[]{:S(2)}) collective-permute-start(bf16[144,1152]{1,0:T(8,128)(2,1)S(1)} %collective-permute-done.4.refs_2_), channel_id=1, source_target_pairs={{0,1},{1,0},{2,3},{3,2},{4,5},{5,4},{6,7},{7,6},{8,9},{9,8},{10,11... | collective-permute-start | bytes 995336 | tf_op jit(solution)/shard_map/ppermute | solution.py:428
  10.3 7.1 %collective-permute-start.5 = (bf16[144,1152]{1,0:T(8,128)(2,1)S(1)}, bf16[144,1152]{1,0:T(8,128)(2,1)S(1)}, u32[]{:S(2)}, u32[]{:S(2)}) collective-permute-start(bf16[144,1152]{1,0:T(8,128)(2,1)S(1)} %collective-permute-done.4.refs_2_), channel_id=1, source_target_pairs={{0,4},{1,3},{4,8},{5,1},{8,12},{9,5},{12,14},{13,9},{14,10},{15,13... | collective-permute-start | bytes 995336 | tf_op jit(solution)/shard_map/ppermute | solution.py:422
  12.4 10.1 %collective-permute-start.10 = (bf16[144,1152]{1,0:T(8,128)(2,1)S(1)}, bf16[144,1152]{1,0:T(8,128)(2,1)S(1)}, u32[]{:S(2)}, u32[]{:S(2)}) collective-permute-start(bf16[144,1152]{1,0:T(8,128)(2,1)S(1)} %collective-permute-done.4.refs_2_), channel_id=1, source_target_pairs={{0,16},{16,0},{1,17},{17,1},{2,18},{18,2},{3,19},{19,3},{4,20},{20... | collective-permute-start | bytes 995336 | tf_op jit(solution)/shard_map/ppermute | solution.py:425
  13.8 8.6 %collective-permute-start.8 = (bf16[144,1152]{1,0:T(8,128)(2,1)S(1)}, bf16[144,1152]{1,0:T(8,128)(2,1)S(1)}, u32[]{:S(2)}, u32[]{:S(2)}) collective-permute-start(bf16[144,1152]{1,0:T(8,128)(2,1)S(1)} %collective-permute-done.1.refs_1_.refs_6_), channel_id=1, source_target_pairs={{0,1},{1,0},{2,3},{3,2},{4,5},{5,4},{6,7},{7,6},{8,9},{9,8},{10,11... | collective-permute-start | bytes 995336 | tf_op jit(solution)/shard_map/ppermute | solution.py:428
  13.9 8.6 %collective-permute-start.3 = (bf16[144,1152]{1,0:T(8,128)(2,1)S(1)}, bf16[144,1152]{1,0:T(8,128)(2,1)S(1)}, u32[]{:S(2)}, u32[]{:S(2)}) collective-permute-start(bf16[144,1152]{1,0:T(8,128)(2,1)S(1)} %collective-permute-done.1.refs_1_.refs_6_), channel_id=1, source_target_pairs={{0,4},{1,3},{4,8},{5,1},{8,12},{9,5},{12,14},{13,9},{14,10},{15,13... | collective-permute-start | bytes 995336 | tf_op jit(solution)/shard_map/ppermute | solution.py:422
  17.4 7.2 %collective-permute-start.13 = (bf16[144,1152]{1,0:T(8,128)(2,1)S(1)}, bf16[144,1152]{1,0:T(8,128)(2,1)S(1)}, u32[]{:S(2)}, u32[]{:S(2)}) collective-permute-start(bf16[144,1152]{1,0:T(8,128)(2,1)S(1)} %shard_map.139.refs_1_.refs_3_), channel_id=1, source_target_pairs={{0,4},{1,3},{4,8},{5,1},{8,12},{9,5},{12,14},{13,9},{14,10},{15,13... | collective-permute-start | bytes 995336 | tf_op jit(solution)/shard_map/ppermute | solution.py:422
  20.9 9.1 %collective-permute-start.2 = (bf16[144,1152]{1,0:T(8,128)(2,1)S(1)}, bf16[144,1152]{1,0:T(8,128)(2,1)S(1)}, u32[]{:S(2)}, u32[]{:S(2)}) collective-permute-start(bf16[144,1152]{1,0:T(8,128)(2,1)S(1)} %collective-permute-done.1.refs_1_.refs_6_), channel_id=1, source_target_pairs={{0,16},{16,0},{1,17},{17,1},{2,18},{18,2},{3,19},{19,3},{4,20},{20... | collective-permute-start | bytes 995336 | tf_op jit(solution)/shard_map/ppermute | solution.py:425
  22.5 9.0 %collective-permute-start.12 = (bf16[144,1152]{1,0:T(8,128)(2,1)S(1)}, bf16[144,1152]{1,0:T(8,128)(2,1)S(1)}, u32[]{:S(2)}, u32[]{:S(2)}) collective-permute-start(bf16[144,1152]{1,0:T(8,128)(2,1)S(1)} %shard_map.140.refs_1_.refs_7_), channel_id=1, source_target_pairs={{0,1},{1,0},{2,3},{3,2},{4,5},{5,4},{6,7},{7,6},{8,9},{9,8},{10,11... | collective-permute-start | bytes 995336 | tf_op jit(solution)/shard_map/ppermute | solution.py:428
  23.0 8.5 %collective-permute-start.9 = (bf16[144,1152]{1,0:T(8,128)(2,1)S(1)}, bf16[144,1152]{1,0:T(8,128)(2,1)S(1)}, u32[]{:S(2)}, u32[]{:S(2)}) collective-permute-start(bf16[144,1152]{1,0:T(8,128)(2,1)S(1)} %shard_map.140.refs_1_.refs_7_), channel_id=1, source_target_pairs={{0,4},{1,3},{4,8},{5,1},{8,12},{9,5},{12,14},{13,9},{14,10},{15,13... | collective-permute-start | bytes 995336 | tf_op jit(solution)/shard_map/ppermute | solution.py:422
  24.6 9.1 %collective-permute-start.14 = (bf16[144,1152]{1,0:T(8,128)(2,1)S(1)}, bf16[144,1152]{1,0:T(8,128)(2,1)S(1)}, u32[]{:S(2)}, u32[]{:S(2)}) collective-permute-start(bf16[144,1152]{1,0:T(8,128)(2,1)S(1)} %shard_map.142.refs_4_), channel_id=1, source_target_pairs={{0,4},{1,3},{4,8},{5,1},{8,12},{9,5},{12,14},{13,9},{14,10},{15,13... | collective-permute-start | bytes 995336 | tf_op jit(solution)/shard_map/ppermute | solution.py:422
  26.7 10.5 %collective-permute-start.19 = (bf16[144,1152]{1,0:T(8,128)(2,1)S(1)}, bf16[144,1152]{1,0:T(8,128)(2,1)S(1)}, u32[]{:S(2)}, u32[]{:S(2)}) collective-permute-start(bf16[144,1152]{1,0:T(8,128)(2,1)S(1)} %collective-permute-done.10.refs_2_.refs_18_), channel_id=1, source_target_pairs={{0,4},{1,3},{4,8},{5,1},{8,12},{9,5},{12,14},{13,9},{14,10},{15,13... | collective-permute-start | bytes 995336 | tf_op jit(solution)/shard_map/ppermute | solution.py:422
  30.0 8.1 %collective-permute-start.20 = (bf16[144,1152]{1,0:T(8,128)(2,1)S(1)}, bf16[144,1152]{1,0:T(8,128)(2,1)S(1)}, u32[]{:S(2)}, u32[]{:S(2)}) collective-permute-start(bf16[144,1152]{1,0:T(8,128)(2,1)S(1)} %shard_map.142.refs_4_), channel_id=1, source_target_pairs={{0,16},{16,0},{1,17},{17,1},{2,18},{18,2},{3,19},{19,3},{4,20},{20... | collective-permute-start | bytes 995336 | tf_op jit(solution)/shard_map/ppermute | solution.py:425
  31.5 6.6 %collective-permute-start.18 = (bf16[144,1152]{1,0:T(8,128)(2,1)S(1)}, bf16[144,1152]{1,0:T(8,128)(2,1)S(1)}, u32[]{:S(2)}, u32[]{:S(2)}) collective-permute-start(bf16[144,1152]{1,0:T(8,128)(2,1)S(1)} %collective-permute-done.9.refs_4_.refs_2_.refs_8_), channel_id=1, source_target_pairs={{0,1},{1,0},{2,3},{3,2},{4,5},{5,4},{6,7},{7,6},{8,9},{9,8},{10,11... | collective-permute-start | bytes 995336 | tf_op jit(solution)/shard_map/ppermute | solution.py:428
  33.6 4.9 %collective-permute-start.17 = (bf16[144,1152]{1,0:T(8,128)(2,1)S(1)}, bf16[144,1152]{1,0:T(8,128)(2,1)S(1)}, u32[]{:S(2)}, u32[]{:S(2)}) collective-permute-start(bf16[144,1152]{1,0:T(8,128)(2,1)S(1)} %shard_map.143.refs_5_), channel_id=1, source_target_pairs={{0,1},{1,0},{2,3},{3,2},{4,5},{5,4},{6,7},{7,6},{8,9},{9,8},{10,11... | collective-permute-start | bytes 995336 | tf_op jit(solution)/shard_map/ppermute | solution.py:428
  33.6 7.1 %collective-permute-start.22 = (bf16[144,1152]{1,0:T(8,128)(2,1)S(1)}, bf16[144,1152]{1,0:T(8,128)(2,1)S(1)}, u32[]{:S(2)}, u32[]{:S(2)}) collective-permute-start(bf16[144,1152]{1,0:T(8,128)(2,1)S(1)} %get-tuple-element.32.refs_1_.refs_22_), channel_id=1, source_target_pairs={{0,4},{1,3},{4,8},{5,1},{8,12},{9,5},{12,14},{13,9},{14,10},{15,13... | collective-permute-start | bytes 995336 | tf_op jit(solution)/shard_map/ppermute | solution.py:422
  37.2 5.1 %collective-permute-start.15 = (bf16[144,1152]{1,0:T(8,128)(2,1)S(1)}, bf16[144,1152]{1,0:T(8,128)(2,1)S(1)}, u32[]{:S(2)}, u32[]{:S(2)}) collective-permute-start(bf16[144,1152]{1,0:T(8,128)(2,1)S(1)} %shard_map.139.refs_1_.refs_3_), channel_id=1, source_target_pairs={{0,1},{1,0},{2,3},{3,2},{4,5},{5,4},{6,7},{7,6},{8,9},{9,8},{10,11... | collective-permute-start | bytes 995336 | tf_op jit(solution)/shard_map/ppermute | solution.py:428
  38.1 4.8 %collective-permute-start.16 = (bf16[144,1152]{1,0:T(8,128)(2,1)S(1)}, bf16[144,1152]{1,0:T(8,128)(2,1)S(1)}, u32[]{:S(2)}, u32[]{:S(2)}) collective-permute-start(bf16[144,1152]{1,0:T(8,128)(2,1)S(1)} %shard_map.142.refs_4_), channel_id=1, source_target_pairs={{0,1},{1,0},{2,3},{3,2},{4,5},{5,4},{6,7},{7,6},{8,9},{9,8},{10,11... | collective-permute-start | bytes 995336 | tf_op jit(solution)/shard_map/ppermute | solution.py:428
  38.6 9.8 %collective-permute-start.21 = (bf16[144,1152]{1,0:T(8,128)(2,1)S(1)}, bf16[144,1152]{1,0:T(8,128)(2,1)S(1)}, u32[]{:S(2)}, u32[]{:S(2)}) collective-permute-start(bf16[144,1152]{1,0:T(8,128)(2,1)S(1)} %shard_map.143.refs_5_), channel_id=1, source_target_pairs={{0,16},{16,0},{1,17},{17,1},{2,18},{18,2},{3,19},{19,3},{4,20},{20... | collective-permute-start | bytes 995336 | tf_op jit(solution)/shard_map/ppermute | solution.py:425
  40.8 7.6 %collective-permute-start.23 = (bf16[144,1152]{1,0:T(8,128)(2,1)S(1)}, bf16[144,1152]{1,0:T(8,128)(2,1)S(1)}, u32[]{:S(2)}, u32[]{:S(2)}) collective-permute-start(bf16[144,1152]{1,0:T(8,128)(2,1)S(1)} %shard_map.144.refs_23_), channel_id=1, source_target_pairs={{0,4},{1,3},{4,8},{5,1},{8,12},{9,5},{12,14},{13,9},{14,10},{15,13... | collective-permute-start | bytes 995336 | tf_op jit(solution)/shard_map/ppermute | solution.py:422
  42.3 6.5 %collective-permute-start.27 = (bf16[144,1152]{1,0:T(8,128)(2,1)S(1)}, bf16[144,1152]{1,0:T(8,128)(2,1)S(1)}, u32[]{:S(2)}, u32[]{:S(2)}) collective-permute-start(bf16[144,1152]{1,0:T(8,128)(2,1)S(1)} %get-tuple-element.32.refs_1_.refs_22_), channel_id=1, source_target_pairs={{0,1},{1,0},{2,3},{3,2},{4,5},{5,4},{6,7},{7,6},{8,9},{9,8},{10,11... | collective-permute-start | bytes 995336 | tf_op jit(solution)/shard_map/ppermute | solution.py:428
  42.4 6.4 %collective-permute-start.25 = (bf16[144,1152]{1,0:T(8,128)(2,1)S(1)}, bf16[144,1152]{1,0:T(8,128)(2,1)S(1)}, u32[]{:S(2)}, u32[]{:S(2)}) collective-permute-start(bf16[144,1152]{1,0:T(8,128)(2,1)S(1)} %collective-permute-done.20.refs_3_.refs_20_), channel_id=1, source_target_pairs={{0,1},{1,0},{2,3},{3,2},{4,5},{5,4},{6,7},{7,6},{8,9},{9,8},{10,11... | collective-permute-start | bytes 995336 | tf_op jit(solution)/shard_map/ppermute | solution.py:428
  42.9 7.1 %collective-permute-start.28 = (bf16[144,1152]{1,0:T(8,128)(2,1)S(1)}, bf16[144,1152]{1,0:T(8,128)(2,1)S(1)}, u32[]{:S(2)}, u32[]{:S(2)}) collective-permute-start(bf16[144,1152]{1,0:T(8,128)(2,1)S(1)} %shard_map.144.refs_23_), channel_id=1, source_target_pairs={{0,1},{1,0},{2,3},{3,2},{4,5},{5,4},{6,7},{7,6},{8,9},{9,8},{10,11... | collective-permute-start | bytes 995336 | tf_op jit(solution)/shard_map/ppermute | solution.py:428
  62.1 7.5 %collective-permute-start.31 = (bf16[32,2304]{1,0:T(8,128)(2,1)S(1)}, bf16[32,2304]{1,0:T(8,128)(2,1)S(1)}, u32[]{:S(2)}, u32[]{:S(2)}) collective-permute-start(bf16[32,2304]{1,0:T(8,128)(2,1)S(1)} %get-tuple-element.36), channel_id=1, source_target_pairs={{0,2},{1,3},{2,0},{3,1},{4,6},{5,7},{6,4},{7,5},{8,10},{9,11},{10,... | collective-permute-start | bytes 442376 | tf_op jit(solution)/shard_map/ppermute | solution.py:585
  65.4 6.7 %collective-permute-start.32 = (bf16[32,2304]{1,0:T(8,128)(2,1)S(1)}, bf16[32,2304]{1,0:T(8,128)(2,1)S(1)}, u32[]{:S(2)}, u32[]{:S(2)}) collective-permute-start(bf16[32,2304]{1,0:T(8,128)(2,1)S(1)} %get-tuple-element.37), channel_id=1, source_target_pairs={{0,4},{1,5},{2,6},{3,7},{4,0},{5,1},{6,2},{7,3},{8,12},{9,13},{10,... | collective-permute-start | bytes 442376 | tf_op jit(solution)/shard_map/ppermute | solution.py:585
  66.6 7.4 %collective-permute-start.33 = (bf16[32,2304]{1,0:T(8,128)(2,1)S(1)}, bf16[32,2304]{1,0:T(8,128)(2,1)S(1)}, u32[]{:S(2)}, u32[]{:S(2)}) collective-permute-start(bf16[32,2304]{1,0:T(8,128)(2,1)S(1)} %get-tuple-element.38), channel_id=1, source_target_pairs={{0,6},{1,7},{2,4},{3,5},{4,2},{5,3},{6,0},{7,1},{8,14},{9,15},{10,... | collective-permute-start | bytes 442376 | tf_op jit(solution)/shard_map/ppermute | solution.py:585
  77.9 6.0 %collective-permute-start.35 = (bf16[32,2304]{1,0:T(8,128)(2,1)S(1)}, bf16[32,2304]{1,0:T(8,128)(2,1)S(1)}, u32[]{:S(2)}, u32[]{:S(2)}) collective-permute-start(bf16[32,2304]{1,0:T(8,128)(2,1)S(1)} %get-tuple-element.42), channel_id=1, source_target_pairs={{0,2},{1,3},{2,0},{3,1},{4,6},{5,7},{6,4},{7,5},{8,10},{9,11},{10,... | collective-permute-start | bytes 442376 | tf_op jit(solution)/shard_map/ppermute | solution.py:585
  79.6 6.7 %collective-permute-start.36 = (bf16[32,2304]{1,0:T(8,128)(2,1)S(1)}, bf16[32,2304]{1,0:T(8,128)(2,1)S(1)}, u32[]{:S(2)}, u32[]{:S(2)}) collective-permute-start(bf16[32,2304]{1,0:T(8,128)(2,1)S(1)} %get-tuple-element.43), channel_id=1, source_target_pairs={{0,4},{1,5},{2,6},{3,7},{4,0},{5,1},{6,2},{7,3},{8,12},{9,13},{10,... | collective-permute-start | bytes 442376 | tf_op jit(solution)/shard_map/ppermute | solution.py:585
  80.8 7.3 %collective-permute-start.37 = (bf16[32,2304]{1,0:T(8,128)(2,1)S(1)}, bf16[32,2304]{1,0:T(8,128)(2,1)S(1)}, u32[]{:S(2)}, u32[]{:S(2)}) collective-permute-start(bf16[32,2304]{1,0:T(8,128)(2,1)S(1)} %get-tuple-element.44), channel_id=1, source_target_pairs={{0,6},{1,7},{2,4},{3,5},{4,2},{5,3},{6,0},{7,1},{8,14},{9,15},{10,... | collective-permute-start | bytes 442376 | tf_op jit(solution)/shard_map/ppermute | solution.py:585
  94.3 13.3 %all-to-all-start = ((bf16[16,2,1152]{2,1,0:T(2,128)(2,1)}), bf16[16,2,1152]{2,1,0:T(2,128)(2,1)S(1)}, u32[]{:S(2)}, u32[]{:S(2)}) async-start(bf16[16,2,1152]{2,1,0:T(2,128)(2,1)} %shard_map.151), calls=%async_computation | async-start | bytes 147456 | tf_op jit(solution)/shard_map/all_to_all | solution.py:627
  (16 other events, 210.3 us)

commit v2 on v0

--- a/solution.py
+++ b/solution.py
@@ -163,16 +163,6 @@
     return lax.rem(ids((1, rows.total), 1), rows.shard) >= rows.qkv
 
 
-def weight_copies(layout, order, pieces, target, sems, which):
-    count = target.shape[1]
-    return [
-        pltpu.make_async_copy(
-            pieces[piece].at[pl.ds(first, count)], target.at[order[index]], sems.at[which, index]
-        )
-        for index, (piece, first) in enumerate(layout)
-    ]
-
-
 def gate(rows, *events, others=()):
     anywhere = pl.BlockSpec(memory_space=pl.ANY)
     arrays = (rows, *others)
@@ -188,27 +178,22 @@
     return results if others else results[0]
 
 
-def start_weights(layouts, order, pieces, space, time, sems):
-    def start(first, second):
-        for copy in weight_copies(first, order, pieces, space, sems, 0):
-            copy.start()
-        for copy in weight_copies(second, order, pieces, time, sems, 1):
-            copy.start()
-
-    plane = order[len(layouts[0])]
-
-    @pl.when(plane == 0)
+def assemble(layouts, order, pieces, space, time):
+    count = space.shape[1]
+
+    def put(layout, target):
+        for index, (piece, first) in enumerate(layout):
+            target[order[index]] = pieces[piece][first : first + count, :]
+
+    @pl.when(order[-1] == 0)
     def _():
-        start(layouts[0], layouts[1])
-
-    @pl.when(plane != 0)
+        put(layouts[0], space)
+        put(layouts[1], time)
+
+    @pl.when(order[-1] != 0)
     def _():
-        start(layouts[1], layouts[0])
-
-
-def wait_weights(layouts, order, pieces, target, sems, which):
-    for copy in weight_copies(layouts[0], order, pieces, target, sems, which):
-        copy.wait()
+        put(layouts[1], space)
+        put(layouts[0], time)
 
 
 def give(direct, stage, outs):
@@ -246,25 +231,16 @@
 
 def front(rows, layouts, order_of, direct, clips, tokens, gains, *refs):
     sends = 2 if direct else 1
-    pieces, refs = refs[: -9 - sends], refs[-9 - sends :]
+    pieces, refs = refs[: -8 - sends], refs[-8 - sends :]
     hidden, saved, shares_out, space, time = refs[:5]
-    project, mixed, stage, sems = refs[-4:]
-    order = order_of()
-    start_weights(layouts, order, pieces, space, time, sems)
+    project, mixed, stage = refs[-3:]
+    assemble(layouts, order_of(), pieces, space, time)
     allowed, live = space_masks(clips)
     values = tokens[0].astype(F32)
     normed = (values * inverse_size(values) * gains[:1]).astype(BF16)
     mixed[...] = jnp.zeros_like(mixed)
     stride = rows.qkv_cut
-    length = stride if len(layouts[0]) > 1 else rows.total
-
-    def project_from(layout):
-        for index, (piece, first) in enumerate(layout):
-            target = pl.ds(pl.multiple_of(order[index] * length, 16), length)
-            project[target, :] = nt(pieces[piece][first : first + length, :], normed)
-
-    pl.when(order[-1] == 0)(lambda: project_from(layouts[0]))
-    pl.when(order[-1] != 0)(lambda: project_from(layouts[1]))
+    project[...] = nt(rows.qkv_weight(space), normed)
     saved[...] = project[...].astype(BF16)
     scale = rows.head ** (-0.5)
     queries, keys, values_in = (
@@ -276,17 +252,15 @@
     for head in range(HEADS):
         shares_out[head] = shares[head]
         write_rows(mixed, rows.out_spans(head, rows.out_cut), blended[head])
-    wait_weights(layouts, order, pieces, space, sems, 0)
     update = tn(mixed[...].astype(BF16), rows.out_weight(space))
     low = (values + update).astype(BF16)
     hidden[...] = low
     values = low.astype(F32)
     normed = (values * inverse_size(values) * gains[1:]).astype(BF16)
-    wait_weights(layouts, order, pieces, time, sems, 1)
     both = nt(jnp.concatenate([normed, tokens[1]], axis=0), time[...].reshape(rows.total, -1))
     count = values.shape[0]
     stage[...] = jnp.where(out_columns(rows), both[count:], both[:count]).astype(BF16)
-    give(direct, stage, refs[5:-4])
+    give(direct, stage, refs[5:-3])
 
 
 def time_core(rows, near, slots, direct, clips, *refs):
@@ -329,7 +303,7 @@
     give(direct, stage, refs[direct or 1 : -3])
 
 
-def time_back(rows, direct, clips, *refs):
+def time_back(rows, direct, factor, clips, *refs):
     arrived, refs = refs[: direct or 1], refs[direct or 1 :]
     tokens, gains, time, space, hidden, saved, shares_in = refs[:7]
     grad_hidden_out, grad_normed_out, gain_parts, project, grad_project, stage = refs[7:]
@@ -366,7 +340,8 @@
     values = tokens[0].astype(F32)
     normed = values * inverse_size(values)
     grad_space_gain = jnp.sum(grad_normed.astype(F32) * normed, axis=0, keepdims=True)
-    both_gains = jnp.concatenate([grad_space_gain, grad_time_gain], axis=0).astype(gain_parts.dtype)
+    both_gains = jnp.concatenate([grad_space_gain, grad_time_gain], axis=0) * factor
+    both_gains = both_gains.astype(gain_parts.dtype)
     gain_parts[...] = jnp.broadcast_to(both_gains[None], gain_parts.shape)
 
 
@@ -428,6 +403,7 @@
     t0 = twin(own)
     o1 = ring(own)
     t1 = ring(t0)
+    t1 = gate(t1, o1)
     t0_other = twin(own_other)
     o2 = ring(o1)
     x_o1 = across(o1)
@@ -448,18 +424,18 @@
     o4 = gate(o4, x_t1, t3)
     x_o3 = across(o3)
     o3_twin = twin(o3)
-    x_o2 = ring(x_o1)
     t3_twin = twin(t3)
     x_t1_twin = twin(x_t1)
     x_t2 = ring(x_t1)
-    x_o4 = across(o4)
+    x_o4 = ring(x_o3)
+    x_o4_twin = twin(x_o4)
     o4_twin = twin(o4)
+    x_o3_twin = twin(x_o3)
+    x_o2 = ring(x_o1)
     x_t2 = gate(x_t2, o4_twin, t3_twin, x_o3, x_o2)
     x_t3 = ring(x_t2)
     x_o2_twin = twin(x_o2)
     x_t2_twin = twin(x_t2)
-    x_o3_twin = twin(x_o3)
-    x_o4_twin = twin(x_o4)
     x_t3_twin = twin(x_t3)
     mine = {"o0": (own, 0), "t0": (t0, 0)}
     other = {"o0": (own_other, 0), "t0": (t0_other, 0)}
@@ -551,7 +527,6 @@
     qkv_wide = pltpu.VMEM((rows.qkv_total, FRAME), F32)
     out_wide = pltpu.VMEM((rows.out_total, FRAME), F32)
     blocks = len(layouts[0])
-    sems = pltpu.SemaphoreType.DMA((2, blocks))
     weight_shape = jax.ShapeDtypeStruct((blocks, rows.total // blocks, features), BF16)
     groups = [list(range(first, first + near)) for first in range(0, size, near)]
 
@@ -592,7 +567,7 @@
             weight_shape,
             *parts,
         ),
-        [qkv_wide, out_wide, stage, sems],
+        [qkv_wide, out_wide, stage],
         clips,
         (both_tokens, both_gains, *pieces),
     )
@@ -607,7 +582,7 @@
     arrived = exchange(sent)
     whole = jax.ShapeDtypeStruct((FRAME, features), BF16)
     grad_hidden, grad_normed, gains = call(
-        functools.partial(time_back, rows, direct),
+        functools.partial(time_back, rows, direct, 1.0 / math.sqrt(everyone * FRAME)),
         (whole, whole, jax.ShapeDtypeStruct((everyone, 2, features), BF16)),
         [out_wide, qkv_wide, stage],
         clips,
@@ -621,7 +596,7 @@
         None,
         (*arrived, both_tokens, both_gains, time_weights, hidden, grad_hidden, grad_normed),
     )
-    gain_grads = jnp.sum(gains.astype(F32), axis=0) * (1.0 / math.sqrt(everyone * FRAME))
+    gain_grads = jnp.sum(gains.astype(F32), axis=0)
     return result[None], grad_tokens[None], gain_grads
 
 

time: 107 us -> 105 us (0.981)
  waiting for transfers between devices: 40.1 us -> 42.7 us
  Pallas kernels: 19 us -> 16.5 us
  starting transfers between devices: 40.8 us -> 38.6 us
    ppermute x10 -> x11, waiting for transfers between devices: 9.79 us -> 17.9 us  [ring(): return lax.ppermute(rows, 'ctx', ring_pairs)]
    ppermute x4 -> x3, waiting for transfers between devices: 7.9 us -> 2.45 us  [across(): lax.ppermute(rows, 'dp', [(index, index ^ 1) for index in range(planes)])]
    pallas_call x6, Pallas kernels: 19 us -> 16.5 us  [call(): pl.pallas_call(body, out_shape=out_shapes, in_specs=[scalars] * len(clips...]
    ppermute x4 -> x3, starting transfers between devices: 6.03 us -> 4.54 us  [across(): lax.ppermute(rows, 'dp', [(index, index ^ 1) for index in range(planes)])]
    ppermute x6, starting transfers between devices: 8.43 us -> 7.18 us  [exchange(): lax.ppermute(rows_away, 'ctx', [(index, index ^ 2 * distance) for index i...]
    ppermute x10 -> x11, starting transfers between devices: 18.8 us -> 19.7 us  [ring(): return lax.ppermute(rows, 'ctx', ring_pairs)]
where the time goes in v2:
time: 105 us
  waiting for transfers between devices  42.7 us (41%)
  starting transfers between devices  38.6 us (37%)
  Pallas kernels  16.5 us (16%)
  local copies, waits for them, and re-layouts  3.93 us (4%)
  other arithmetic  2.2 us (2%)
    ppermute x11, starting transfers between devices, ring(): return lax.ppermute(rows, 'ctx', ring_pairs)  19.7 us
    ppermute x11, waiting for transfers between devices, ring(): return lax.ppermute(rows, 'ctx', ring_pairs)  17.9 us
    pallas_call x6, Pallas kernels, call(): pl.pallas_call(body, out_shape=out_shapes, in_specs=[scalars] * len(clips...  16.5 us
    ppermute x6, waiting for transfers between devices, exchange(): lax.ppermute(rows_away, 'ctx', [(index, index ^ 2 * distance) for index i...  13.8 us
    ppermute x6, starting transfers between devices, exchange(): lax.ppermute(rows_away, 'ctx', [(index, index ^ 2 * distance) for index i...  7.18 us
    all_to_all x1, starting transfers between devices, shards(): lax.all_to_all(gains, ('dp', 'ctx'), split_axis=0, concat_axis=0, tiled=T...  4.62 us
    ppermute x3, starting transfers between devices, across(): lax.ppermute(rows, 'dp', [(index, index ^ 1) for index in range(planes)])  4.54 us
    all_to_all x1, waiting for transfers between devices, shards(): lax.all_to_all(gains, ('dp', 'ctx'), split_axis=0, concat_axis=0, tiled=T...  3.97 us
  transfers between devices with their start and end apart: 39, of which 19 were waited for; matrix products, arithmetic and copies ran while one was open for 1% of the time, Pallas kernels for 2%

profile of v2, /device:TPU:0, one launch (start us, length us, event | category | flops | bytes accessed | tf_op | source)
XLA Modules:
  0.0 104.7 jit_solution(9763755202508164063)
XLA Ops:
  2.6 2.6 %collective-permute-start.2 = (bf16[144,1152]{1,0:T(8,128)(2,1)S(1)}, bf16[144,1152]{1,0:T(8,128)(2,1)S(1)}, u32[]{:S(2)}, u32[]{:S(2)}) collective-permute-start(bf16[144,1152]{1,0:T(8,128)(2,1)S(1)} %get-tuple-element.56.refs_0_), channel_id=1, source_target_pairs={{0,4},{1,3},{4,8},{5,1},{8,12},{9,5},{12,14},{13,9},{14,10},{15,13... | collective-permute-start | bytes 995336 | tf_op jit(solution)/shard_map/ppermute | solution.py:393
  5.2 1.6 %collective-permute-start.1 = (bf16[144,1152]{1,0:T(8,128)(2,1)S(1)}, bf16[144,1152]{1,0:T(8,128)(2,1)S(1)}, u32[]{:S(2)}, u32[]{:S(2)}) collective-permute-start(bf16[144,1152]{1,0:T(8,128)(2,1)S(1)} %collective-permute-done.refs_1_), channel_id=1, source_target_pairs={{0,4},{1,3},{4,8},{5,1},{8,12},{9,5},{12,14},{13,9},{14,10},{15,13... | collective-permute-start | bytes 995336 | tf_op jit(solution)/shard_map/ppermute | solution.py:393
  6.8 3.5 %collective-permute-done.2.refs_1_.refs_2_ = bf16[144,1152]{1,0:T(8,128)(2,1)S(1)} collective-permute-done((bf16[144,1152]{1,0:T(8,128)(2,1)S(1)}, bf16[144,1152]{1,0:T(8,128)(2,1)S(1)}, u32[]{:S(2)}, u32[]{:S(2)}) %collective-permute-start.2) | collective-permute-done | bytes 331808 | tf_op jit(solution)/shard_map/ppermute | solution.py:393
  10.3 2.1 %collective-permute-start.5 = (bf16[144,1152]{1,0:T(8,128)(2,1)S(1)}, bf16[144,1152]{1,0:T(8,128)(2,1)S(1)}, u32[]{:S(2)}, u32[]{:S(2)}) collective-permute-start(bf16[144,1152]{1,0:T(8,128)(2,1)S(1)} %collective-permute-done.2.refs_1_.refs_2_), channel_id=1, source_target_pairs={{0,4},{1,3},{4,8},{5,1},{8,12},{9,5},{12,14},{13,9},{14,10},{15,13... | collective-permute-start | bytes 995336 | tf_op jit(solution)/shard_map/ppermute | solution.py:393
  13.9 2.1 %collective-permute-start.4 = (bf16[144,1152]{1,0:T(8,128)(2,1)S(1)}, bf16[144,1152]{1,0:T(8,128)(2,1)S(1)}, u32[]{:S(2)}, u32[]{:S(2)}) collective-permute-start(bf16[144,1152]{1,0:T(8,128)(2,1)S(1)} %shard_map.139.refs_1_.refs_6_), channel_id=1, source_target_pairs={{0,4},{1,3},{4,8},{5,1},{8,12},{9,5},{12,14},{13,9},{14,10},{15,13... | collective-permute-start | bytes 995336 | tf_op jit(solution)/shard_map/ppermute | solution.py:393
  17.4 2.1 %collective-permute-start.13 = (bf16[144,1152]{1,0:T(8,128)(2,1)S(1)}, bf16[144,1152]{1,0:T(8,128)(2,1)S(1)}, u32[]{:S(2)}, u32[]{:S(2)}) collective-permute-start(bf16[144,1152]{1,0:T(8,128)(2,1)S(1)} %shard_map.140.refs_1_.refs_3_), channel_id=1, source_target_pairs={{0,4},{1,3},{4,8},{5,1},{8,12},{9,5},{12,14},{13,9},{14,10},{15,13... | collective-permute-start | bytes 995336 | tf_op jit(solution)/shard_map/ppermute | solution.py:393
  23.0 1.6 %collective-permute-start.9 = (bf16[144,1152]{1,0:T(8,128)(2,1)S(1)}, bf16[144,1152]{1,0:T(8,128)(2,1)S(1)}, u32[]{:S(2)}, u32[]{:S(2)}) collective-permute-start(bf16[144,1152]{1,0:T(8,128)(2,1)S(1)} %shard_map.141.refs_1_.refs_7_), channel_id=1, source_target_pairs={{0,4},{1,3},{4,8},{5,1},{8,12},{9,5},{12,14},{13,9},{14,10},{15,13... | collective-permute-start | bytes 995336 | tf_op jit(solution)/shard_map/ppermute | solution.py:393
  24.6 2.0 %collective-permute-start.14 = (bf16[144,1152]{1,0:T(8,128)(2,1)S(1)}, bf16[144,1152]{1,0:T(8,128)(2,1)S(1)}, u32[]{:S(2)}, u32[]{:S(2)}) collective-permute-start(bf16[144,1152]{1,0:T(8,128)(2,1)S(1)} %shard_map.143.refs_4_), channel_id=1, source_target_pairs={{0,4},{1,3},{4,8},{5,1},{8,12},{9,5},{12,14},{13,9},{14,10},{15,13... | collective-permute-start | bytes 995336 | tf_op jit(solution)/shard_map/ppermute | solution.py:393
  26.8 1.6 %collective-permute-start.19 = (bf16[144,1152]{1,0:T(8,128)(2,1)S(1)}, bf16[144,1152]{1,0:T(8,128)(2,1)S(1)}, u32[]{:S(2)}, u32[]{:S(2)}) collective-permute-start(bf16[144,1152]{1,0:T(8,128)(2,1)S(1)} %collective-permute-done.10.refs_2_.refs_18_), channel_id=1, source_target_pairs={{0,4},{1,3},{4,8},{5,1},{8,12},{9,5},{12,14},{13,9},{14,10},{15,13... | collective-permute-start | bytes 995336 | tf_op jit(solution)/shard_map/ppermute | solution.py:393
  28.4 1.6 %collective-permute-done.3.refs_0_ = bf16[144,1152]{1,0:T(8,128)(2,1)S(1)} collective-permute-done((bf16[144,1152]{1,0:T(8,128)(2,1)S(1)}, bf16[144,1152]{1,0:T(8,128)(2,1)S(1)}, u32[]{:S(2)}, u32[]{:S(2)}) %collective-permute-start.3) | collective-permute-done | bytes 331808 | tf_op jit(solution)/shard_map/ppermute | solution.py:396
  31.5 2.2 %collective-permute-done.14.refs_0_ = bf16[144,1152]{1,0:T(8,128)(2,1)S(1)} collective-permute-done((bf16[144,1152]{1,0:T(8,128)(2,1)S(1)}, bf16[144,1152]{1,0:T(8,128)(2,1)S(1)}, u32[]{:S(2)}, u32[]{:S(2)}) %collective-permute-start.14) | collective-permute-done | bytes 331808 | tf_op jit(solution)/shard_map/ppermute | solution.py:393
  33.6 1.6 %collective-permute-start.22 = (bf16[144,1152]{1,0:T(8,128)(2,1)S(1)}, bf16[144,1152]{1,0:T(8,128)(2,1)S(1)}, u32[]{:S(2)}, u32[]{:S(2)}) collective-permute-start(bf16[144,1152]{1,0:T(8,128)(2,1)S(1)} %get-tuple-element.32.refs_1_.refs_22_), channel_id=1, source_target_pairs={{0,4},{1,3},{4,8},{5,1},{8,12},{9,5},{12,14},{13,9},{14,10},{15,13... | collective-permute-start | bytes 995336 | tf_op jit(solution)/shard_map/ppermute | solution.py:393
  35.2 2.0 %collective-permute-done.19.refs_4_.refs_19_ = bf16[144,1152]{1,0:T(8,128)(2,1)S(1)} collective-permute-done((bf16[144,1152]{1,0:T(8,128)(2,1)S(1)}, bf16[144,1152]{1,0:T(8,128)(2,1)S(1)}, u32[]{:S(2)}, u32[]{:S(2)}) %collective-permute-start.19) | collective-permute-done | bytes 331808 | tf_op jit(solution)/shard_map/ppermute | solution.py:393
  40.8 1.6 %collective-permute-start.23 = (bf16[144,1152]{1,0:T(8,128)(2,1)S(1)}, bf16[144,1152]{1,0:T(8,128)(2,1)S(1)}, u32[]{:S(2)}, u32[]{:S(2)}) collective-permute-start(bf16[144,1152]{1,0:T(8,128)(2,1)S(1)} %shard_map.145.refs_23_), channel_id=1, source_target_pairs={{0,4},{1,3},{4,8},{5,1},{8,12},{9,5},{12,14},{13,9},{14,10},{15,13... | collective-permute-start | bytes 995336 | tf_op jit(solution)/shard_map/ppermute | solution.py:393
  43.1 3.9 %collective-permute-done.21.refs_21_ = bf16[144,1152]{1,0:T(8,128)(2,1)S(1)} collective-permute-done((bf16[144,1152]{1,0:T(8,128)(2,1)S(1)}, bf16[144,1152]{1,0:T(8,128)(2,1)S(1)}, u32[]{:S(2)}, u32[]{:S(2)}) %collective-permute-start.21) | collective-permute-done | bytes 331808 | tf_op jit(solution)/shard_map/ppermute | solution.py:393
  47.0 3.6 %collective-permute-done.23.refs_24_ = bf16[144,1152]{1,0:T(8,128)(2,1)S(1)} collective-permute-done((bf16[144,1152]{1,0:T(8,128)(2,1)S(1)}, bf16[144,1152]{1,0:T(8,128)(2,1)S(1)}, u32[]{:S(2)}, u32[]{:S(2)}) %collective-permute-start.23) | collective-permute-done | bytes 331808 | tf_op jit(solution)/shard_map/ppermute | solution.py:393
  50.5 1.6 %collective-permute-done.29.refs_31_ = bf16[144,1152]{1,0:T(8,128)(2,1)S(1)} collective-permute-done((bf16[144,1152]{1,0:T(8,128)(2,1)S(1)}, bf16[144,1152]{1,0:T(8,128)(2,1)S(1)}, u32[]{:S(2)}, u32[]{:S(2)}) %collective-permute-start.29) | collective-permute-done | bytes 331808 | tf_op jit(solution)/shard_map/ppermute | solution.py:399
  52.1 7.4 %shard_map.146 = (bf16[128,1152]{1,0:T(8,128)(2,1)S(1)}, bf16[1792,128]{1,0:T(8,128)(2,1)S(1)}, bf16[8,128,128]{2,1,0:T(8,128)(2,1)S(1)}, bf16[16,144,1152]{2,1,...) custom-call(s32[4,8]{1,0:T(4,128)S(1)} %get-tuple-element.29.clips, ...), custom_call_target="tpu_custom_call" | custom-call | tf_op jit(solution)/shard_map/pallas_call | solution.py:366
  61.2 2.1 %collective-permute-start.31 = (bf16[32,2304]{1,0:T(8,128)(2,1)S(1)}, bf16[32,2304]{1,0:T(8,128)(2,1)S(1)}, u32[]{:S(2)}, u32[]{:S(2)}) collective-permute-start(bf16[32,2304]{1,0:T(8,128)(2,1)S(1)} %get-tuple-element.36), channel_id=1, source_target_pairs={{0,2},{1,3},{2,0},{3,1},{4,6},{5,7},{6,4},{7,5},{8,10},{9,11},{10,... | collective-permute-start | bytes 442376 | tf_op jit(solution)/shard_map/ppermute | solution.py:556
  64.9 2.6 %collective-permute-done.31.refs_1_ = bf16[32,2304]{1,0:T(8,128)(2,1)S(1)} collective-permute-done((bf16[32,2304]{1,0:T(8,128)(2,1)S(1)}, bf16[32,2304]{1,0:T(8,128)(2,1)S(1)}, u32[]{:S(2)}, u32[]{:S(2)}) %collective-permute-start.31) | collective-permute-done | bytes 147488 | tf_op jit(solution)/shard_map/ppermute | solution.py:556
  67.5 2.6 %collective-permute-done.32.refs_2_ = bf16[32,2304]{1,0:T(8,128)(2,1)S(1)} collective-permute-done((bf16[32,2304]{1,0:T(8,128)(2,1)S(1)}, bf16[32,2304]{1,0:T(8,128)(2,1)S(1)}, u32[]{:S(2)}, u32[]{:S(2)}) %collective-permute-start.32) | collective-permute-done | bytes 147488 | tf_op jit(solution)/shard_map/ppermute | solution.py:556
  70.1 1.8 %collective-permute-done.33.refs_3_ = bf16[32,2304]{1,0:T(8,128)(2,1)S(1)} collective-permute-done((bf16[32,2304]{1,0:T(8,128)(2,1)S(1)}, bf16[32,2304]{1,0:T(8,128)(2,1)S(1)}, u32[]{:S(2)}, u32[]{:S(2)}) %collective-permute-start.33) | collective-permute-done | bytes 147488 | tf_op jit(solution)/shard_map/ppermute | solution.py:556
  71.9 2.2 %shard_map.148 = (bf16[64,2304]{1,0:T(8,128)(2,1)S(1)}, bf16[64,2304]{1,0:T(8,128)(2,1)S(1)}) custom-call(s32[4,8]{1,0:T(4,128)S(1)} %get-tuple-element.29.clips, bf16[32,2304]{1,0:T(8,128)(2,1)S(1)} %get-tuple-element.35.refs_0_, bf16[32,2304]{1,0:T(8,128)(2,1)S(1)} %collective-permute-done.31.refs_1_, ...), custom_call_target="tpu_custom_call" | custom-call | tf_op jit(solution)/shard_map/pallas_call | solution.py:366
  75.8 1.7 %collective-permute-start.35 = (bf16[32,2304]{1,0:T(8,128)(2,1)S(1)}, bf16[32,2304]{1,0:T(8,128)(2,1)S(1)}, u32[]{:S(2)}, u32[]{:S(2)}) collective-permute-start(bf16[32,2304]{1,0:T(8,128)(2,1)S(1)} %get-tuple-element.42), channel_id=1, source_target_pairs={{0,2},{1,3},{2,0},{3,1},{4,6},{5,7},{6,4},{7,5},{8,10},{9,11},{10,... | collective-permute-start | bytes 442376 | tf_op jit(solution)/shard_map/ppermute | solution.py:556
  79.3 2.4 %collective-permute-done.35.refs_1_ = bf16[32,2304]{1,0:T(8,128)(2,1)S(1)} collective-permute-done((bf16[32,2304]{1,0:T(8,128)(2,1)S(1)}, bf16[32,2304]{1,0:T(8,128)(2,1)S(1)}, u32[]{:S(2)}, u32[]{:S(2)}) %collective-permute-start.35) | collective-permute-done | bytes 147488 | tf_op jit(solution)/shard_map/ppermute | solution.py:556
  81.7 2.5 %collective-permute-done.36.refs_2_ = bf16[32,2304]{1,0:T(8,128)(2,1)S(1)} collective-permute-done((bf16[32,2304]{1,0:T(8,128)(2,1)S(1)}, bf16[32,2304]{1,0:T(8,128)(2,1)S(1)}, u32[]{:S(2)}, u32[]{:S(2)}) %collective-permute-start.36) | collective-permute-done | bytes 147488 | tf_op jit(solution)/shard_map/ppermute | solution.py:556
  84.2 1.8 %collective-permute-done.37.refs_3_ = bf16[32,2304]{1,0:T(8,128)(2,1)S(1)} collective-permute-done((bf16[32,2304]{1,0:T(8,128)(2,1)S(1)}, bf16[32,2304]{1,0:T(8,128)(2,1)S(1)}, u32[]{:S(2)}, u32[]{:S(2)}) %collective-permute-start.37) | collective-permute-done | bytes 147488 | tf_op jit(solution)/shard_map/ppermute | solution.py:556
  86.1 4.9 %shard_map.150 = (bf16[128,1152]{1,0:T(8,128)(2,1)S(1)}, bf16[128,1152]{1,0:T(8,128)(2,1)S(1)}, bf16[32,2,1152]{2,1,0:T(2,128)(2,1)}) custom-call(s32[4,8]{1,0:T(4,128)S(1)} %get-tuple-element.29.clips, bf16[32,2304]{1,0:T(8,128)(2,1)S(1)} %get-tuple-element.41.refs_0_, bf16[32,2304]{1,0:T(8,128)(2,1)S(1)} %collective-permute-done.35.refs_1_, ...), custom_call_target="tpu_custom_call" | custom-call | tf_op jit(solution)/shard_map/pallas_call | solution.py:366
  91.0 4.6 %all-to-all-start = ((bf16[32,2,1152]{2,1,0:T(2,128)(2,1)}), bf16[32,2,1152]{2,1,0:T(2,128)(2,1)S(1)}, u32[]{:S(2)}, u32[]{:S(2)}) async-start(bf16[32,2,1152]{2,1,0:T(2,128)(2,1)} %get-tuple-element.54), calls=%async_computation | async-start | bytes 294912 | tf_op jit(solution)/shard_map/all_to_all | solution.py:591
  95.6 2.5 %copy-done.1 = bf16[16,144,1152]{2,1,0:T(8,128)(2,1)S(1)} copy-done((bf16[16,144,1152]{2,1,0:T(8,128)(2,1)S(1)}, bf16[16,144,1152]{2,1,0:T(8,128)(2,1)}, u32[]{:S(2)}) %copy-start.1) | copy-done | bytes 5308440
  98.1 1.9 %shard_map.151 = (bf16[128,1152]{1,0:T(8,128)(2,1)}, bf16[128,1152]{1,0:T(8,128)(2,1)}) custom-call(bf16[32,2304]{1,0:T(8,128)(2,1)S(1)} %get-tuple-element.41.refs_0_, bf16[32,2304]{1,0:T(8,128)(2,1)S(1)} %collective-permute-done.35.refs_1_, bf16[32,2304]{1,0:T(8,128)(2,1)S(1)} %collective-permute-done.36.refs_2_, ...), custom_call_target="tpu_custom_call" | custom-call | tf_op jit(solution)/shard_map/pallas_call | solution.py:366
  100.0 4.0 %all-to-all-done = bf16[32,2,1152]{2,1,0:T(2,128)(2,1)S(1)} async-done(((bf16[32,2,1152]{2,1,0:T(2,128)(2,1)}), bf16[32,2,1152]{2,1,0:T(2,128)(2,1)S(1)}, u32[]{:S(2)}, u32[]{:S(2)}) %all-to-all-start) | async-done | bytes 147488 | tf_op jit(solution)/shard_map/all_to_all | solution.py:591
  (82 shorter events, 21.7 us)
Async XLA Ops:
  2.6 7.7 %collective-permute-start.2 = (bf16[144,1152]{1,0:T(8,128)(2,1)S(1)}, bf16[144,1152]{1,0:T(8,128)(2,1)S(1)}, u32[]{:S(2)}, u32[]{:S(2)}) collective-permute-start(bf16[144,1152]{1,0:T(8,128)(2,1)S(1)} %get-tuple-element.56.refs_0_), channel_id=1, source_target_pairs={{0,4},{1,3},{4,8},{5,1},{8,12},{9,5},{12,14},{13,9},{14,10},{15,13... | collective-permute-start | bytes 995336 | tf_op jit(solution)/shard_map/ppermute | solution.py:393
  5.2 8.6 %collective-permute-start.1 = (bf16[144,1152]{1,0:T(8,128)(2,1)S(1)}, bf16[144,1152]{1,0:T(8,128)(2,1)S(1)}, u32[]{:S(2)}, u32[]{:S(2)}) collective-permute-start(bf16[144,1152]{1,0:T(8,128)(2,1)S(1)} %collective-permute-done.refs_1_), channel_id=1, source_target_pairs={{0,4},{1,3},{4,8},{5,1},{8,12},{9,5},{12,14},{13,9},{14,10},{15,13... | collective-permute-start | bytes 995336 | tf_op jit(solution)/shard_map/ppermute | solution.py:393
  6.8 7.0 %collective-permute-start.7 = (bf16[144,1152]{1,0:T(8,128)(2,1)S(1)}, bf16[144,1152]{1,0:T(8,128)(2,1)S(1)}, u32[]{:S(2)}, u32[]{:S(2)}) collective-permute-start(bf16[144,1152]{1,0:T(8,128)(2,1)S(1)} %get-tuple-element.55.refs_16_), channel_id=1, source_target_pairs={{0,1},{1,0},{2,3},{3,2},{4,5},{5,4},{6,7},{7,6},{8,9},{9,8},{10,11... | collective-permute-start | bytes 995336 | tf_op jit(solution)/shard_map/ppermute | solution.py:399
  10.3 5.7 %collective-permute-start.6 = (bf16[144,1152]{1,0:T(8,128)(2,1)S(1)}, bf16[144,1152]{1,0:T(8,128)(2,1)S(1)}, u32[]{:S(2)}, u32[]{:S(2)}) collective-permute-start(bf16[144,1152]{1,0:T(8,128)(2,1)S(1)} %collective-permute-done.2.refs_1_.refs_2_), channel_id=1, source_target_pairs={{0,1},{1,0},{2,3},{3,2},{4,5},{5,4},{6,7},{7,6},{8,9},{9,8},{10,11... | collective-permute-start | bytes 995336 | tf_op jit(solution)/shard_map/ppermute | solution.py:399
  10.3 7.1 %collective-permute-start.5 = (bf16[144,1152]{1,0:T(8,128)(2,1)S(1)}, bf16[144,1152]{1,0:T(8,128)(2,1)S(1)}, u32[]{:S(2)}, u32[]{:S(2)}) collective-permute-start(bf16[144,1152]{1,0:T(8,128)(2,1)S(1)} %collective-permute-done.2.refs_1_.refs_2_), channel_id=1, source_target_pairs={{0,4},{1,3},{4,8},{5,1},{8,12},{9,5},{12,14},{13,9},{14,10},{15,13... | collective-permute-start | bytes 995336 | tf_op jit(solution)/shard_map/ppermute | solution.py:393
  12.4 10.1 %collective-permute-start.10 = (bf16[144,1152]{1,0:T(8,128)(2,1)S(1)}, bf16[144,1152]{1,0:T(8,128)(2,1)S(1)}, u32[]{:S(2)}, u32[]{:S(2)}) collective-permute-start(bf16[144,1152]{1,0:T(8,128)(2,1)S(1)} %collective-permute-done.2.refs_1_.refs_2_), channel_id=1, source_target_pairs={{0,16},{16,0},{1,17},{17,1},{2,18},{18,2},{3,19},{19,3},{4,20},{20... | collective-permute-start | bytes 995336 | tf_op jit(solution)/shard_map/ppermute | solution.py:396
  13.8 8.6 %collective-permute-start.8 = (bf16[144,1152]{1,0:T(8,128)(2,1)S(1)}, bf16[144,1152]{1,0:T(8,128)(2,1)S(1)}, u32[]{:S(2)}, u32[]{:S(2)}) collective-permute-start(bf16[144,1152]{1,0:T(8,128)(2,1)S(1)} %shard_map.139.refs_1_.refs_6_), channel_id=1, source_target_pairs={{0,1},{1,0},{2,3},{3,2},{4,5},{5,4},{6,7},{7,6},{8,9},{9,8},{10,11... | collective-permute-start | bytes 995336 | tf_op jit(solution)/shard_map/ppermute | solution.py:399
  13.9 8.6 %collective-permute-start.4 = (bf16[144,1152]{1,0:T(8,128)(2,1)S(1)}, bf16[144,1152]{1,0:T(8,128)(2,1)S(1)}, u32[]{:S(2)}, u32[]{:S(2)}) collective-permute-start(bf16[144,1152]{1,0:T(8,128)(2,1)S(1)} %shard_map.139.refs_1_.refs_6_), channel_id=1, source_target_pairs={{0,4},{1,3},{4,8},{5,1},{8,12},{9,5},{12,14},{13,9},{14,10},{15,13... | collective-permute-start | bytes 995336 | tf_op jit(solution)/shard_map/ppermute | solution.py:393
  17.4 7.2 %collective-permute-start.13 = (bf16[144,1152]{1,0:T(8,128)(2,1)S(1)}, bf16[144,1152]{1,0:T(8,128)(2,1)S(1)}, u32[]{:S(2)}, u32[]{:S(2)}) collective-permute-start(bf16[144,1152]{1,0:T(8,128)(2,1)S(1)} %shard_map.140.refs_1_.refs_3_), channel_id=1, source_target_pairs={{0,4},{1,3},{4,8},{5,1},{8,12},{9,5},{12,14},{13,9},{14,10},{15,13... | collective-permute-start | bytes 995336 | tf_op jit(solution)/shard_map/ppermute | solution.py:393
  20.9 9.1 %collective-permute-start.3 = (bf16[144,1152]{1,0:T(8,128)(2,1)S(1)}, bf16[144,1152]{1,0:T(8,128)(2,1)S(1)}, u32[]{:S(2)}, u32[]{:S(2)}) collective-permute-start(bf16[144,1152]{1,0:T(8,128)(2,1)S(1)} %shard_map.139.refs_1_.refs_6_), channel_id=1, source_target_pairs={{0,16},{16,0},{1,17},{17,1},{2,18},{18,2},{3,19},{19,3},{4,20},{20... | collective-permute-start | bytes 995336 | tf_op jit(solution)/shard_map/ppermute | solution.py:396
  22.5 9.0 %collective-permute-start.12 = (bf16[144,1152]{1,0:T(8,128)(2,1)S(1)}, bf16[144,1152]{1,0:T(8,128)(2,1)S(1)}, u32[]{:S(2)}, u32[]{:S(2)}) collective-permute-start(bf16[144,1152]{1,0:T(8,128)(2,1)S(1)} %shard_map.141.refs_1_.refs_7_), channel_id=1, source_target_pairs={{0,1},{1,0},{2,3},{3,2},{4,5},{5,4},{6,7},{7,6},{8,9},{9,8},{10,11... | collective-permute-start | bytes 995336 | tf_op jit(solution)/shard_map/ppermute | solution.py:399
  23.0 8.5 %collective-permute-start.9 = (bf16[144,1152]{1,0:T(8,128)(2,1)S(1)}, bf16[144,1152]{1,0:T(8,128)(2,1)S(1)}, u32[]{:S(2)}, u32[]{:S(2)}) collective-permute-start(bf16[144,1152]{1,0:T(8,128)(2,1)S(1)} %shard_map.141.refs_1_.refs_7_), channel_id=1, source_target_pairs={{0,4},{1,3},{4,8},{5,1},{8,12},{9,5},{12,14},{13,9},{14,10},{15,13... | collective-permute-start | bytes 995336 | tf_op jit(solution)/shard_map/ppermute | solution.py:393
  24.6 9.1 %collective-permute-start.14 = (bf16[144,1152]{1,0:T(8,128)(2,1)S(1)}, bf16[144,1152]{1,0:T(8,128)(2,1)S(1)}, u32[]{:S(2)}, u32[]{:S(2)}) collective-permute-start(bf16[144,1152]{1,0:T(8,128)(2,1)S(1)} %shard_map.143.refs_4_), channel_id=1, source_target_pairs={{0,4},{1,3},{4,8},{5,1},{8,12},{9,5},{12,14},{13,9},{14,10},{15,13... | collective-permute-start | bytes 995336 | tf_op jit(solution)/shard_map/ppermute | solution.py:393
  26.8 10.4 %collective-permute-start.19 = (bf16[144,1152]{1,0:T(8,128)(2,1)S(1)}, bf16[144,1152]{1,0:T(8,128)(2,1)S(1)}, u32[]{:S(2)}, u32[]{:S(2)}) collective-permute-start(bf16[144,1152]{1,0:T(8,128)(2,1)S(1)} %collective-permute-done.10.refs_2_.refs_18_), channel_id=1, source_target_pairs={{0,4},{1,3},{4,8},{5,1},{8,12},{9,5},{12,14},{13,9},{14,10},{15,13... | collective-permute-start | bytes 995336 | tf_op jit(solution)/shard_map/ppermute | solution.py:393
  30.0 8.1 %collective-permute-start.20 = (bf16[144,1152]{1,0:T(8,128)(2,1)S(1)}, bf16[144,1152]{1,0:T(8,128)(2,1)S(1)}, u32[]{:S(2)}, u32[]{:S(2)}) collective-permute-start(bf16[144,1152]{1,0:T(8,128)(2,1)S(1)} %shard_map.143.refs_4_), channel_id=1, source_target_pairs={{0,16},{16,0},{1,17},{17,1},{2,18},{18,2},{3,19},{19,3},{4,20},{20... | collective-permute-start | bytes 995336 | tf_op jit(solution)/shard_map/ppermute | solution.py:396
  31.5 6.6 %collective-permute-start.18 = (bf16[144,1152]{1,0:T(8,128)(2,1)S(1)}, bf16[144,1152]{1,0:T(8,128)(2,1)S(1)}, u32[]{:S(2)}, u32[]{:S(2)}) collective-permute-start(bf16[144,1152]{1,0:T(8,128)(2,1)S(1)} %collective-permute-done.9.refs_4_.refs_2_.refs_8_), channel_id=1, source_target_pairs={{0,1},{1,0},{2,3},{3,2},{4,5},{5,4},{6,7},{7,6},{8,9},{9,8},{10,11... | collective-permute-start | bytes 995336 | tf_op jit(solution)/shard_map/ppermute | solution.py:399
  33.6 4.9 %collective-permute-start.17 = (bf16[144,1152]{1,0:T(8,128)(2,1)S(1)}, bf16[144,1152]{1,0:T(8,128)(2,1)S(1)}, u32[]{:S(2)}, u32[]{:S(2)}) collective-permute-start(bf16[144,1152]{1,0:T(8,128)(2,1)S(1)} %shard_map.144.refs_5_), channel_id=1, source_target_pairs={{0,1},{1,0},{2,3},{3,2},{4,5},{5,4},{6,7},{7,6},{8,9},{9,8},{10,11... | collective-permute-start | bytes 995336 | tf_op jit(solution)/shard_map/ppermute | solution.py:399
  33.6 7.1 %collective-permute-start.22 = (bf16[144,1152]{1,0:T(8,128)(2,1)S(1)}, bf16[144,1152]{1,0:T(8,128)(2,1)S(1)}, u32[]{:S(2)}, u32[]{:S(2)}) collective-permute-start(bf16[144,1152]{1,0:T(8,128)(2,1)S(1)} %get-tuple-element.32.refs_1_.refs_22_), channel_id=1, source_target_pairs={{0,4},{1,3},{4,8},{5,1},{8,12},{9,5},{12,14},{13,9},{14,10},{15,13... | collective-permute-start | bytes 995336 | tf_op jit(solution)/shard_map/ppermute | solution.py:393
  37.2 5.1 %collective-permute-start.15 = (bf16[144,1152]{1,0:T(8,128)(2,1)S(1)}, bf16[144,1152]{1,0:T(8,128)(2,1)S(1)}, u32[]{:S(2)}, u32[]{:S(2)}) collective-permute-start(bf16[144,1152]{1,0:T(8,128)(2,1)S(1)} %shard_map.140.refs_1_.refs_3_), channel_id=1, source_target_pairs={{0,1},{1,0},{2,3},{3,2},{4,5},{5,4},{6,7},{7,6},{8,9},{9,8},{10,11... | collective-permute-start | bytes 995336 | tf_op jit(solution)/shard_map/ppermute | solution.py:399
  38.1 4.8 %collective-permute-start.16 = (bf16[144,1152]{1,0:T(8,128)(2,1)S(1)}, bf16[144,1152]{1,0:T(8,128)(2,1)S(1)}, u32[]{:S(2)}, u32[]{:S(2)}) collective-permute-start(bf16[144,1152]{1,0:T(8,128)(2,1)S(1)} %shard_map.143.refs_4_), channel_id=1, source_target_pairs={{0,1},{1,0},{2,3},{3,2},{4,5},{5,4},{6,7},{7,6},{8,9},{9,8},{10,11... | collective-permute-start | bytes 995336 | tf_op jit(solution)/shard_map/ppermute | solution.py:399
  38.6 8.4 %collective-permute-start.21 = (bf16[144,1152]{1,0:T(8,128)(2,1)S(1)}, bf16[144,1152]{1,0:T(8,128)(2,1)S(1)}, u32[]{:S(2)}, u32[]{:S(2)}) collective-permute-start(bf16[144,1152]{1,0:T(8,128)(2,1)S(1)} %collective-permute-done.20.refs_3_.refs_20_), channel_id=1, source_target_pairs={{0,4},{1,3},{4,8},{5,1},{8,12},{9,5},{12,14},{13,9},{14,10},{15,13... | collective-permute-start | bytes 995336 | tf_op jit(solution)/shard_map/ppermute | solution.py:393
  40.8 9.7 %collective-permute-start.23 = (bf16[144,1152]{1,0:T(8,128)(2,1)S(1)}, bf16[144,1152]{1,0:T(8,128)(2,1)S(1)}, u32[]{:S(2)}, u32[]{:S(2)}) collective-permute-start(bf16[144,1152]{1,0:T(8,128)(2,1)S(1)} %shard_map.145.refs_23_), channel_id=1, source_target_pairs={{0,4},{1,3},{4,8},{5,1},{8,12},{9,5},{12,14},{13,9},{14,10},{15,13... | collective-permute-start | bytes 995336 | tf_op jit(solution)/shard_map/ppermute | solution.py:393
  42.3 8.2 %collective-permute-start.27 = (bf16[144,1152]{1,0:T(8,128)(2,1)S(1)}, bf16[144,1152]{1,0:T(8,128)(2,1)S(1)}, u32[]{:S(2)}, u32[]{:S(2)}) collective-permute-start(bf16[144,1152]{1,0:T(8,128)(2,1)S(1)} %get-tuple-element.32.refs_1_.refs_22_), channel_id=1, source_target_pairs={{0,1},{1,0},{2,3},{3,2},{4,5},{5,4},{6,7},{7,6},{8,9},{9,8},{10,11... | collective-permute-start | bytes 995336 | tf_op jit(solution)/shard_map/ppermute | solution.py:399
  42.6 7.9 %collective-permute-start.25 = (bf16[144,1152]{1,0:T(8,128)(2,1)S(1)}, bf16[144,1152]{1,0:T(8,128)(2,1)S(1)}, u32[]{:S(2)}, u32[]{:S(2)}) collective-permute-start(bf16[144,1152]{1,0:T(8,128)(2,1)S(1)} %collective-permute-done.20.refs_3_.refs_20_), channel_id=1, source_target_pairs={{0,1},{1,0},{2,3},{3,2},{4,5},{5,4},{6,7},{7,6},{8,9},{9,8},{10,11... | collective-permute-start | bytes 995336 | tf_op jit(solution)/shard_map/ppermute | solution.py:399
  42.9 7.7 %collective-permute-start.28 = (bf16[144,1152]{1,0:T(8,128)(2,1)S(1)}, bf16[144,1152]{1,0:T(8,128)(2,1)S(1)}, u32[]{:S(2)}, u32[]{:S(2)}) collective-permute-start(bf16[144,1152]{1,0:T(8,128)(2,1)S(1)} %shard_map.145.refs_23_), channel_id=1, source_target_pairs={{0,1},{1,0},{2,3},{3,2},{4,5},{5,4},{6,7},{7,6},{8,9},{9,8},{10,11... | collective-permute-start | bytes 995336 | tf_op jit(solution)/shard_map/ppermute | solution.py:399
  61.2 6.2 %collective-permute-start.31 = (bf16[32,2304]{1,0:T(8,128)(2,1)S(1)}, bf16[32,2304]{1,0:T(8,128)(2,1)S(1)}, u32[]{:S(2)}, u32[]{:S(2)}) collective-permute-start(bf16[32,2304]{1,0:T(8,128)(2,1)S(1)} %get-tuple-element.36), channel_id=1, source_target_pairs={{0,2},{1,3},{2,0},{3,1},{4,6},{5,7},{6,4},{7,5},{8,10},{9,11},{10,... | collective-permute-start | bytes 442376 | tf_op jit(solution)/shard_map/ppermute | solution.py:556
  63.3 6.7 %collective-permute-start.32 = (bf16[32,2304]{1,0:T(8,128)(2,1)S(1)}, bf16[32,2304]{1,0:T(8,128)(2,1)S(1)}, u32[]{:S(2)}, u32[]{:S(2)}) collective-permute-start(bf16[32,2304]{1,0:T(8,128)(2,1)S(1)} %get-tuple-element.37), channel_id=1, source_target_pairs={{0,4},{1,5},{2,6},{3,7},{4,0},{5,1},{6,2},{7,3},{8,12},{9,13},{10,... | collective-permute-start | bytes 442376 | tf_op jit(solution)/shard_map/ppermute | solution.py:556
  64.5 7.4 %collective-permute-start.33 = (bf16[32,2304]{1,0:T(8,128)(2,1)S(1)}, bf16[32,2304]{1,0:T(8,128)(2,1)S(1)}, u32[]{:S(2)}, u32[]{:S(2)}) collective-permute-start(bf16[32,2304]{1,0:T(8,128)(2,1)S(1)} %get-tuple-element.38), channel_id=1, source_target_pairs={{0,6},{1,7},{2,4},{3,5},{4,2},{5,3},{6,0},{7,1},{8,14},{9,15},{10,... | collective-permute-start | bytes 442376 | tf_op jit(solution)/shard_map/ppermute | solution.py:556
  75.8 6.0 %collective-permute-start.35 = (bf16[32,2304]{1,0:T(8,128)(2,1)S(1)}, bf16[32,2304]{1,0:T(8,128)(2,1)S(1)}, u32[]{:S(2)}, u32[]{:S(2)}) collective-permute-start(bf16[32,2304]{1,0:T(8,128)(2,1)S(1)} %get-tuple-element.42), channel_id=1, source_target_pairs={{0,2},{1,3},{2,0},{3,1},{4,6},{5,7},{6,4},{7,5},{8,10},{9,11},{10,... | collective-permute-start | bytes 442376 | tf_op jit(solution)/shard_map/ppermute | solution.py:556
  77.5 6.7 %collective-permute-start.36 = (bf16[32,2304]{1,0:T(8,128)(2,1)S(1)}, bf16[32,2304]{1,0:T(8,128)(2,1)S(1)}, u32[]{:S(2)}, u32[]{:S(2)}) collective-permute-start(bf16[32,2304]{1,0:T(8,128)(2,1)S(1)} %get-tuple-element.43), channel_id=1, source_target_pairs={{0,4},{1,5},{2,6},{3,7},{4,0},{5,1},{6,2},{7,3},{8,12},{9,13},{10,... | collective-permute-start | bytes 442376 | tf_op jit(solution)/shard_map/ppermute | solution.py:556
  78.7 7.4 %collective-permute-start.37 = (bf16[32,2304]{1,0:T(8,128)(2,1)S(1)}, bf16[32,2304]{1,0:T(8,128)(2,1)S(1)}, u32[]{:S(2)}, u32[]{:S(2)}) collective-permute-start(bf16[32,2304]{1,0:T(8,128)(2,1)S(1)} %get-tuple-element.44), channel_id=1, source_target_pairs={{0,6},{1,7},{2,4},{3,5},{4,2},{5,3},{6,0},{7,1},{8,14},{9,15},{10,... | collective-permute-start | bytes 442376 | tf_op jit(solution)/shard_map/ppermute | solution.py:556
  91.0 13.0 %all-to-all-start = ((bf16[32,2,1152]{2,1,0:T(2,128)(2,1)}), bf16[32,2,1152]{2,1,0:T(2,128)(2,1)S(1)}, u32[]{:S(2)}, u32[]{:S(2)}) async-start(bf16[32,2,1152]{2,1,0:T(2,128)(2,1)} %get-tuple-element.54), calls=%async_computation | async-start | bytes 294912 | tf_op jit(solution)/shard_map/all_to_all | solution.py:591
  (15 other events, 210.4 us)

commit v3 on v2

--- a/solution.py
+++ b/solution.py
@@ -403,7 +403,6 @@
     t0 = twin(own)
     o1 = ring(own)
     t1 = ring(t0)
-    t1 = gate(t1, o1)
     t0_other = twin(own_other)
     o2 = ring(o1)
     x_o1 = across(o1)
@@ -424,19 +423,19 @@
     o4 = gate(o4, x_t1, t3)
     x_o3 = across(o3)
     o3_twin = twin(o3)
+    x_o2 = ring(x_o1)
     t3_twin = twin(t3)
     x_t1_twin = twin(x_t1)
     x_t2 = ring(x_t1)
-    x_o4 = ring(x_o3)
-    x_o4_twin = twin(x_o4)
+    x_o4 = across(o4)
     o4_twin = twin(o4)
-    x_o3_twin = twin(x_o3)
-    x_o2 = ring(x_o1)
     x_t2 = gate(x_t2, o4_twin, t3_twin, x_o3, x_o2)
     x_t3 = ring(x_t2)
     x_o2_twin = twin(x_o2)
     x_t2_twin = twin(x_t2)
+    x_o3_twin = twin(x_o3)
     x_t3_twin = twin(x_t3)
+    x_o4_twin = twin(x_o4)
     mine = {"o0": (own, 0), "t0": (t0, 0)}
     other = {"o0": (own_other, 0), "t0": (t0_other, 0)}
     mine |= {"o1": (o1, 0), "o1_twin": (o1_twin, 0)}

time: 105 us -> 105 us (level)
  waiting for transfers between devices: 42.7 us -> 40.1 us
  starting transfers between devices: 38.6 us -> 40.8 us
    ppermute x11 -> x10, waiting for transfers between devices: 17.9 us -> 9.79 us  [ring(): return lax.ppermute(rows, 'ctx', ring_pairs)]
    ppermute x3 -> x4, waiting for transfers between devices: 2.45 us -> 7.9 us  [across(): lax.ppermute(rows, 'dp', [(index, index ^ 1) for index in range(planes)])]
    ppermute x3 -> x4, starting transfers between devices: 4.54 us -> 6.03 us  [across(): lax.ppermute(rows, 'dp', [(index, index ^ 1) for index in range(planes)])]
    ppermute x6, starting transfers between devices: 7.18 us -> 8.43 us  [exchange(): lax.ppermute(rows_away, 'ctx', [(index, index ^ 2 * distance) for index i...]
    ppermute x11 -> x10, starting transfers between devices: 19.7 us -> 18.8 us  [ring(): return lax.ppermute(rows, 'ctx', ring_pairs)]
where the time goes in v3:
time: 105 us; the launch traced here: 104 us
  starting transfers between devices  40.8 us (39%)
  waiting for transfers between devices  40.1 us (38%)
  Pallas kernels  16.5 us (16%)
  local copies, waits for them, and re-layouts  3.93 us (4%)
  other arithmetic  2.2 us (2%)
    ppermute x10, starting transfers between devices, ring(): return lax.ppermute(rows, 'ctx', ring_pairs)  18.8 us
    pallas_call x6, Pallas kernels, call(): pl.pallas_call(body, out_shape=out_shapes, in_specs=[scalars] * len(clips...  16.5 us
    ppermute x6, waiting for transfers between devices, exchange(): lax.ppermute(rows_away, 'ctx', [(index, index ^ 2 * distance) for index i...  13.8 us
    ppermute x10, waiting for transfers between devices, ring(): return lax.ppermute(rows, 'ctx', ring_pairs)  9.79 us
    ppermute x6, starting transfers between devices, exchange(): lax.ppermute(rows_away, 'ctx', [(index, index ^ 2 * distance) for index i...  8.43 us
    ppermute x4, waiting for transfers between devices, across(): lax.ppermute(rows, 'dp', [(index, index ^ 1) for index in range(planes)])  7.9 us
    ppermute x4, starting transfers between devices, across(): lax.ppermute(rows, 'dp', [(index, index ^ 1) for index in range(planes)])  6.03 us
    all_to_all x1, starting transfers between devices, shards(): lax.all_to_all(gains, ('dp', 'ctx'), split_axis=0, concat_axis=0, tiled=T...  4.61 us
  transfers between devices with their start and end apart: 39, of which 19 were waited for; matrix products, arithmetic and copies ran while one was open for 1% of the time, Pallas kernels for 2%

profile of v3, /device:TPU:0, one launch (start us, length us, event | category | flops | bytes accessed | tf_op | source)
XLA Modules:
  0.0 104.3 jit_solution(11985383564740807090)
XLA Ops:
  2.6 2.6 %collective-permute-start.4 = (bf16[144,1152]{1,0:T(8,128)(2,1)S(1)}, bf16[144,1152]{1,0:T(8,128)(2,1)S(1)}, u32[]{:S(2)}, u32[]{:S(2)}) collective-permute-start(bf16[144,1152]{1,0:T(8,128)(2,1)S(1)} %get-tuple-element.56.refs_0_), channel_id=1, source_target_pairs={{0,4},{1,3},{4,8},{5,1},{8,12},{9,5},{12,14},{13,9},{14,10},{15,13... | collective-permute-start | bytes 995336 | tf_op jit(solution)/shard_map/ppermute | solution.py:393
  5.2 1.6 %collective-permute-start.1 = (bf16[144,1152]{1,0:T(8,128)(2,1)S(1)}, bf16[144,1152]{1,0:T(8,128)(2,1)S(1)}, u32[]{:S(2)}, u32[]{:S(2)}) collective-permute-start(bf16[144,1152]{1,0:T(8,128)(2,1)S(1)} %collective-permute-done.refs_1_), channel_id=1, source_target_pairs={{0,4},{1,3},{4,8},{5,1},{8,12},{9,5},{12,14},{13,9},{14,10},{15,13... | collective-permute-start | bytes 995336 | tf_op jit(solution)/shard_map/ppermute | solution.py:393
  6.8 3.5 %collective-permute-done.4.refs_2_ = bf16[144,1152]{1,0:T(8,128)(2,1)S(1)} collective-permute-done((bf16[144,1152]{1,0:T(8,128)(2,1)S(1)}, bf16[144,1152]{1,0:T(8,128)(2,1)S(1)}, u32[]{:S(2)}, u32[]{:S(2)}) %collective-permute-start.4) | collective-permute-done | bytes 331808 | tf_op jit(solution)/shard_map/ppermute | solution.py:393
  10.3 2.1 %collective-permute-start.5 = (bf16[144,1152]{1,0:T(8,128)(2,1)S(1)}, bf16[144,1152]{1,0:T(8,128)(2,1)S(1)}, u32[]{:S(2)}, u32[]{:S(2)}) collective-permute-start(bf16[144,1152]{1,0:T(8,128)(2,1)S(1)} %collective-permute-done.4.refs_2_), channel_id=1, source_target_pairs={{0,4},{1,3},{4,8},{5,1},{8,12},{9,5},{12,14},{13,9},{14,10},{15,13... | collective-permute-start | bytes 995336 | tf_op jit(solution)/shard_map/ppermute | solution.py:393
  13.9 2.1 %collective-permute-start.3 = (bf16[144,1152]{1,0:T(8,128)(2,1)S(1)}, bf16[144,1152]{1,0:T(8,128)(2,1)S(1)}, u32[]{:S(2)}, u32[]{:S(2)}) collective-permute-start(bf16[144,1152]{1,0:T(8,128)(2,1)S(1)} %collective-permute-done.1.refs_1_.refs_6_), channel_id=1, source_target_pairs={{0,4},{1,3},{4,8},{5,1},{8,12},{9,5},{12,14},{13,9},{14,10},{15,13... | collective-permute-start | bytes 995336 | tf_op jit(solution)/shard_map/ppermute | solution.py:393
  17.4 2.1 %collective-permute-start.13 = (bf16[144,1152]{1,0:T(8,128)(2,1)S(1)}, bf16[144,1152]{1,0:T(8,128)(2,1)S(1)}, u32[]{:S(2)}, u32[]{:S(2)}) collective-permute-start(bf16[144,1152]{1,0:T(8,128)(2,1)S(1)} %shard_map.139.refs_1_.refs_3_), channel_id=1, source_target_pairs={{0,4},{1,3},{4,8},{5,1},{8,12},{9,5},{12,14},{13,9},{14,10},{15,13... | collective-permute-start | bytes 995336 | tf_op jit(solution)/shard_map/ppermute | solution.py:393
  20.9 1.6 %collective-permute-start.2 = (bf16[144,1152]{1,0:T(8,128)(2,1)S(1)}, bf16[144,1152]{1,0:T(8,128)(2,1)S(1)}, u32[]{:S(2)}, u32[]{:S(2)}) collective-permute-start(bf16[144,1152]{1,0:T(8,128)(2,1)S(1)} %collective-permute-done.1.refs_1_.refs_6_), channel_id=1, source_target_pairs={{0,16},{16,0},{1,17},{17,1},{2,18},{18,2},{3,19},{19,3},{4,20},{20... | collective-permute-start | bytes 995336 | tf_op jit(solution)/shard_map/ppermute | solution.py:396
  23.0 1.6 %collective-permute-start.9 = (bf16[144,1152]{1,0:T(8,128)(2,1)S(1)}, bf16[144,1152]{1,0:T(8,128)(2,1)S(1)}, u32[]{:S(2)}, u32[]{:S(2)}) collective-permute-start(bf16[144,1152]{1,0:T(8,128)(2,1)S(1)} %shard_map.140.refs_1_.refs_7_), channel_id=1, source_target_pairs={{0,4},{1,3},{4,8},{5,1},{8,12},{9,5},{12,14},{13,9},{14,10},{15,13... | collective-permute-start | bytes 995336 | tf_op jit(solution)/shard_map/ppermute | solution.py:393
  24.6 2.0 %collective-permute-start.14 = (bf16[144,1152]{1,0:T(8,128)(2,1)S(1)}, bf16[144,1152]{1,0:T(8,128)(2,1)S(1)}, u32[]{:S(2)}, u32[]{:S(2)}) collective-permute-start(bf16[144,1152]{1,0:T(8,128)(2,1)S(1)} %shard_map.142.refs_4_), channel_id=1, source_target_pairs={{0,4},{1,3},{4,8},{5,1},{8,12},{9,5},{12,14},{13,9},{14,10},{15,13... | collective-permute-start | bytes 995336 | tf_op jit(solution)/shard_map/ppermute | solution.py:393
  26.7 1.6 %collective-permute-start.19 = (bf16[144,1152]{1,0:T(8,128)(2,1)S(1)}, bf16[144,1152]{1,0:T(8,128)(2,1)S(1)}, u32[]{:S(2)}, u32[]{:S(2)}) collective-permute-start(bf16[144,1152]{1,0:T(8,128)(2,1)S(1)} %collective-permute-done.10.refs_2_.refs_18_), channel_id=1, source_target_pairs={{0,4},{1,3},{4,8},{5,1},{8,12},{9,5},{12,14},{13,9},{14,10},{15,13... | collective-permute-start | bytes 995336 | tf_op jit(solution)/shard_map/ppermute | solution.py:393
  28.4 1.6 %collective-permute-done.2.refs_0_ = bf16[144,1152]{1,0:T(8,128)(2,1)S(1)} collective-permute-done((bf16[144,1152]{1,0:T(8,128)(2,1)S(1)}, bf16[144,1152]{1,0:T(8,128)(2,1)S(1)}, u32[]{:S(2)}, u32[]{:S(2)}) %collective-permute-start.2) | collective-permute-done | bytes 331808 | tf_op jit(solution)/shard_map/ppermute | solution.py:396
  31.5 2.2 %collective-permute-done.14.refs_0_ = bf16[144,1152]{1,0:T(8,128)(2,1)S(1)} collective-permute-done((bf16[144,1152]{1,0:T(8,128)(2,1)S(1)}, bf16[144,1152]{1,0:T(8,128)(2,1)S(1)}, u32[]{:S(2)}, u32[]{:S(2)}) %collective-permute-start.14) | collective-permute-done | bytes 331808 | tf_op jit(solution)/shard_map/ppermute | solution.py:393
  33.6 1.6 %collective-permute-start.22 = (bf16[144,1152]{1,0:T(8,128)(2,1)S(1)}, bf16[144,1152]{1,0:T(8,128)(2,1)S(1)}, u32[]{:S(2)}, u32[]{:S(2)}) collective-permute-start(bf16[144,1152]{1,0:T(8,128)(2,1)S(1)} %get-tuple-element.32.refs_1_.refs_22_), channel_id=1, source_target_pairs={{0,4},{1,3},{4,8},{5,1},{8,12},{9,5},{12,14},{13,9},{14,10},{15,13... | collective-permute-start | bytes 995336 | tf_op jit(solution)/shard_map/ppermute | solution.py:393
  35.2 2.0 %collective-permute-done.19.refs_4_.refs_19_ = bf16[144,1152]{1,0:T(8,128)(2,1)S(1)} collective-permute-done((bf16[144,1152]{1,0:T(8,128)(2,1)S(1)}, bf16[144,1152]{1,0:T(8,128)(2,1)S(1)}, u32[]{:S(2)}, u32[]{:S(2)}) %collective-permute-start.19) | collective-permute-done | bytes 331808 | tf_op jit(solution)/shard_map/ppermute | solution.py:393
  40.8 1.6 %collective-permute-start.23 = (bf16[144,1152]{1,0:T(8,128)(2,1)S(1)}, bf16[144,1152]{1,0:T(8,128)(2,1)S(1)}, u32[]{:S(2)}, u32[]{:S(2)}) collective-permute-start(bf16[144,1152]{1,0:T(8,128)(2,1)S(1)} %shard_map.144.refs_23_), channel_id=1, source_target_pairs={{0,4},{1,3},{4,8},{5,1},{8,12},{9,5},{12,14},{13,9},{14,10},{15,13... | collective-permute-start | bytes 995336 | tf_op jit(solution)/shard_map/ppermute | solution.py:393
  43.0 5.4 %collective-permute-done.21.refs_21_ = bf16[144,1152]{1,0:T(8,128)(2,1)S(1)} collective-permute-done((bf16[144,1152]{1,0:T(8,128)(2,1)S(1)}, bf16[144,1152]{1,0:T(8,128)(2,1)S(1)}, u32[]{:S(2)}, u32[]{:S(2)}) %collective-permute-start.21) | collective-permute-done | bytes 331808 | tf_op jit(solution)/shard_map/ppermute | solution.py:396
  50.5 7.4 %shard_map.145 = (bf16[128,1152]{1,0:T(8,128)(2,1)S(1)}, bf16[1792,128]{1,0:T(8,128)(2,1)S(1)}, bf16[8,128,128]{2,1,0:T(8,128)(2,1)S(1)}, bf16[16,144,1152]{2,1,...) custom-call(s32[4,8]{1,0:T(4,128)S(1)} %get-tuple-element.29.clips, ...), custom_call_target="tpu_custom_call" | custom-call | tf_op jit(solution)/shard_map/pallas_call | solution.py:366
  59.6 3.3 %collective-permute-start.31 = (bf16[32,2304]{1,0:T(8,128)(2,1)S(1)}, bf16[32,2304]{1,0:T(8,128)(2,1)S(1)}, u32[]{:S(2)}, u32[]{:S(2)}) collective-permute-start(bf16[32,2304]{1,0:T(8,128)(2,1)S(1)} %get-tuple-element.36), channel_id=1, source_target_pairs={{0,2},{1,3},{2,0},{3,1},{4,6},{5,7},{6,4},{7,5},{8,10},{9,11},{10,... | collective-permute-start | bytes 442376 | tf_op jit(solution)/shard_map/ppermute | solution.py:555
  64.4 2.6 %collective-permute-done.31.refs_1_ = bf16[32,2304]{1,0:T(8,128)(2,1)S(1)} collective-permute-done((bf16[32,2304]{1,0:T(8,128)(2,1)S(1)}, bf16[32,2304]{1,0:T(8,128)(2,1)S(1)}, u32[]{:S(2)}, u32[]{:S(2)}) %collective-permute-start.31) | collective-permute-done | bytes 147488 | tf_op jit(solution)/shard_map/ppermute | solution.py:555
  67.1 2.6 %collective-permute-done.32.refs_2_ = bf16[32,2304]{1,0:T(8,128)(2,1)S(1)} collective-permute-done((bf16[32,2304]{1,0:T(8,128)(2,1)S(1)}, bf16[32,2304]{1,0:T(8,128)(2,1)S(1)}, u32[]{:S(2)}, u32[]{:S(2)}) %collective-permute-start.32) | collective-permute-done | bytes 147488 | tf_op jit(solution)/shard_map/ppermute | solution.py:555
  69.6 1.8 %collective-permute-done.33.refs_3_ = bf16[32,2304]{1,0:T(8,128)(2,1)S(1)} collective-permute-done((bf16[32,2304]{1,0:T(8,128)(2,1)S(1)}, bf16[32,2304]{1,0:T(8,128)(2,1)S(1)}, u32[]{:S(2)}, u32[]{:S(2)}) %collective-permute-start.33) | collective-permute-done | bytes 147488 | tf_op jit(solution)/shard_map/ppermute | solution.py:555
  71.5 2.2 %shard_map.147 = (bf16[64,2304]{1,0:T(8,128)(2,1)S(1)}, bf16[64,2304]{1,0:T(8,128)(2,1)S(1)}) custom-call(s32[4,8]{1,0:T(4,128)S(1)} %get-tuple-element.29.clips, bf16[32,2304]{1,0:T(8,128)(2,1)S(1)} %get-tuple-element.35.refs_0_, bf16[32,2304]{1,0:T(8,128)(2,1)S(1)} %collective-permute-done.31.refs_1_, ...), custom_call_target="tpu_custom_call" | custom-call | tf_op jit(solution)/shard_map/pallas_call | solution.py:366
  73.7 1.6 %collective-permute-done.34.from_twin = bf16[64,2304]{1,0:T(8,128)(2,1)S(1)} collective-permute-done((bf16[64,2304]{1,0:T(8,128)(2,1)S(1)}, bf16[64,2304]{1,0:T(8,128)(2,1)S(1)}, u32[]{:S(2)}, u32[]{:S(2)}) %collective-permute-start.34) | collective-permute-done | bytes 294944 | tf_op jit(solution)/shard_map/ppermute | solution.py:549
  75.3 1.7 %collective-permute-start.35 = (bf16[32,2304]{1,0:T(8,128)(2,1)S(1)}, bf16[32,2304]{1,0:T(8,128)(2,1)S(1)}, u32[]{:S(2)}, u32[]{:S(2)}) collective-permute-start(bf16[32,2304]{1,0:T(8,128)(2,1)S(1)} %get-tuple-element.42), channel_id=1, source_target_pairs={{0,2},{1,3},{2,0},{3,1},{4,6},{5,7},{6,4},{7,5},{8,10},{9,11},{10,... | collective-permute-start | bytes 442376 | tf_op jit(solution)/shard_map/ppermute | solution.py:555
  78.9 2.4 %collective-permute-done.35.refs_1_ = bf16[32,2304]{1,0:T(8,128)(2,1)S(1)} collective-permute-done((bf16[32,2304]{1,0:T(8,128)(2,1)S(1)}, bf16[32,2304]{1,0:T(8,128)(2,1)S(1)}, u32[]{:S(2)}, u32[]{:S(2)}) %collective-permute-start.35) | collective-permute-done | bytes 147488 | tf_op jit(solution)/shard_map/ppermute | solution.py:555
  81.3 2.5 %collective-permute-done.36.refs_2_ = bf16[32,2304]{1,0:T(8,128)(2,1)S(1)} collective-permute-done((bf16[32,2304]{1,0:T(8,128)(2,1)S(1)}, bf16[32,2304]{1,0:T(8,128)(2,1)S(1)}, u32[]{:S(2)}, u32[]{:S(2)}) %collective-permute-start.36) | collective-permute-done | bytes 147488 | tf_op jit(solution)/shard_map/ppermute | solution.py:555
  83.8 1.8 %collective-permute-done.37.refs_3_ = bf16[32,2304]{1,0:T(8,128)(2,1)S(1)} collective-permute-done((bf16[32,2304]{1,0:T(8,128)(2,1)S(1)}, bf16[32,2304]{1,0:T(8,128)(2,1)S(1)}, u32[]{:S(2)}, u32[]{:S(2)}) %collective-permute-start.37) | collective-permute-done | bytes 147488 | tf_op jit(solution)/shard_map/ppermute | solution.py:555
  85.6 4.9 %shard_map.149 = (bf16[128,1152]{1,0:T(8,128)(2,1)S(1)}, bf16[128,1152]{1,0:T(8,128)(2,1)S(1)}, bf16[32,2,1152]{2,1,0:T(2,128)(2,1)}) custom-call(s32[4,8]{1,0:T(4,128)S(1)} %get-tuple-element.29.clips, bf16[32,2304]{1,0:T(8,128)(2,1)S(1)} %get-tuple-element.41.refs_0_, bf16[32,2304]{1,0:T(8,128)(2,1)S(1)} %collective-permute-done.35.refs_1_, ...), custom_call_target="tpu_custom_call" | custom-call | tf_op jit(solution)/shard_map/pallas_call | solution.py:366
  90.5 4.6 %all-to-all-start = ((bf16[32,2,1152]{2,1,0:T(2,128)(2,1)}), bf16[32,2,1152]{2,1,0:T(2,128)(2,1)S(1)}, u32[]{:S(2)}, u32[]{:S(2)}) async-start(bf16[32,2,1152]{2,1,0:T(2,128)(2,1)} %get-tuple-element.54), calls=%async_computation | async-start | bytes 294912 | tf_op jit(solution)/shard_map/all_to_all | solution.py:590
  95.2 2.5 %copy-done.1 = bf16[16,144,1152]{2,1,0:T(8,128)(2,1)S(1)} copy-done((bf16[16,144,1152]{2,1,0:T(8,128)(2,1)S(1)}, bf16[16,144,1152]{2,1,0:T(8,128)(2,1)}, u32[]{:S(2)}) %copy-start.1) | copy-done | bytes 5308440
  97.7 1.9 %shard_map.150 = (bf16[128,1152]{1,0:T(8,128)(2,1)}, bf16[128,1152]{1,0:T(8,128)(2,1)}) custom-call(bf16[32,2304]{1,0:T(8,128)(2,1)S(1)} %get-tuple-element.41.refs_0_, bf16[32,2304]{1,0:T(8,128)(2,1)S(1)} %collective-permute-done.35.refs_1_, bf16[32,2304]{1,0:T(8,128)(2,1)S(1)} %collective-permute-done.36.refs_2_, ...), custom_call_target="tpu_custom_call" | custom-call | tf_op jit(solution)/shard_map/pallas_call | solution.py:366
  99.6 4.0 %all-to-all-done = bf16[32,2,1152]{2,1,0:T(2,128)(2,1)S(1)} async-done(((bf16[32,2,1152]{2,1,0:T(2,128)(2,1)}), bf16[32,2,1152]{2,1,0:T(2,128)(2,1)S(1)}, u32[]{:S(2)}, u32[]{:S(2)}) %all-to-all-start) | async-done | bytes 147488 | tf_op jit(solution)/shard_map/all_to_all | solution.py:590
  (81 shorter events, 20.6 us)
Async XLA Ops:
  2.6 7.7 %collective-permute-start.4 = (bf16[144,1152]{1,0:T(8,128)(2,1)S(1)}, bf16[144,1152]{1,0:T(8,128)(2,1)S(1)}, u32[]{:S(2)}, u32[]{:S(2)}) collective-permute-start(bf16[144,1152]{1,0:T(8,128)(2,1)S(1)} %get-tuple-element.56.refs_0_), channel_id=1, source_target_pairs={{0,4},{1,3},{4,8},{5,1},{8,12},{9,5},{12,14},{13,9},{14,10},{15,13... | collective-permute-start | bytes 995336 | tf_op jit(solution)/shard_map/ppermute | solution.py:393
  5.2 8.6 %collective-permute-start.1 = (bf16[144,1152]{1,0:T(8,128)(2,1)S(1)}, bf16[144,1152]{1,0:T(8,128)(2,1)S(1)}, u32[]{:S(2)}, u32[]{:S(2)}) collective-permute-start(bf16[144,1152]{1,0:T(8,128)(2,1)S(1)} %collective-permute-done.refs_1_), channel_id=1, source_target_pairs={{0,4},{1,3},{4,8},{5,1},{8,12},{9,5},{12,14},{13,9},{14,10},{15,13... | collective-permute-start | bytes 995336 | tf_op jit(solution)/shard_map/ppermute | solution.py:393
  6.8 7.0 %collective-permute-start.7 = (bf16[144,1152]{1,0:T(8,128)(2,1)S(1)}, bf16[144,1152]{1,0:T(8,128)(2,1)S(1)}, u32[]{:S(2)}, u32[]{:S(2)}) collective-permute-start(bf16[144,1152]{1,0:T(8,128)(2,1)S(1)} %get-tuple-element.55.refs_16_), channel_id=1, source_target_pairs={{0,1},{1,0},{2,3},{3,2},{4,5},{5,4},{6,7},{7,6},{8,9},{9,8},{10,11... | collective-permute-start | bytes 995336 | tf_op jit(solution)/shard_map/ppermute | solution.py:399
  10.3 5.6 %collective-permute-start.6 = (bf16[144,1152]{1,0:T(8,128)(2,1)S(1)}, bf16[144,1152]{1,0:T(8,128)(2,1)S(1)}, u32[]{:S(2)}, u32[]{:S(2)}) collective-permute-start(bf16[144,1152]{1,0:T(8,128)(2,1)S(1)} %collective-permute-done.4.refs_2_), channel_id=1, source_target_pairs={{0,1},{1,0},{2,3},{3,2},{4,5},{5,4},{6,7},{7,6},{8,9},{9,8},{10,11... | collective-permute-start | bytes 995336 | tf_op jit(solution)/shard_map/ppermute | solution.py:399
  10.3 7.1 %collective-permute-start.5 = (bf16[144,1152]{1,0:T(8,128)(2,1)S(1)}, bf16[144,1152]{1,0:T(8,128)(2,1)S(1)}, u32[]{:S(2)}, u32[]{:S(2)}) collective-permute-start(bf16[144,1152]{1,0:T(8,128)(2,1)S(1)} %collective-permute-done.4.refs_2_), channel_id=1, source_target_pairs={{0,4},{1,3},{4,8},{5,1},{8,12},{9,5},{12,14},{13,9},{14,10},{15,13... | collective-permute-start | bytes 995336 | tf_op jit(solution)/shard_map/ppermute | solution.py:393
  12.4 10.1 %collective-permute-start.10 = (bf16[144,1152]{1,0:T(8,128)(2,1)S(1)}, bf16[144,1152]{1,0:T(8,128)(2,1)S(1)}, u32[]{:S(2)}, u32[]{:S(2)}) collective-permute-start(bf16[144,1152]{1,0:T(8,128)(2,1)S(1)} %collective-permute-done.4.refs_2_), channel_id=1, source_target_pairs={{0,16},{16,0},{1,17},{17,1},{2,18},{18,2},{3,19},{19,3},{4,20},{20... | collective-permute-start | bytes 995336 | tf_op jit(solution)/shard_map/ppermute | solution.py:396
  13.8 8.6 %collective-permute-start.8 = (bf16[144,1152]{1,0:T(8,128)(2,1)S(1)}, bf16[144,1152]{1,0:T(8,128)(2,1)S(1)}, u32[]{:S(2)}, u32[]{:S(2)}) collective-permute-start(bf16[144,1152]{1,0:T(8,128)(2,1)S(1)} %collective-permute-done.1.refs_1_.refs_6_), channel_id=1, source_target_pairs={{0,1},{1,0},{2,3},{3,2},{4,5},{5,4},{6,7},{7,6},{8,9},{9,8},{10,11... | collective-permute-start | bytes 995336 | tf_op jit(solution)/shard_map/ppermute | solution.py:399
  13.9 8.6 %collective-permute-start.3 = (bf16[144,1152]{1,0:T(8,128)(2,1)S(1)}, bf16[144,1152]{1,0:T(8,128)(2,1)S(1)}, u32[]{:S(2)}, u32[]{:S(2)}) collective-permute-start(bf16[144,1152]{1,0:T(8,128)(2,1)S(1)} %collective-permute-done.1.refs_1_.refs_6_), channel_id=1, source_target_pairs={{0,4},{1,3},{4,8},{5,1},{8,12},{9,5},{12,14},{13,9},{14,10},{15,13... | collective-permute-start | bytes 995336 | tf_op jit(solution)/shard_map/ppermute | solution.py:393
  17.4 7.2 %collective-permute-start.13 = (bf16[144,1152]{1,0:T(8,128)(2,1)S(1)}, bf16[144,1152]{1,0:T(8,128)(2,1)S(1)}, u32[]{:S(2)}, u32[]{:S(2)}) collective-permute-start(bf16[144,1152]{1,0:T(8,128)(2,1)S(1)} %shard_map.139.refs_1_.refs_3_), channel_id=1, source_target_pairs={{0,4},{1,3},{4,8},{5,1},{8,12},{9,5},{12,14},{13,9},{14,10},{15,13... | collective-permute-start | bytes 995336 | tf_op jit(solution)/shard_map/ppermute | solution.py:393
  20.9 9.1 %collective-permute-start.2 = (bf16[144,1152]{1,0:T(8,128)(2,1)S(1)}, bf16[144,1152]{1,0:T(8,128)(2,1)S(1)}, u32[]{:S(2)}, u32[]{:S(2)}) collective-permute-start(bf16[144,1152]{1,0:T(8,128)(2,1)S(1)} %collective-permute-done.1.refs_1_.refs_6_), channel_id=1, source_target_pairs={{0,16},{16,0},{1,17},{17,1},{2,18},{18,2},{3,19},{19,3},{4,20},{20... | collective-permute-start | bytes 995336 | tf_op jit(solution)/shard_map/ppermute | solution.py:396
  22.5 9.0 %collective-permute-start.12 = (bf16[144,1152]{1,0:T(8,128)(2,1)S(1)}, bf16[144,1152]{1,0:T(8,128)(2,1)S(1)}, u32[]{:S(2)}, u32[]{:S(2)}) collective-permute-start(bf16[144,1152]{1,0:T(8,128)(2,1)S(1)} %shard_map.140.refs_1_.refs_7_), channel_id=1, source_target_pairs={{0,1},{1,0},{2,3},{3,2},{4,5},{5,4},{6,7},{7,6},{8,9},{9,8},{10,11... | collective-permute-start | bytes 995336 | tf_op jit(solution)/shard_map/ppermute | solution.py:399
  23.0 8.5 %collective-permute-start.9 = (bf16[144,1152]{1,0:T(8,128)(2,1)S(1)}, bf16[144,1152]{1,0:T(8,128)(2,1)S(1)}, u32[]{:S(2)}, u32[]{:S(2)}) collective-permute-start(bf16[144,1152]{1,0:T(8,128)(2,1)S(1)} %shard_map.140.refs_1_.refs_7_), channel_id=1, source_target_pairs={{0,4},{1,3},{4,8},{5,1},{8,12},{9,5},{12,14},{13,9},{14,10},{15,13... | collective-permute-start | bytes 995336 | tf_op jit(solution)/shard_map/ppermute | solution.py:393
  24.6 9.1 %collective-permute-start.14 = (bf16[144,1152]{1,0:T(8,128)(2,1)S(1)}, bf16[144,1152]{1,0:T(8,128)(2,1)S(1)}, u32[]{:S(2)}, u32[]{:S(2)}) collective-permute-start(bf16[144,1152]{1,0:T(8,128)(2,1)S(1)} %shard_map.142.refs_4_), channel_id=1, source_target_pairs={{0,4},{1,3},{4,8},{5,1},{8,12},{9,5},{12,14},{13,9},{14,10},{15,13... | collective-permute-start | bytes 995336 | tf_op jit(solution)/shard_map/ppermute | solution.py:393
  26.7 10.5 %collective-permute-start.19 = (bf16[144,1152]{1,0:T(8,128)(2,1)S(1)}, bf16[144,1152]{1,0:T(8,128)(2,1)S(1)}, u32[]{:S(2)}, u32[]{:S(2)}) collective-permute-start(bf16[144,1152]{1,0:T(8,128)(2,1)S(1)} %collective-permute-done.10.refs_2_.refs_18_), channel_id=1, source_target_pairs={{0,4},{1,3},{4,8},{5,1},{8,12},{9,5},{12,14},{13,9},{14,10},{15,13... | collective-permute-start | bytes 995336 | tf_op jit(solution)/shard_map/ppermute | solution.py:393
  30.0 8.1 %collective-permute-start.20 = (bf16[144,1152]{1,0:T(8,128)(2,1)S(1)}, bf16[144,1152]{1,0:T(8,128)(2,1)S(1)}, u32[]{:S(2)}, u32[]{:S(2)}) collective-permute-start(bf16[144,1152]{1,0:T(8,128)(2,1)S(1)} %shard_map.142.refs_4_), channel_id=1, source_target_pairs={{0,16},{16,0},{1,17},{17,1},{2,18},{18,2},{3,19},{19,3},{4,20},{20... | collective-permute-start | bytes 995336 | tf_op jit(solution)/shard_map/ppermute | solution.py:396
  31.5 6.6 %collective-permute-start.18 = (bf16[144,1152]{1,0:T(8,128)(2,1)S(1)}, bf16[144,1152]{1,0:T(8,128)(2,1)S(1)}, u32[]{:S(2)}, u32[]{:S(2)}) collective-permute-start(bf16[144,1152]{1,0:T(8,128)(2,1)S(1)} %collective-permute-done.9.refs_4_.refs_2_.refs_8_), channel_id=1, source_target_pairs={{0,1},{1,0},{2,3},{3,2},{4,5},{5,4},{6,7},{7,6},{8,9},{9,8},{10,11... | collective-permute-start | bytes 995336 | tf_op jit(solution)/shard_map/ppermute | solution.py:399
  33.6 4.9 %collective-permute-start.17 = (bf16[144,1152]{1,0:T(8,128)(2,1)S(1)}, bf16[144,1152]{1,0:T(8,128)(2,1)S(1)}, u32[]{:S(2)}, u32[]{:S(2)}) collective-permute-start(bf16[144,1152]{1,0:T(8,128)(2,1)S(1)} %shard_map.143.refs_5_), channel_id=1, source_target_pairs={{0,1},{1,0},{2,3},{3,2},{4,5},{5,4},{6,7},{7,6},{8,9},{9,8},{10,11... | collective-permute-start | bytes 995336 | tf_op jit(solution)/shard_map/ppermute | solution.py:399
  33.6 7.1 %collective-permute-start.22 = (bf16[144,1152]{1,0:T(8,128)(2,1)S(1)}, bf16[144,1152]{1,0:T(8,128)(2,1)S(1)}, u32[]{:S(2)}, u32[]{:S(2)}) collective-permute-start(bf16[144,1152]{1,0:T(8,128)(2,1)S(1)} %get-tuple-element.32.refs_1_.refs_22_), channel_id=1, source_target_pairs={{0,4},{1,3},{4,8},{5,1},{8,12},{9,5},{12,14},{13,9},{14,10},{15,13... | collective-permute-start | bytes 995336 | tf_op jit(solution)/shard_map/ppermute | solution.py:393
  37.2 5.1 %collective-permute-start.15 = (bf16[144,1152]{1,0:T(8,128)(2,1)S(1)}, bf16[144,1152]{1,0:T(8,128)(2,1)S(1)}, u32[]{:S(2)}, u32[]{:S(2)}) collective-permute-start(bf16[144,1152]{1,0:T(8,128)(2,1)S(1)} %shard_map.139.refs_1_.refs_3_), channel_id=1, source_target_pairs={{0,1},{1,0},{2,3},{3,2},{4,5},{5,4},{6,7},{7,6},{8,9},{9,8},{10,11... | collective-permute-start | bytes 995336 | tf_op jit(solution)/shard_map/ppermute | solution.py:399
  38.1 4.8 %collective-permute-start.16 = (bf16[144,1152]{1,0:T(8,128)(2,1)S(1)}, bf16[144,1152]{1,0:T(8,128)(2,1)S(1)}, u32[]{:S(2)}, u32[]{:S(2)}) collective-permute-start(bf16[144,1152]{1,0:T(8,128)(2,1)S(1)} %shard_map.142.refs_4_), channel_id=1, source_target_pairs={{0,1},{1,0},{2,3},{3,2},{4,5},{5,4},{6,7},{7,6},{8,9},{9,8},{10,11... | collective-permute-start | bytes 995336 | tf_op jit(solution)/shard_map/ppermute | solution.py:399
  38.6 9.8 %collective-permute-start.21 = (bf16[144,1152]{1,0:T(8,128)(2,1)S(1)}, bf16[144,1152]{1,0:T(8,128)(2,1)S(1)}, u32[]{:S(2)}, u32[]{:S(2)}) collective-permute-start(bf16[144,1152]{1,0:T(8,128)(2,1)S(1)} %shard_map.143.refs_5_), channel_id=1, source_target_pairs={{0,16},{16,0},{1,17},{17,1},{2,18},{18,2},{3,19},{19,3},{4,20},{20... | collective-permute-start | bytes 995336 | tf_op jit(solution)/shard_map/ppermute | solution.py:396
  40.8 7.6 %collective-permute-start.23 = (bf16[144,1152]{1,0:T(8,128)(2,1)S(1)}, bf16[144,1152]{1,0:T(8,128)(2,1)S(1)}, u32[]{:S(2)}, u32[]{:S(2)}) collective-permute-start(bf16[144,1152]{1,0:T(8,128)(2,1)S(1)} %shard_map.144.refs_23_), channel_id=1, source_target_pairs={{0,4},{1,3},{4,8},{5,1},{8,12},{9,5},{12,14},{13,9},{14,10},{15,13... | collective-permute-start | bytes 995336 | tf_op jit(solution)/shard_map/ppermute | solution.py:393
  42.3 6.5 %collective-permute-start.27 = (bf16[144,1152]{1,0:T(8,128)(2,1)S(1)}, bf16[144,1152]{1,0:T(8,128)(2,1)S(1)}, u32[]{:S(2)}, u32[]{:S(2)}) collective-permute-start(bf16[144,1152]{1,0:T(8,128)(2,1)S(1)} %get-tuple-element.32.refs_1_.refs_22_), channel_id=1, source_target_pairs={{0,1},{1,0},{2,3},{3,2},{4,5},{5,4},{6,7},{7,6},{8,9},{9,8},{10,11... | collective-permute-start | bytes 995336 | tf_op jit(solution)/shard_map/ppermute | solution.py:399
  42.4 6.4 %collective-permute-start.25 = (bf16[144,1152]{1,0:T(8,128)(2,1)S(1)}, bf16[144,1152]{1,0:T(8,128)(2,1)S(1)}, u32[]{:S(2)}, u32[]{:S(2)}) collective-permute-start(bf16[144,1152]{1,0:T(8,128)(2,1)S(1)} %collective-permute-done.20.refs_3_.refs_20_), channel_id=1, source_target_pairs={{0,1},{1,0},{2,3},{3,2},{4,5},{5,4},{6,7},{7,6},{8,9},{9,8},{10,11... | collective-permute-start | bytes 995336 | tf_op jit(solution)/shard_map/ppermute | solution.py:399
  42.9 7.1 %collective-permute-start.28 = (bf16[144,1152]{1,0:T(8,128)(2,1)S(1)}, bf16[144,1152]{1,0:T(8,128)(2,1)S(1)}, u32[]{:S(2)}, u32[]{:S(2)}) collective-permute-start(bf16[144,1152]{1,0:T(8,128)(2,1)S(1)} %shard_map.144.refs_23_), channel_id=1, source_target_pairs={{0,1},{1,0},{2,3},{3,2},{4,5},{5,4},{6,7},{7,6},{8,9},{9,8},{10,11... | collective-permute-start | bytes 995336 | tf_op jit(solution)/shard_map/ppermute | solution.py:399
  59.6 7.5 %collective-permute-start.31 = (bf16[32,2304]{1,0:T(8,128)(2,1)S(1)}, bf16[32,2304]{1,0:T(8,128)(2,1)S(1)}, u32[]{:S(2)}, u32[]{:S(2)}) collective-permute-start(bf16[32,2304]{1,0:T(8,128)(2,1)S(1)} %get-tuple-element.36), channel_id=1, source_target_pairs={{0,2},{1,3},{2,0},{3,1},{4,6},{5,7},{6,4},{7,5},{8,10},{9,11},{10,... | collective-permute-start | bytes 442376 | tf_op jit(solution)/shard_map/ppermute | solution.py:555
  62.9 6.7 %collective-permute-start.32 = (bf16[32,2304]{1,0:T(8,128)(2,1)S(1)}, bf16[32,2304]{1,0:T(8,128)(2,1)S(1)}, u32[]{:S(2)}, u32[]{:S(2)}) collective-permute-start(bf16[32,2304]{1,0:T(8,128)(2,1)S(1)} %get-tuple-element.37), channel_id=1, source_target_pairs={{0,4},{1,5},{2,6},{3,7},{4,0},{5,1},{6,2},{7,3},{8,12},{9,13},{10,... | collective-permute-start | bytes 442376 | tf_op jit(solution)/shard_map/ppermute | solution.py:555
  64.1 7.4 %collective-permute-start.33 = (bf16[32,2304]{1,0:T(8,128)(2,1)S(1)}, bf16[32,2304]{1,0:T(8,128)(2,1)S(1)}, u32[]{:S(2)}, u32[]{:S(2)}) collective-permute-start(bf16[32,2304]{1,0:T(8,128)(2,1)S(1)} %get-tuple-element.38), channel_id=1, source_target_pairs={{0,6},{1,7},{2,4},{3,5},{4,2},{5,3},{6,0},{7,1},{8,14},{9,15},{10,... | collective-permute-start | bytes 442376 | tf_op jit(solution)/shard_map/ppermute | solution.py:555
  75.3 6.0 %collective-permute-start.35 = (bf16[32,2304]{1,0:T(8,128)(2,1)S(1)}, bf16[32,2304]{1,0:T(8,128)(2,1)S(1)}, u32[]{:S(2)}, u32[]{:S(2)}) collective-permute-start(bf16[32,2304]{1,0:T(8,128)(2,1)S(1)} %get-tuple-element.42), channel_id=1, source_target_pairs={{0,2},{1,3},{2,0},{3,1},{4,6},{5,7},{6,4},{7,5},{8,10},{9,11},{10,... | collective-permute-start | bytes 442376 | tf_op jit(solution)/shard_map/ppermute | solution.py:555
  77.1 6.7 %collective-permute-start.36 = (bf16[32,2304]{1,0:T(8,128)(2,1)S(1)}, bf16[32,2304]{1,0:T(8,128)(2,1)S(1)}, u32[]{:S(2)}, u32[]{:S(2)}) collective-permute-start(bf16[32,2304]{1,0:T(8,128)(2,1)S(1)} %get-tuple-element.43), channel_id=1, source_target_pairs={{0,4},{1,5},{2,6},{3,7},{4,0},{5,1},{6,2},{7,3},{8,12},{9,13},{10,... | collective-permute-start | bytes 442376 | tf_op jit(solution)/shard_map/ppermute | solution.py:555
  78.3 7.4 %collective-permute-start.37 = (bf16[32,2304]{1,0:T(8,128)(2,1)S(1)}, bf16[32,2304]{1,0:T(8,128)(2,1)S(1)}, u32[]{:S(2)}, u32[]{:S(2)}) collective-permute-start(bf16[32,2304]{1,0:T(8,128)(2,1)S(1)} %get-tuple-element.44), channel_id=1, source_target_pairs={{0,6},{1,7},{2,4},{3,5},{4,2},{5,3},{6,0},{7,1},{8,14},{9,15},{10,... | collective-permute-start | bytes 442376 | tf_op jit(solution)/shard_map/ppermute | solution.py:555
  90.5 13.0 %all-to-all-start = ((bf16[32,2,1152]{2,1,0:T(2,128)(2,1)}), bf16[32,2,1152]{2,1,0:T(2,128)(2,1)S(1)}, u32[]{:S(2)}, u32[]{:S(2)}) async-start(bf16[32,2,1152]{2,1,0:T(2,128)(2,1)} %get-tuple-element.54), calls=%async_computation | async-start | bytes 294912 | tf_op jit(solution)/shard_map/all_to_all | solution.py:590
  (15 other events, 209.7 us)

commit v4 on v3

--- a/solution.py
+++ b/solution.py
@@ -231,20 +231,19 @@
 
 def front(rows, layouts, order_of, direct, clips, tokens, gains, *refs):
     sends = 2 if direct else 1
-    pieces, refs = refs[: -8 - sends], refs[-8 - sends :]
+    pieces, refs = refs[: -7 - sends], refs[-7 - sends :]
     hidden, saved, shares_out, space, time = refs[:5]
-    project, mixed, stage = refs[-3:]
+    mixed, stage = refs[-2:]
     assemble(layouts, order_of(), pieces, space, time)
     allowed, live = space_masks(clips)
     values = tokens[0].astype(F32)
     normed = (values * inverse_size(values) * gains[:1]).astype(BF16)
     mixed[...] = jnp.zeros_like(mixed)
     stride = rows.qkv_cut
-    project[...] = nt(rows.qkv_weight(space), normed)
-    saved[...] = project[...].astype(BF16)
+    saved[...] = nt(rows.qkv_weight(space), normed)
     scale = rows.head ** (-0.5)
     queries, keys, values_in = (
-        [read_rows(project, rows.qkv_spans(which, head, stride)).astype(BF16) for head in range(HEADS)]
+        [read_rows(saved, rows.qkv_spans(which, head, stride)).astype(BF16) for head in range(HEADS)]
         for which in range(3)
     )
     shares = [share.astype(BF16) for share in shares_of(queries, keys, allowed, live, scale)]
@@ -260,7 +259,7 @@
     both = nt(jnp.concatenate([normed, tokens[1]], axis=0), time[...].reshape(rows.total, -1))
     count = values.shape[0]
     stage[...] = jnp.where(out_columns(rows), both[count:], both[:count]).astype(BF16)
-    give(direct, stage, refs[5:-3])
+    give(direct, stage, refs[5:-2])
 
 
 def time_core(rows, near, slots, direct, clips, *refs):
@@ -434,8 +433,8 @@
     x_o2_twin = twin(x_o2)
     x_t2_twin = twin(x_t2)
     x_o3_twin = twin(x_o3)
+    x_o4_twin = twin(x_o4)
     x_t3_twin = twin(x_t3)
-    x_o4_twin = twin(x_o4)
     mine = {"o0": (own, 0), "t0": (t0, 0)}
     other = {"o0": (own_other, 0), "t0": (t0_other, 0)}
     mine |= {"o1": (o1, 0), "o1_twin": (o1_twin, 0)}
@@ -560,13 +559,13 @@
         functools.partial(front, rows, layouts, order_of, direct),
         (
             jax.ShapeDtypeStruct((FRAME, features), BF16),
-            jax.ShapeDtypeStruct((rows.qkv_total, FRAME), BF16),
+            jax.ShapeDtypeStruct((rows.qkv_total, FRAME), F32),
             jax.ShapeDtypeStruct((HEADS, FRAME, FRAME), BF16),
             weight_shape,
             weight_shape,
             *parts,
         ),
-        [qkv_wide, out_wide, stage],
+        [out_wide, stage],
         clips,
         (both_tokens, both_gains, *pieces),
     )

time: 105 us -> 105 us (level)
  no operation moved by 1% of the time
where the time goes in v4:
time: 105 us; the launch traced here: 104 us
  starting transfers between devices  40.8 us (39%)
  waiting for transfers between devices  40.1 us (38%)
  Pallas kernels  16.5 us (16%)
  local copies, waits for them, and re-layouts  3.93 us (4%)
  other arithmetic  2.2 us (2%)
    ppermute x10, starting transfers between devices, ring(): return lax.ppermute(rows, 'ctx', ring_pairs)  18.8 us
    pallas_call x6, Pallas kernels, call(): pl.pallas_call(body, out_shape=out_shapes, in_specs=[scalars] * len(clips...  16.5 us
    ppermute x6, waiting for transfers between devices, exchange(): lax.ppermute(rows_away, 'ctx', [(index, index ^ 2 * distance) for index i...  13.8 us
    ppermute x10, waiting for transfers between devices, ring(): return lax.ppermute(rows, 'ctx', ring_pairs)  9.79 us
    ppermute x6, starting transfers between devices, exchange(): lax.ppermute(rows_away, 'ctx', [(index, index ^ 2 * distance) for index i...  8.43 us
    ppermute x4, waiting for transfers between devices, across(): lax.ppermute(rows, 'dp', [(index, index ^ 1) for index in range(planes)])  7.9 us
    ppermute x4, starting transfers between devices, across(): lax.ppermute(rows, 'dp', [(index, index ^ 1) for index in range(planes)])  6.03 us
    all_to_all x1, starting transfers between devices, shards(): lax.all_to_all(gains, ('dp', 'ctx'), split_axis=0, concat_axis=0, tiled=T...  4.61 us
  transfers between devices with their start and end apart: 39, of which 19 were waited for; matrix products, arithmetic and copies ran while one was open for 1% of the time, Pallas kernels for 2%

profile of v4, /device:TPU:0, one launch (start us, length us, event | category | flops | bytes accessed | tf_op | source)
XLA Modules:
  0.0 104.3 jit_solution(16443544875144138829)
XLA Ops:
  2.6 2.6 %collective-permute-start.4 = (bf16[144,1152]{1,0:T(8,128)(2,1)S(1)}, bf16[144,1152]{1,0:T(8,128)(2,1)S(1)}, u32[]{:S(2)}, u32[]{:S(2)}) collective-permute-start(bf16[144,1152]{1,0:T(8,128)(2,1)S(1)} %get-tuple-element.56.refs_0_), channel_id=1, source_target_pairs={{0,4},{1,3},{4,8},{5,1},{8,12},{9,5},{12,14},{13,9},{14,10},{15,13... | collective-permute-start | bytes 995336 | tf_op jit(solution)/shard_map/ppermute | solution.py:392
  5.2 1.6 %collective-permute-start.1 = (bf16[144,1152]{1,0:T(8,128)(2,1)S(1)}, bf16[144,1152]{1,0:T(8,128)(2,1)S(1)}, u32[]{:S(2)}, u32[]{:S(2)}) collective-permute-start(bf16[144,1152]{1,0:T(8,128)(2,1)S(1)} %collective-permute-done.refs_1_), channel_id=1, source_target_pairs={{0,4},{1,3},{4,8},{5,1},{8,12},{9,5},{12,14},{13,9},{14,10},{15,13... | collective-permute-start | bytes 995336 | tf_op jit(solution)/shard_map/ppermute | solution.py:392
  6.8 3.5 %collective-permute-done.4.refs_2_ = bf16[144,1152]{1,0:T(8,128)(2,1)S(1)} collective-permute-done((bf16[144,1152]{1,0:T(8,128)(2,1)S(1)}, bf16[144,1152]{1,0:T(8,128)(2,1)S(1)}, u32[]{:S(2)}, u32[]{:S(2)}) %collective-permute-start.4) | collective-permute-done | bytes 331808 | tf_op jit(solution)/shard_map/ppermute | solution.py:392
  10.3 2.1 %collective-permute-start.5 = (bf16[144,1152]{1,0:T(8,128)(2,1)S(1)}, bf16[144,1152]{1,0:T(8,128)(2,1)S(1)}, u32[]{:S(2)}, u32[]{:S(2)}) collective-permute-start(bf16[144,1152]{1,0:T(8,128)(2,1)S(1)} %collective-permute-done.4.refs_2_), channel_id=1, source_target_pairs={{0,4},{1,3},{4,8},{5,1},{8,12},{9,5},{12,14},{13,9},{14,10},{15,13... | collective-permute-start | bytes 995336 | tf_op jit(solution)/shard_map/ppermute | solution.py:392
  13.9 2.1 %collective-permute-start.3 = (bf16[144,1152]{1,0:T(8,128)(2,1)S(1)}, bf16[144,1152]{1,0:T(8,128)(2,1)S(1)}, u32[]{:S(2)}, u32[]{:S(2)}) collective-permute-start(bf16[144,1152]{1,0:T(8,128)(2,1)S(1)} %collective-permute-done.1.refs_1_.refs_6_), channel_id=1, source_target_pairs={{0,4},{1,3},{4,8},{5,1},{8,12},{9,5},{12,14},{13,9},{14,10},{15,13... | collective-permute-start | bytes 995336 | tf_op jit(solution)/shard_map/ppermute | solution.py:392
  17.4 2.1 %collective-permute-start.13 = (bf16[144,1152]{1,0:T(8,128)(2,1)S(1)}, bf16[144,1152]{1,0:T(8,128)(2,1)S(1)}, u32[]{:S(2)}, u32[]{:S(2)}) collective-permute-start(bf16[144,1152]{1,0:T(8,128)(2,1)S(1)} %shard_map.139.refs_1_.refs_3_), channel_id=1, source_target_pairs={{0,4},{1,3},{4,8},{5,1},{8,12},{9,5},{12,14},{13,9},{14,10},{15,13... | collective-permute-start | bytes 995336 | tf_op jit(solution)/shard_map/ppermute | solution.py:392
  20.9 1.6 %collective-permute-start.2 = (bf16[144,1152]{1,0:T(8,128)(2,1)S(1)}, bf16[144,1152]{1,0:T(8,128)(2,1)S(1)}, u32[]{:S(2)}, u32[]{:S(2)}) collective-permute-start(bf16[144,1152]{1,0:T(8,128)(2,1)S(1)} %collective-permute-done.1.refs_1_.refs_6_), channel_id=1, source_target_pairs={{0,16},{16,0},{1,17},{17,1},{2,18},{18,2},{3,19},{19,3},{4,20},{20... | collective-permute-start | bytes 995336 | tf_op jit(solution)/shard_map/ppermute | solution.py:395
  23.0 1.6 %collective-permute-start.9 = (bf16[144,1152]{1,0:T(8,128)(2,1)S(1)}, bf16[144,1152]{1,0:T(8,128)(2,1)S(1)}, u32[]{:S(2)}, u32[]{:S(2)}) collective-permute-start(bf16[144,1152]{1,0:T(8,128)(2,1)S(1)} %shard_map.140.refs_1_.refs_7_), channel_id=1, source_target_pairs={{0,4},{1,3},{4,8},{5,1},{8,12},{9,5},{12,14},{13,9},{14,10},{15,13... | collective-permute-start | bytes 995336 | tf_op jit(solution)/shard_map/ppermute | solution.py:392
  24.6 2.0 %collective-permute-start.14 = (bf16[144,1152]{1,0:T(8,128)(2,1)S(1)}, bf16[144,1152]{1,0:T(8,128)(2,1)S(1)}, u32[]{:S(2)}, u32[]{:S(2)}) collective-permute-start(bf16[144,1152]{1,0:T(8,128)(2,1)S(1)} %shard_map.142.refs_4_), channel_id=1, source_target_pairs={{0,4},{1,3},{4,8},{5,1},{8,12},{9,5},{12,14},{13,9},{14,10},{15,13... | collective-permute-start | bytes 995336 | tf_op jit(solution)/shard_map/ppermute | solution.py:392
  26.7 1.6 %collective-permute-start.19 = (bf16[144,1152]{1,0:T(8,128)(2,1)S(1)}, bf16[144,1152]{1,0:T(8,128)(2,1)S(1)}, u32[]{:S(2)}, u32[]{:S(2)}) collective-permute-start(bf16[144,1152]{1,0:T(8,128)(2,1)S(1)} %collective-permute-done.10.refs_2_.refs_18_), channel_id=1, source_target_pairs={{0,4},{1,3},{4,8},{5,1},{8,12},{9,5},{12,14},{13,9},{14,10},{15,13... | collective-permute-start | bytes 995336 | tf_op jit(solution)/shard_map/ppermute | solution.py:392
  28.4 1.6 %collective-permute-done.2.refs_0_ = bf16[144,1152]{1,0:T(8,128)(2,1)S(1)} collective-permute-done((bf16[144,1152]{1,0:T(8,128)(2,1)S(1)}, bf16[144,1152]{1,0:T(8,128)(2,1)S(1)}, u32[]{:S(2)}, u32[]{:S(2)}) %collective-permute-start.2) | collective-permute-done | bytes 331808 | tf_op jit(solution)/shard_map/ppermute | solution.py:395
  31.5 2.2 %collective-permute-done.14.refs_0_ = bf16[144,1152]{1,0:T(8,128)(2,1)S(1)} collective-permute-done((bf16[144,1152]{1,0:T(8,128)(2,1)S(1)}, bf16[144,1152]{1,0:T(8,128)(2,1)S(1)}, u32[]{:S(2)}, u32[]{:S(2)}) %collective-permute-start.14) | collective-permute-done | bytes 331808 | tf_op jit(solution)/shard_map/ppermute | solution.py:392
  33.6 1.6 %collective-permute-start.22 = (bf16[144,1152]{1,0:T(8,128)(2,1)S(1)}, bf16[144,1152]{1,0:T(8,128)(2,1)S(1)}, u32[]{:S(2)}, u32[]{:S(2)}) collective-permute-start(bf16[144,1152]{1,0:T(8,128)(2,1)S(1)} %get-tuple-element.32.refs_1_.refs_22_), channel_id=1, source_target_pairs={{0,4},{1,3},{4,8},{5,1},{8,12},{9,5},{12,14},{13,9},{14,10},{15,13... | collective-permute-start | bytes 995336 | tf_op jit(solution)/shard_map/ppermute | solution.py:392
  35.2 2.0 %collective-permute-done.19.refs_4_.refs_19_ = bf16[144,1152]{1,0:T(8,128)(2,1)S(1)} collective-permute-done((bf16[144,1152]{1,0:T(8,128)(2,1)S(1)}, bf16[144,1152]{1,0:T(8,128)(2,1)S(1)}, u32[]{:S(2)}, u32[]{:S(2)}) %collective-permute-start.19) | collective-permute-done | bytes 331808 | tf_op jit(solution)/shard_map/ppermute | solution.py:392
  40.8 1.6 %collective-permute-start.23 = (bf16[144,1152]{1,0:T(8,128)(2,1)S(1)}, bf16[144,1152]{1,0:T(8,128)(2,1)S(1)}, u32[]{:S(2)}, u32[]{:S(2)}) collective-permute-start(bf16[144,1152]{1,0:T(8,128)(2,1)S(1)} %shard_map.144.refs_23_), channel_id=1, source_target_pairs={{0,4},{1,3},{4,8},{5,1},{8,12},{9,5},{12,14},{13,9},{14,10},{15,13... | collective-permute-start | bytes 995336 | tf_op jit(solution)/shard_map/ppermute | solution.py:392
  43.0 5.4 %collective-permute-done.21.refs_21_ = bf16[144,1152]{1,0:T(8,128)(2,1)S(1)} collective-permute-done((bf16[144,1152]{1,0:T(8,128)(2,1)S(1)}, bf16[144,1152]{1,0:T(8,128)(2,1)S(1)}, u32[]{:S(2)}, u32[]{:S(2)}) %collective-permute-start.21) | collective-permute-done | bytes 331808 | tf_op jit(solution)/shard_map/ppermute | solution.py:395
  50.5 7.4 %shard_map.145 = (bf16[128,1152]{1,0:T(8,128)(2,1)S(1)}, f32[1792,128]{1,0:T(8,128)S(1)}, bf16[8,128,128]{2,1,0:T(8,128)(2,1)S(1)}, bf16[16,144,1152]{2,1,0:T(8,...) custom-call(s32[4,8]{1,0:T(4,128)S(1)} %get-tuple-element.29.clips, ...), custom_call_target="tpu_custom_call" | custom-call | tf_op jit(solution)/shard_map/pallas_call | solution.py:365
  59.6 3.3 %collective-permute-start.31 = (bf16[32,2304]{1,0:T(8,128)(2,1)S(1)}, bf16[32,2304]{1,0:T(8,128)(2,1)S(1)}, u32[]{:S(2)}, u32[]{:S(2)}) collective-permute-start(bf16[32,2304]{1,0:T(8,128)(2,1)S(1)} %get-tuple-element.36), channel_id=1, source_target_pairs={{0,2},{1,3},{2,0},{3,1},{4,6},{5,7},{6,4},{7,5},{8,10},{9,11},{10,... | collective-permute-start | bytes 442376 | tf_op jit(solution)/shard_map/ppermute | solution.py:554
  64.4 2.6 %collective-permute-done.31.refs_1_ = bf16[32,2304]{1,0:T(8,128)(2,1)S(1)} collective-permute-done((bf16[32,2304]{1,0:T(8,128)(2,1)S(1)}, bf16[32,2304]{1,0:T(8,128)(2,1)S(1)}, u32[]{:S(2)}, u32[]{:S(2)}) %collective-permute-start.31) | collective-permute-done | bytes 147488 | tf_op jit(solution)/shard_map/ppermute | solution.py:554
  67.1 2.6 %collective-permute-done.32.refs_2_ = bf16[32,2304]{1,0:T(8,128)(2,1)S(1)} collective-permute-done((bf16[32,2304]{1,0:T(8,128)(2,1)S(1)}, bf16[32,2304]{1,0:T(8,128)(2,1)S(1)}, u32[]{:S(2)}, u32[]{:S(2)}) %collective-permute-start.32) | collective-permute-done | bytes 147488 | tf_op jit(solution)/shard_map/ppermute | solution.py:554
  69.6 1.8 %collective-permute-done.33.refs_3_ = bf16[32,2304]{1,0:T(8,128)(2,1)S(1)} collective-permute-done((bf16[32,2304]{1,0:T(8,128)(2,1)S(1)}, bf16[32,2304]{1,0:T(8,128)(2,1)S(1)}, u32[]{:S(2)}, u32[]{:S(2)}) %collective-permute-start.33) | collective-permute-done | bytes 147488 | tf_op jit(solution)/shard_map/ppermute | solution.py:554
  71.5 2.2 %shard_map.147 = (bf16[64,2304]{1,0:T(8,128)(2,1)S(1)}, bf16[64,2304]{1,0:T(8,128)(2,1)S(1)}) custom-call(s32[4,8]{1,0:T(4,128)S(1)} %get-tuple-element.29.clips, bf16[32,2304]{1,0:T(8,128)(2,1)S(1)} %get-tuple-element.35.refs_0_, bf16[32,2304]{1,0:T(8,128)(2,1)S(1)} %collective-permute-done.31.refs_1_, ...), custom_call_target="tpu_custom_call" | custom-call | tf_op jit(solution)/shard_map/pallas_call | solution.py:365
  73.7 1.6 %collective-permute-done.34.from_twin = bf16[64,2304]{1,0:T(8,128)(2,1)S(1)} collective-permute-done((bf16[64,2304]{1,0:T(8,128)(2,1)S(1)}, bf16[64,2304]{1,0:T(8,128)(2,1)S(1)}, u32[]{:S(2)}, u32[]{:S(2)}) %collective-permute-start.34) | collective-permute-done | bytes 294944 | tf_op jit(solution)/shard_map/ppermute | solution.py:548
  75.3 1.7 %collective-permute-start.35 = (bf16[32,2304]{1,0:T(8,128)(2,1)S(1)}, bf16[32,2304]{1,0:T(8,128)(2,1)S(1)}, u32[]{:S(2)}, u32[]{:S(2)}) collective-permute-start(bf16[32,2304]{1,0:T(8,128)(2,1)S(1)} %get-tuple-element.42), channel_id=1, source_target_pairs={{0,2},{1,3},{2,0},{3,1},{4,6},{5,7},{6,4},{7,5},{8,10},{9,11},{10,... | collective-permute-start | bytes 442376 | tf_op jit(solution)/shard_map/ppermute | solution.py:554
  78.9 2.4 %collective-permute-done.35.refs_1_ = bf16[32,2304]{1,0:T(8,128)(2,1)S(1)} collective-permute-done((bf16[32,2304]{1,0:T(8,128)(2,1)S(1)}, bf16[32,2304]{1,0:T(8,128)(2,1)S(1)}, u32[]{:S(2)}, u32[]{:S(2)}) %collective-permute-start.35) | collective-permute-done | bytes 147488 | tf_op jit(solution)/shard_map/ppermute | solution.py:554
  81.3 2.5 %collective-permute-done.36.refs_2_ = bf16[32,2304]{1,0:T(8,128)(2,1)S(1)} collective-permute-done((bf16[32,2304]{1,0:T(8,128)(2,1)S(1)}, bf16[32,2304]{1,0:T(8,128)(2,1)S(1)}, u32[]{:S(2)}, u32[]{:S(2)}) %collective-permute-start.36) | collective-permute-done | bytes 147488 | tf_op jit(solution)/shard_map/ppermute | solution.py:554
  83.8 1.8 %collective-permute-done.37.refs_3_ = bf16[32,2304]{1,0:T(8,128)(2,1)S(1)} collective-permute-done((bf16[32,2304]{1,0:T(8,128)(2,1)S(1)}, bf16[32,2304]{1,0:T(8,128)(2,1)S(1)}, u32[]{:S(2)}, u32[]{:S(2)}) %collective-permute-start.37) | collective-permute-done | bytes 147488 | tf_op jit(solution)/shard_map/ppermute | solution.py:554
  85.6 4.9 %shard_map.149 = (bf16[128,1152]{1,0:T(8,128)(2,1)S(1)}, bf16[128,1152]{1,0:T(8,128)(2,1)S(1)}, bf16[32,2,1152]{2,1,0:T(2,128)(2,1)}) custom-call(s32[4,8]{1,0:T(4,128)S(1)} %get-tuple-element.29.clips, bf16[32,2304]{1,0:T(8,128)(2,1)S(1)} %get-tuple-element.41.refs_0_, bf16[32,2304]{1,0:T(8,128)(2,1)S(1)} %collective-permute-done.35.refs_1_, ...), custom_call_target="tpu_custom_call" | custom-call | tf_op jit(solution)/shard_map/pallas_call | solution.py:365
  90.5 4.6 %all-to-all-start = ((bf16[32,2,1152]{2,1,0:T(2,128)(2,1)}), bf16[32,2,1152]{2,1,0:T(2,128)(2,1)S(1)}, u32[]{:S(2)}, u32[]{:S(2)}) async-start(bf16[32,2,1152]{2,1,0:T(2,128)(2,1)} %get-tuple-element.54), calls=%async_computation | async-start | bytes 294912 | tf_op jit(solution)/shard_map/all_to_all | solution.py:589
  95.2 2.5 %copy-done.1 = bf16[16,144,1152]{2,1,0:T(8,128)(2,1)S(1)} copy-done((bf16[16,144,1152]{2,1,0:T(8,128)(2,1)S(1)}, bf16[16,144,1152]{2,1,0:T(8,128)(2,1)}, u32[]{:S(2)}) %copy-start.1) | copy-done | bytes 5308440
  97.7 1.9 %shard_map.150 = (bf16[128,1152]{1,0:T(8,128)(2,1)}, bf16[128,1152]{1,0:T(8,128)(2,1)}) custom-call(bf16[32,2304]{1,0:T(8,128)(2,1)S(1)} %get-tuple-element.41.refs_0_, bf16[32,2304]{1,0:T(8,128)(2,1)S(1)} %collective-permute-done.35.refs_1_, bf16[32,2304]{1,0:T(8,128)(2,1)S(1)} %collective-permute-done.36.refs_2_, ...), custom_call_target="tpu_custom_call" | custom-call | tf_op jit(solution)/shard_map/pallas_call | solution.py:365
  99.6 4.0 %all-to-all-done = bf16[32,2,1152]{2,1,0:T(2,128)(2,1)S(1)} async-done(((bf16[32,2,1152]{2,1,0:T(2,128)(2,1)}), bf16[32,2,1152]{2,1,0:T(2,128)(2,1)S(1)}, u32[]{:S(2)}, u32[]{:S(2)}) %all-to-all-start) | async-done | bytes 147488 | tf_op jit(solution)/shard_map/all_to_all | solution.py:589
  (81 shorter events, 20.6 us)
Async XLA Ops:
  2.6 7.7 %collective-permute-start.4 = (bf16[144,1152]{1,0:T(8,128)(2,1)S(1)}, bf16[144,1152]{1,0:T(8,128)(2,1)S(1)}, u32[]{:S(2)}, u32[]{:S(2)}) collective-permute-start(bf16[144,1152]{1,0:T(8,128)(2,1)S(1)} %get-tuple-element.56.refs_0_), channel_id=1, source_target_pairs={{0,4},{1,3},{4,8},{5,1},{8,12},{9,5},{12,14},{13,9},{14,10},{15,13... | collective-permute-start | bytes 995336 | tf_op jit(solution)/shard_map/ppermute | solution.py:392
  5.2 8.6 %collective-permute-start.1 = (bf16[144,1152]{1,0:T(8,128)(2,1)S(1)}, bf16[144,1152]{1,0:T(8,128)(2,1)S(1)}, u32[]{:S(2)}, u32[]{:S(2)}) collective-permute-start(bf16[144,1152]{1,0:T(8,128)(2,1)S(1)} %collective-permute-done.refs_1_), channel_id=1, source_target_pairs={{0,4},{1,3},{4,8},{5,1},{8,12},{9,5},{12,14},{13,9},{14,10},{15,13... | collective-permute-start | bytes 995336 | tf_op jit(solution)/shard_map/ppermute | solution.py:392
  6.8 7.0 %collective-permute-start.7 = (bf16[144,1152]{1,0:T(8,128)(2,1)S(1)}, bf16[144,1152]{1,0:T(8,128)(2,1)S(1)}, u32[]{:S(2)}, u32[]{:S(2)}) collective-permute-start(bf16[144,1152]{1,0:T(8,128)(2,1)S(1)} %get-tuple-element.55.refs_16_), channel_id=1, source_target_pairs={{0,1},{1,0},{2,3},{3,2},{4,5},{5,4},{6,7},{7,6},{8,9},{9,8},{10,11... | collective-permute-start | bytes 995336 | tf_op jit(solution)/shard_map/ppermute | solution.py:398
  10.3 5.6 %collective-permute-start.6 = (bf16[144,1152]{1,0:T(8,128)(2,1)S(1)}, bf16[144,1152]{1,0:T(8,128)(2,1)S(1)}, u32[]{:S(2)}, u32[]{:S(2)}) collective-permute-start(bf16[144,1152]{1,0:T(8,128)(2,1)S(1)} %collective-permute-done.4.refs_2_), channel_id=1, source_target_pairs={{0,1},{1,0},{2,3},{3,2},{4,5},{5,4},{6,7},{7,6},{8,9},{9,8},{10,11... | collective-permute-start | bytes 995336 | tf_op jit(solution)/shard_map/ppermute | solution.py:398
  10.3 7.1 %collective-permute-start.5 = (bf16[144,1152]{1,0:T(8,128)(2,1)S(1)}, bf16[144,1152]{1,0:T(8,128)(2,1)S(1)}, u32[]{:S(2)}, u32[]{:S(2)}) collective-permute-start(bf16[144,1152]{1,0:T(8,128)(2,1)S(1)} %collective-permute-done.4.refs_2_), channel_id=1, source_target_pairs={{0,4},{1,3},{4,8},{5,1},{8,12},{9,5},{12,14},{13,9},{14,10},{15,13... | collective-permute-start | bytes 995336 | tf_op jit(solution)/shard_map/ppermute | solution.py:392
  12.4 10.1 %collective-permute-start.10 = (bf16[144,1152]{1,0:T(8,128)(2,1)S(1)}, bf16[144,1152]{1,0:T(8,128)(2,1)S(1)}, u32[]{:S(2)}, u32[]{:S(2)}) collective-permute-start(bf16[144,1152]{1,0:T(8,128)(2,1)S(1)} %collective-permute-done.4.refs_2_), channel_id=1, source_target_pairs={{0,16},{16,0},{1,17},{17,1},{2,18},{18,2},{3,19},{19,3},{4,20},{20... | collective-permute-start | bytes 995336 | tf_op jit(solution)/shard_map/ppermute | solution.py:395
  13.8 8.6 %collective-permute-start.8 = (bf16[144,1152]{1,0:T(8,128)(2,1)S(1)}, bf16[144,1152]{1,0:T(8,128)(2,1)S(1)}, u32[]{:S(2)}, u32[]{:S(2)}) collective-permute-start(bf16[144,1152]{1,0:T(8,128)(2,1)S(1)} %collective-permute-done.1.refs_1_.refs_6_), channel_id=1, source_target_pairs={{0,1},{1,0},{2,3},{3,2},{4,5},{5,4},{6,7},{7,6},{8,9},{9,8},{10,11... | collective-permute-start | bytes 995336 | tf_op jit(solution)/shard_map/ppermute | solution.py:398
  13.9 8.6 %collective-permute-start.3 = (bf16[144,1152]{1,0:T(8,128)(2,1)S(1)}, bf16[144,1152]{1,0:T(8,128)(2,1)S(1)}, u32[]{:S(2)}, u32[]{:S(2)}) collective-permute-start(bf16[144,1152]{1,0:T(8,128)(2,1)S(1)} %collective-permute-done.1.refs_1_.refs_6_), channel_id=1, source_target_pairs={{0,4},{1,3},{4,8},{5,1},{8,12},{9,5},{12,14},{13,9},{14,10},{15,13... | collective-permute-start | bytes 995336 | tf_op jit(solution)/shard_map/ppermute | solution.py:392
  17.4 7.2 %collective-permute-start.13 = (bf16[144,1152]{1,0:T(8,128)(2,1)S(1)}, bf16[144,1152]{1,0:T(8,128)(2,1)S(1)}, u32[]{:S(2)}, u32[]{:S(2)}) collective-permute-start(bf16[144,1152]{1,0:T(8,128)(2,1)S(1)} %shard_map.139.refs_1_.refs_3_), channel_id=1, source_target_pairs={{0,4},{1,3},{4,8},{5,1},{8,12},{9,5},{12,14},{13,9},{14,10},{15,13... | collective-permute-start | bytes 995336 | tf_op jit(solution)/shard_map/ppermute | solution.py:392
  20.9 9.1 %collective-permute-start.2 = (bf16[144,1152]{1,0:T(8,128)(2,1)S(1)}, bf16[144,1152]{1,0:T(8,128)(2,1)S(1)}, u32[]{:S(2)}, u32[]{:S(2)}) collective-permute-start(bf16[144,1152]{1,0:T(8,128)(2,1)S(1)} %collective-permute-done.1.refs_1_.refs_6_), channel_id=1, source_target_pairs={{0,16},{16,0},{1,17},{17,1},{2,18},{18,2},{3,19},{19,3},{4,20},{20... | collective-permute-start | bytes 995336 | tf_op jit(solution)/shard_map/ppermute | solution.py:395
  22.5 9.0 %collective-permute-start.12 = (bf16[144,1152]{1,0:T(8,128)(2,1)S(1)}, bf16[144,1152]{1,0:T(8,128)(2,1)S(1)}, u32[]{:S(2)}, u32[]{:S(2)}) collective-permute-start(bf16[144,1152]{1,0:T(8,128)(2,1)S(1)} %shard_map.140.refs_1_.refs_7_), channel_id=1, source_target_pairs={{0,1},{1,0},{2,3},{3,2},{4,5},{5,4},{6,7},{7,6},{8,9},{9,8},{10,11... | collective-permute-start | bytes 995336 | tf_op jit(solution)/shard_map/ppermute | solution.py:398
  23.0 8.5 %collective-permute-start.9 = (bf16[144,1152]{1,0:T(8,128)(2,1)S(1)}, bf16[144,1152]{1,0:T(8,128)(2,1)S(1)}, u32[]{:S(2)}, u32[]{:S(2)}) collective-permute-start(bf16[144,1152]{1,0:T(8,128)(2,1)S(1)} %shard_map.140.refs_1_.refs_7_), channel_id=1, source_target_pairs={{0,4},{1,3},{4,8},{5,1},{8,12},{9,5},{12,14},{13,9},{14,10},{15,13... | collective-permute-start | bytes 995336 | tf_op jit(solution)/shard_map/ppermute | solution.py:392
  24.6 9.1 %collective-permute-start.14 = (bf16[144,1152]{1,0:T(8,128)(2,1)S(1)}, bf16[144,1152]{1,0:T(8,128)(2,1)S(1)}, u32[]{:S(2)}, u32[]{:S(2)}) collective-permute-start(bf16[144,1152]{1,0:T(8,128)(2,1)S(1)} %shard_map.142.refs_4_), channel_id=1, source_target_pairs={{0,4},{1,3},{4,8},{5,1},{8,12},{9,5},{12,14},{13,9},{14,10},{15,13... | collective-permute-start | bytes 995336 | tf_op jit(solution)/shard_map/ppermute | solution.py:392
  26.7 10.5 %collective-permute-start.19 = (bf16[144,1152]{1,0:T(8,128)(2,1)S(1)}, bf16[144,1152]{1,0:T(8,128)(2,1)S(1)}, u32[]{:S(2)}, u32[]{:S(2)}) collective-permute-start(bf16[144,1152]{1,0:T(8,128)(2,1)S(1)} %collective-permute-done.10.refs_2_.refs_18_), channel_id=1, source_target_pairs={{0,4},{1,3},{4,8},{5,1},{8,12},{9,5},{12,14},{13,9},{14,10},{15,13... | collective-permute-start | bytes 995336 | tf_op jit(solution)/shard_map/ppermute | solution.py:392
  30.0 8.1 %collective-permute-start.20 = (bf16[144,1152]{1,0:T(8,128)(2,1)S(1)}, bf16[144,1152]{1,0:T(8,128)(2,1)S(1)}, u32[]{:S(2)}, u32[]{:S(2)}) collective-permute-start(bf16[144,1152]{1,0:T(8,128)(2,1)S(1)} %shard_map.142.refs_4_), channel_id=1, source_target_pairs={{0,16},{16,0},{1,17},{17,1},{2,18},{18,2},{3,19},{19,3},{4,20},{20... | collective-permute-start | bytes 995336 | tf_op jit(solution)/shard_map/ppermute | solution.py:395
  31.5 6.6 %collective-permute-start.18 = (bf16[144,1152]{1,0:T(8,128)(2,1)S(1)}, bf16[144,1152]{1,0:T(8,128)(2,1)S(1)}, u32[]{:S(2)}, u32[]{:S(2)}) collective-permute-start(bf16[144,1152]{1,0:T(8,128)(2,1)S(1)} %collective-permute-done.9.refs_4_.refs_2_.refs_8_), channel_id=1, source_target_pairs={{0,1},{1,0},{2,3},{3,2},{4,5},{5,4},{6,7},{7,6},{8,9},{9,8},{10,11... | collective-permute-start | bytes 995336 | tf_op jit(solution)/shard_map/ppermute | solution.py:398
  33.6 4.9 %collective-permute-start.17 = (bf16[144,1152]{1,0:T(8,128)(2,1)S(1)}, bf16[144,1152]{1,0:T(8,128)(2,1)S(1)}, u32[]{:S(2)}, u32[]{:S(2)}) collective-permute-start(bf16[144,1152]{1,0:T(8,128)(2,1)S(1)} %shard_map.143.refs_5_), channel_id=1, source_target_pairs={{0,1},{1,0},{2,3},{3,2},{4,5},{5,4},{6,7},{7,6},{8,9},{9,8},{10,11... | collective-permute-start | bytes 995336 | tf_op jit(solution)/shard_map/ppermute | solution.py:398
  33.6 7.1 %collective-permute-start.22 = (bf16[144,1152]{1,0:T(8,128)(2,1)S(1)}, bf16[144,1152]{1,0:T(8,128)(2,1)S(1)}, u32[]{:S(2)}, u32[]{:S(2)}) collective-permute-start(bf16[144,1152]{1,0:T(8,128)(2,1)S(1)} %get-tuple-element.32.refs_1_.refs_22_), channel_id=1, source_target_pairs={{0,4},{1,3},{4,8},{5,1},{8,12},{9,5},{12,14},{13,9},{14,10},{15,13... | collective-permute-start | bytes 995336 | tf_op jit(solution)/shard_map/ppermute | solution.py:392
  37.2 5.1 %collective-permute-start.15 = (bf16[144,1152]{1,0:T(8,128)(2,1)S(1)}, bf16[144,1152]{1,0:T(8,128)(2,1)S(1)}, u32[]{:S(2)}, u32[]{:S(2)}) collective-permute-start(bf16[144,1152]{1,0:T(8,128)(2,1)S(1)} %shard_map.139.refs_1_.refs_3_), channel_id=1, source_target_pairs={{0,1},{1,0},{2,3},{3,2},{4,5},{5,4},{6,7},{7,6},{8,9},{9,8},{10,11... | collective-permute-start | bytes 995336 | tf_op jit(solution)/shard_map/ppermute | solution.py:398
  38.1 4.8 %collective-permute-start.16 = (bf16[144,1152]{1,0:T(8,128)(2,1)S(1)}, bf16[144,1152]{1,0:T(8,128)(2,1)S(1)}, u32[]{:S(2)}, u32[]{:S(2)}) collective-permute-start(bf16[144,1152]{1,0:T(8,128)(2,1)S(1)} %shard_map.142.refs_4_), channel_id=1, source_target_pairs={{0,1},{1,0},{2,3},{3,2},{4,5},{5,4},{6,7},{7,6},{8,9},{9,8},{10,11... | collective-permute-start | bytes 995336 | tf_op jit(solution)/shard_map/ppermute | solution.py:398
  38.6 9.8 %collective-permute-start.21 = (bf16[144,1152]{1,0:T(8,128)(2,1)S(1)}, bf16[144,1152]{1,0:T(8,128)(2,1)S(1)}, u32[]{:S(2)}, u32[]{:S(2)}) collective-permute-start(bf16[144,1152]{1,0:T(8,128)(2,1)S(1)} %shard_map.143.refs_5_), channel_id=1, source_target_pairs={{0,16},{16,0},{1,17},{17,1},{2,18},{18,2},{3,19},{19,3},{4,20},{20... | collective-permute-start | bytes 995336 | tf_op jit(solution)/shard_map/ppermute | solution.py:395
  40.8 7.6 %collective-permute-start.23 = (bf16[144,1152]{1,0:T(8,128)(2,1)S(1)}, bf16[144,1152]{1,0:T(8,128)(2,1)S(1)}, u32[]{:S(2)}, u32[]{:S(2)}) collective-permute-start(bf16[144,1152]{1,0:T(8,128)(2,1)S(1)} %shard_map.144.refs_23_), channel_id=1, source_target_pairs={{0,4},{1,3},{4,8},{5,1},{8,12},{9,5},{12,14},{13,9},{14,10},{15,13... | collective-permute-start | bytes 995336 | tf_op jit(solution)/shard_map/ppermute | solution.py:392
  42.3 6.5 %collective-permute-start.27 = (bf16[144,1152]{1,0:T(8,128)(2,1)S(1)}, bf16[144,1152]{1,0:T(8,128)(2,1)S(1)}, u32[]{:S(2)}, u32[]{:S(2)}) collective-permute-start(bf16[144,1152]{1,0:T(8,128)(2,1)S(1)} %get-tuple-element.32.refs_1_.refs_22_), channel_id=1, source_target_pairs={{0,1},{1,0},{2,3},{3,2},{4,5},{5,4},{6,7},{7,6},{8,9},{9,8},{10,11... | collective-permute-start | bytes 995336 | tf_op jit(solution)/shard_map/ppermute | solution.py:398
  42.4 6.4 %collective-permute-start.25 = (bf16[144,1152]{1,0:T(8,128)(2,1)S(1)}, bf16[144,1152]{1,0:T(8,128)(2,1)S(1)}, u32[]{:S(2)}, u32[]{:S(2)}) collective-permute-start(bf16[144,1152]{1,0:T(8,128)(2,1)S(1)} %collective-permute-done.20.refs_3_.refs_20_), channel_id=1, source_target_pairs={{0,1},{1,0},{2,3},{3,2},{4,5},{5,4},{6,7},{7,6},{8,9},{9,8},{10,11... | collective-permute-start | bytes 995336 | tf_op jit(solution)/shard_map/ppermute | solution.py:398
  42.9 7.1 %collective-permute-start.28 = (bf16[144,1152]{1,0:T(8,128)(2,1)S(1)}, bf16[144,1152]{1,0:T(8,128)(2,1)S(1)}, u32[]{:S(2)}, u32[]{:S(2)}) collective-permute-start(bf16[144,1152]{1,0:T(8,128)(2,1)S(1)} %shard_map.144.refs_23_), channel_id=1, source_target_pairs={{0,1},{1,0},{2,3},{3,2},{4,5},{5,4},{6,7},{7,6},{8,9},{9,8},{10,11... | collective-permute-start | bytes 995336 | tf_op jit(solution)/shard_map/ppermute | solution.py:398
  59.6 7.5 %collective-permute-start.31 = (bf16[32,2304]{1,0:T(8,128)(2,1)S(1)}, bf16[32,2304]{1,0:T(8,128)(2,1)S(1)}, u32[]{:S(2)}, u32[]{:S(2)}) collective-permute-start(bf16[32,2304]{1,0:T(8,128)(2,1)S(1)} %get-tuple-element.36), channel_id=1, source_target_pairs={{0,2},{1,3},{2,0},{3,1},{4,6},{5,7},{6,4},{7,5},{8,10},{9,11},{10,... | collective-permute-start | bytes 442376 | tf_op jit(solution)/shard_map/ppermute | solution.py:554
  62.9 6.7 %collective-permute-start.32 = (bf16[32,2304]{1,0:T(8,128)(2,1)S(1)}, bf16[32,2304]{1,0:T(8,128)(2,1)S(1)}, u32[]{:S(2)}, u32[]{:S(2)}) collective-permute-start(bf16[32,2304]{1,0:T(8,128)(2,1)S(1)} %get-tuple-element.37), channel_id=1, source_target_pairs={{0,4},{1,5},{2,6},{3,7},{4,0},{5,1},{6,2},{7,3},{8,12},{9,13},{10,... | collective-permute-start | bytes 442376 | tf_op jit(solution)/shard_map/ppermute | solution.py:554
  64.1 7.4 %collective-permute-start.33 = (bf16[32,2304]{1,0:T(8,128)(2,1)S(1)}, bf16[32,2304]{1,0:T(8,128)(2,1)S(1)}, u32[]{:S(2)}, u32[]{:S(2)}) collective-permute-start(bf16[32,2304]{1,0:T(8,128)(2,1)S(1)} %get-tuple-element.38), channel_id=1, source_target_pairs={{0,6},{1,7},{2,4},{3,5},{4,2},{5,3},{6,0},{7,1},{8,14},{9,15},{10,... | collective-permute-start | bytes 442376 | tf_op jit(solution)/shard_map/ppermute | solution.py:554
  75.3 6.0 %collective-permute-start.35 = (bf16[32,2304]{1,0:T(8,128)(2,1)S(1)}, bf16[32,2304]{1,0:T(8,128)(2,1)S(1)}, u32[]{:S(2)}, u32[]{:S(2)}) collective-permute-start(bf16[32,2304]{1,0:T(8,128)(2,1)S(1)} %get-tuple-element.42), channel_id=1, source_target_pairs={{0,2},{1,3},{2,0},{3,1},{4,6},{5,7},{6,4},{7,5},{8,10},{9,11},{10,... | collective-permute-start | bytes 442376 | tf_op jit(solution)/shard_map/ppermute | solution.py:554
  77.1 6.7 %collective-permute-start.36 = (bf16[32,2304]{1,0:T(8,128)(2,1)S(1)}, bf16[32,2304]{1,0:T(8,128)(2,1)S(1)}, u32[]{:S(2)}, u32[]{:S(2)}) collective-permute-start(bf16[32,2304]{1,0:T(8,128)(2,1)S(1)} %get-tuple-element.43), channel_id=1, source_target_pairs={{0,4},{1,5},{2,6},{3,7},{4,0},{5,1},{6,2},{7,3},{8,12},{9,13},{10,... | collective-permute-start | bytes 442376 | tf_op jit(solution)/shard_map/ppermute | solution.py:554
  78.3 7.4 %collective-permute-start.37 = (bf16[32,2304]{1,0:T(8,128)(2,1)S(1)}, bf16[32,2304]{1,0:T(8,128)(2,1)S(1)}, u32[]{:S(2)}, u32[]{:S(2)}) collective-permute-start(bf16[32,2304]{1,0:T(8,128)(2,1)S(1)} %get-tuple-element.44), channel_id=1, source_target_pairs={{0,6},{1,7},{2,4},{3,5},{4,2},{5,3},{6,0},{7,1},{8,14},{9,15},{10,... | collective-permute-start | bytes 442376 | tf_op jit(solution)/shard_map/ppermute | solution.py:554
  90.5 13.0 %all-to-all-start = ((bf16[32,2,1152]{2,1,0:T(2,128)(2,1)}), bf16[32,2,1152]{2,1,0:T(2,128)(2,1)S(1)}, u32[]{:S(2)}, u32[]{:S(2)}) async-start(bf16[32,2,1152]{2,1,0:T(2,128)(2,1)} %get-tuple-element.54), calls=%async_computation | async-start | bytes 294912 | tf_op jit(solution)/shard_map/all_to_all | solution.py:589
  (15 other events, 209.7 us)

commit v5 on v4

--- a/solution.py
+++ b/solution.py
@@ -433,8 +433,8 @@
     x_o2_twin = twin(x_o2)
     x_t2_twin = twin(x_t2)
     x_o3_twin = twin(x_o3)
+    x_t3_twin = twin(x_t3)
     x_o4_twin = twin(x_o4)
-    x_t3_twin = twin(x_t3)
     mine = {"o0": (own, 0), "t0": (t0, 0)}
     other = {"o0": (own_other, 0), "t0": (t0_other, 0)}
     mine |= {"o1": (o1, 0), "o1_twin": (o1_twin, 0)}

time: 105 us -> 105 us (level)
  no operation moved by 1% of the time
where the time goes in v5:
time: 105 us; the launch traced here: 104 us
  starting transfers between devices  40.8 us (39%)
  waiting for transfers between devices  40.1 us (38%)
  Pallas kernels  16.5 us (16%)
  local copies, waits for them, and re-layouts  3.93 us (4%)
  other arithmetic  2.2 us (2%)
    ppermute x10, starting transfers between devices, ring(): return lax.ppermute(rows, 'ctx', ring_pairs)  18.8 us
    pallas_call x6, Pallas kernels, call(): pl.pallas_call(body, out_shape=out_shapes, in_specs=[scalars] * len(clips...  16.5 us
    ppermute x6, waiting for transfers between devices, exchange(): lax.ppermute(rows_away, 'ctx', [(index, index ^ 2 * distance) for index i...  13.8 us
    ppermute x10, waiting for transfers between devices, ring(): return lax.ppermute(rows, 'ctx', ring_pairs)  9.79 us
    ppermute x6, starting transfers between devices, exchange(): lax.ppermute(rows_away, 'ctx', [(index, index ^ 2 * distance) for index i...  8.43 us
    ppermute x4, waiting for transfers between devices, across(): lax.ppermute(rows, 'dp', [(index, index ^ 1) for index in range(planes)])  7.9 us
    ppermute x4, starting transfers between devices, across(): lax.ppermute(rows, 'dp', [(index, index ^ 1) for index in range(planes)])  6.03 us
    all_to_all x1, starting transfers between devices, shards(): lax.all_to_all(gains, ('dp', 'ctx'), split_axis=0, concat_axis=0, tiled=T...  4.61 us
  transfers between devices with their start and end apart: 39, of which 19 were waited for; matrix products, arithmetic and copies ran while one was open for 1% of the time, Pallas kernels for 2%

profile of v5, /device:TPU:0, one launch (start us, length us, event | category | flops | bytes accessed | tf_op | source)
XLA Modules:
  0.0 104.3 jit_solution(16443544875144138829)
XLA Ops:
  2.6 2.6 %collective-permute-start.4 = (bf16[144,1152]{1,0:T(8,128)(2,1)S(1)}, bf16[144,1152]{1,0:T(8,128)(2,1)S(1)}, u32[]{:S(2)}, u32[]{:S(2)}) collective-permute-start(bf16[144,1152]{1,0:T(8,128)(2,1)S(1)} %get-tuple-element.56.refs_0_), channel_id=1, source_target_pairs={{0,4},{1,3},{4,8},{5,1},{8,12},{9,5},{12,14},{13,9},{14,10},{15,13... | collective-permute-start | bytes 995336 | tf_op jit(solution)/shard_map/ppermute | solution.py:392
  5.2 1.6 %collective-permute-start.1 = (bf16[144,1152]{1,0:T(8,128)(2,1)S(1)}, bf16[144,1152]{1,0:T(8,128)(2,1)S(1)}, u32[]{:S(2)}, u32[]{:S(2)}) collective-permute-start(bf16[144,1152]{1,0:T(8,128)(2,1)S(1)} %collective-permute-done.refs_1_), channel_id=1, source_target_pairs={{0,4},{1,3},{4,8},{5,1},{8,12},{9,5},{12,14},{13,9},{14,10},{15,13... | collective-permute-start | bytes 995336 | tf_op jit(solution)/shard_map/ppermute | solution.py:392
  6.8 3.5 %collective-permute-done.4.refs_2_ = bf16[144,1152]{1,0:T(8,128)(2,1)S(1)} collective-permute-done((bf16[144,1152]{1,0:T(8,128)(2,1)S(1)}, bf16[144,1152]{1,0:T(8,128)(2,1)S(1)}, u32[]{:S(2)}, u32[]{:S(2)}) %collective-permute-start.4) | collective-permute-done | bytes 331808 | tf_op jit(solution)/shard_map/ppermute | solution.py:392
  10.3 2.1 %collective-permute-start.5 = (bf16[144,1152]{1,0:T(8,128)(2,1)S(1)}, bf16[144,1152]{1,0:T(8,128)(2,1)S(1)}, u32[]{:S(2)}, u32[]{:S(2)}) collective-permute-start(bf16[144,1152]{1,0:T(8,128)(2,1)S(1)} %collective-permute-done.4.refs_2_), channel_id=1, source_target_pairs={{0,4},{1,3},{4,8},{5,1},{8,12},{9,5},{12,14},{13,9},{14,10},{15,13... | collective-permute-start | bytes 995336 | tf_op jit(solution)/shard_map/ppermute | solution.py:392
  13.9 2.1 %collective-permute-start.3 = (bf16[144,1152]{1,0:T(8,128)(2,1)S(1)}, bf16[144,1152]{1,0:T(8,128)(2,1)S(1)}, u32[]{:S(2)}, u32[]{:S(2)}) collective-permute-start(bf16[144,1152]{1,0:T(8,128)(2,1)S(1)} %collective-permute-done.1.refs_1_.refs_6_), channel_id=1, source_target_pairs={{0,4},{1,3},{4,8},{5,1},{8,12},{9,5},{12,14},{13,9},{14,10},{15,13... | collective-permute-start | bytes 995336 | tf_op jit(solution)/shard_map/ppermute | solution.py:392
  17.4 2.1 %collective-permute-start.13 = (bf16[144,1152]{1,0:T(8,128)(2,1)S(1)}, bf16[144,1152]{1,0:T(8,128)(2,1)S(1)}, u32[]{:S(2)}, u32[]{:S(2)}) collective-permute-start(bf16[144,1152]{1,0:T(8,128)(2,1)S(1)} %shard_map.139.refs_1_.refs_3_), channel_id=1, source_target_pairs={{0,4},{1,3},{4,8},{5,1},{8,12},{9,5},{12,14},{13,9},{14,10},{15,13... | collective-permute-start | bytes 995336 | tf_op jit(solution)/shard_map/ppermute | solution.py:392
  20.9 1.6 %collective-permute-start.2 = (bf16[144,1152]{1,0:T(8,128)(2,1)S(1)}, bf16[144,1152]{1,0:T(8,128)(2,1)S(1)}, u32[]{:S(2)}, u32[]{:S(2)}) collective-permute-start(bf16[144,1152]{1,0:T(8,128)(2,1)S(1)} %collective-permute-done.1.refs_1_.refs_6_), channel_id=1, source_target_pairs={{0,16},{16,0},{1,17},{17,1},{2,18},{18,2},{3,19},{19,3},{4,20},{20... | collective-permute-start | bytes 995336 | tf_op jit(solution)/shard_map/ppermute | solution.py:395
  23.0 1.6 %collective-permute-start.9 = (bf16[144,1152]{1,0:T(8,128)(2,1)S(1)}, bf16[144,1152]{1,0:T(8,128)(2,1)S(1)}, u32[]{:S(2)}, u32[]{:S(2)}) collective-permute-start(bf16[144,1152]{1,0:T(8,128)(2,1)S(1)} %shard_map.140.refs_1_.refs_7_), channel_id=1, source_target_pairs={{0,4},{1,3},{4,8},{5,1},{8,12},{9,5},{12,14},{13,9},{14,10},{15,13... | collective-permute-start | bytes 995336 | tf_op jit(solution)/shard_map/ppermute | solution.py:392
  24.6 2.0 %collective-permute-start.14 = (bf16[144,1152]{1,0:T(8,128)(2,1)S(1)}, bf16[144,1152]{1,0:T(8,128)(2,1)S(1)}, u32[]{:S(2)}, u32[]{:S(2)}) collective-permute-start(bf16[144,1152]{1,0:T(8,128)(2,1)S(1)} %shard_map.142.refs_4_), channel_id=1, source_target_pairs={{0,4},{1,3},{4,8},{5,1},{8,12},{9,5},{12,14},{13,9},{14,10},{15,13... | collective-permute-start | bytes 995336 | tf_op jit(solution)/shard_map/ppermute | solution.py:392
  26.7 1.6 %collective-permute-start.19 = (bf16[144,1152]{1,0:T(8,128)(2,1)S(1)}, bf16[144,1152]{1,0:T(8,128)(2,1)S(1)}, u32[]{:S(2)}, u32[]{:S(2)}) collective-permute-start(bf16[144,1152]{1,0:T(8,128)(2,1)S(1)} %collective-permute-done.10.refs_2_.refs_18_), channel_id=1, source_target_pairs={{0,4},{1,3},{4,8},{5,1},{8,12},{9,5},{12,14},{13,9},{14,10},{15,13... | collective-permute-start | bytes 995336 | tf_op jit(solution)/shard_map/ppermute | solution.py:392
  28.4 1.6 %collective-permute-done.2.refs_0_ = bf16[144,1152]{1,0:T(8,128)(2,1)S(1)} collective-permute-done((bf16[144,1152]{1,0:T(8,128)(2,1)S(1)}, bf16[144,1152]{1,0:T(8,128)(2,1)S(1)}, u32[]{:S(2)}, u32[]{:S(2)}) %collective-permute-start.2) | collective-permute-done | bytes 331808 | tf_op jit(solution)/shard_map/ppermute | solution.py:395
  31.5 2.2 %collective-permute-done.14.refs_0_ = bf16[144,1152]{1,0:T(8,128)(2,1)S(1)} collective-permute-done((bf16[144,1152]{1,0:T(8,128)(2,1)S(1)}, bf16[144,1152]{1,0:T(8,128)(2,1)S(1)}, u32[]{:S(2)}, u32[]{:S(2)}) %collective-permute-start.14) | collective-permute-done | bytes 331808 | tf_op jit(solution)/shard_map/ppermute | solution.py:392
  33.6 1.6 %collective-permute-start.22 = (bf16[144,1152]{1,0:T(8,128)(2,1)S(1)}, bf16[144,1152]{1,0:T(8,128)(2,1)S(1)}, u32[]{:S(2)}, u32[]{:S(2)}) collective-permute-start(bf16[144,1152]{1,0:T(8,128)(2,1)S(1)} %get-tuple-element.32.refs_1_.refs_22_), channel_id=1, source_target_pairs={{0,4},{1,3},{4,8},{5,1},{8,12},{9,5},{12,14},{13,9},{14,10},{15,13... | collective-permute-start | bytes 995336 | tf_op jit(solution)/shard_map/ppermute | solution.py:392
  35.2 2.0 %collective-permute-done.19.refs_4_.refs_19_ = bf16[144,1152]{1,0:T(8,128)(2,1)S(1)} collective-permute-done((bf16[144,1152]{1,0:T(8,128)(2,1)S(1)}, bf16[144,1152]{1,0:T(8,128)(2,1)S(1)}, u32[]{:S(2)}, u32[]{:S(2)}) %collective-permute-start.19) | collective-permute-done | bytes 331808 | tf_op jit(solution)/shard_map/ppermute | solution.py:392
  40.8 1.6 %collective-permute-start.23 = (bf16[144,1152]{1,0:T(8,128)(2,1)S(1)}, bf16[144,1152]{1,0:T(8,128)(2,1)S(1)}, u32[]{:S(2)}, u32[]{:S(2)}) collective-permute-start(bf16[144,1152]{1,0:T(8,128)(2,1)S(1)} %shard_map.144.refs_23_), channel_id=1, source_target_pairs={{0,4},{1,3},{4,8},{5,1},{8,12},{9,5},{12,14},{13,9},{14,10},{15,13... | collective-permute-start | bytes 995336 | tf_op jit(solution)/shard_map/ppermute | solution.py:392
  43.0 5.4 %collective-permute-done.21.refs_21_ = bf16[144,1152]{1,0:T(8,128)(2,1)S(1)} collective-permute-done((bf16[144,1152]{1,0:T(8,128)(2,1)S(1)}, bf16[144,1152]{1,0:T(8,128)(2,1)S(1)}, u32[]{:S(2)}, u32[]{:S(2)}) %collective-permute-start.21) | collective-permute-done | bytes 331808 | tf_op jit(solution)/shard_map/ppermute | solution.py:395
  50.5 7.4 %shard_map.145 = (bf16[128,1152]{1,0:T(8,128)(2,1)S(1)}, f32[1792,128]{1,0:T(8,128)S(1)}, bf16[8,128,128]{2,1,0:T(8,128)(2,1)S(1)}, bf16[16,144,1152]{2,1,0:T(8,...) custom-call(s32[4,8]{1,0:T(4,128)S(1)} %get-tuple-element.29.clips, ...), custom_call_target="tpu_custom_call" | custom-call | tf_op jit(solution)/shard_map/pallas_call | solution.py:365
  59.6 3.3 %collective-permute-start.31 = (bf16[32,2304]{1,0:T(8,128)(2,1)S(1)}, bf16[32,2304]{1,0:T(8,128)(2,1)S(1)}, u32[]{:S(2)}, u32[]{:S(2)}) collective-permute-start(bf16[32,2304]{1,0:T(8,128)(2,1)S(1)} %get-tuple-element.36), channel_id=1, source_target_pairs={{0,2},{1,3},{2,0},{3,1},{4,6},{5,7},{6,4},{7,5},{8,10},{9,11},{10,... | collective-permute-start | bytes 442376 | tf_op jit(solution)/shard_map/ppermute | solution.py:554
  64.4 2.6 %collective-permute-done.31.refs_1_ = bf16[32,2304]{1,0:T(8,128)(2,1)S(1)} collective-permute-done((bf16[32,2304]{1,0:T(8,128)(2,1)S(1)}, bf16[32,2304]{1,0:T(8,128)(2,1)S(1)}, u32[]{:S(2)}, u32[]{:S(2)}) %collective-permute-start.31) | collective-permute-done | bytes 147488 | tf_op jit(solution)/shard_map/ppermute | solution.py:554
  67.1 2.6 %collective-permute-done.32.refs_2_ = bf16[32,2304]{1,0:T(8,128)(2,1)S(1)} collective-permute-done((bf16[32,2304]{1,0:T(8,128)(2,1)S(1)}, bf16[32,2304]{1,0:T(8,128)(2,1)S(1)}, u32[]{:S(2)}, u32[]{:S(2)}) %collective-permute-start.32) | collective-permute-done | bytes 147488 | tf_op jit(solution)/shard_map/ppermute | solution.py:554
  69.6 1.8 %collective-permute-done.33.refs_3_ = bf16[32,2304]{1,0:T(8,128)(2,1)S(1)} collective-permute-done((bf16[32,2304]{1,0:T(8,128)(2,1)S(1)}, bf16[32,2304]{1,0:T(8,128)(2,1)S(1)}, u32[]{:S(2)}, u32[]{:S(2)}) %collective-permute-start.33) | collective-permute-done | bytes 147488 | tf_op jit(solution)/shard_map/ppermute | solution.py:554
  71.5 2.2 %shard_map.147 = (bf16[64,2304]{1,0:T(8,128)(2,1)S(1)}, bf16[64,2304]{1,0:T(8,128)(2,1)S(1)}) custom-call(s32[4,8]{1,0:T(4,128)S(1)} %get-tuple-element.29.clips, bf16[32,2304]{1,0:T(8,128)(2,1)S(1)} %get-tuple-element.35.refs_0_, bf16[32,2304]{1,0:T(8,128)(2,1)S(1)} %collective-permute-done.31.refs_1_, ...), custom_call_target="tpu_custom_call" | custom-call | tf_op jit(solution)/shard_map/pallas_call | solution.py:365
  73.7 1.6 %collective-permute-done.34.from_twin = bf16[64,2304]{1,0:T(8,128)(2,1)S(1)} collective-permute-done((bf16[64,2304]{1,0:T(8,128)(2,1)S(1)}, bf16[64,2304]{1,0:T(8,128)(2,1)S(1)}, u32[]{:S(2)}, u32[]{:S(2)}) %collective-permute-start.34) | collective-permute-done | bytes 294944 | tf_op jit(solution)/shard_map/ppermute | solution.py:548
  75.3 1.7 %collective-permute-start.35 = (bf16[32,2304]{1,0:T(8,128)(2,1)S(1)}, bf16[32,2304]{1,0:T(8,128)(2,1)S(1)}, u32[]{:S(2)}, u32[]{:S(2)}) collective-permute-start(bf16[32,2304]{1,0:T(8,128)(2,1)S(1)} %get-tuple-element.42), channel_id=1, source_target_pairs={{0,2},{1,3},{2,0},{3,1},{4,6},{5,7},{6,4},{7,5},{8,10},{9,11},{10,... | collective-permute-start | bytes 442376 | tf_op jit(solution)/shard_map/ppermute | solution.py:554
  78.9 2.4 %collective-permute-done.35.refs_1_ = bf16[32,2304]{1,0:T(8,128)(2,1)S(1)} collective-permute-done((bf16[32,2304]{1,0:T(8,128)(2,1)S(1)}, bf16[32,2304]{1,0:T(8,128)(2,1)S(1)}, u32[]{:S(2)}, u32[]{:S(2)}) %collective-permute-start.35) | collective-permute-done | bytes 147488 | tf_op jit(solution)/shard_map/ppermute | solution.py:554
  81.3 2.5 %collective-permute-done.36.refs_2_ = bf16[32,2304]{1,0:T(8,128)(2,1)S(1)} collective-permute-done((bf16[32,2304]{1,0:T(8,128)(2,1)S(1)}, bf16[32,2304]{1,0:T(8,128)(2,1)S(1)}, u32[]{:S(2)}, u32[]{:S(2)}) %collective-permute-start.36) | collective-permute-done | bytes 147488 | tf_op jit(solution)/shard_map/ppermute | solution.py:554
  83.8 1.8 %collective-permute-done.37.refs_3_ = bf16[32,2304]{1,0:T(8,128)(2,1)S(1)} collective-permute-done((bf16[32,2304]{1,0:T(8,128)(2,1)S(1)}, bf16[32,2304]{1,0:T(8,128)(2,1)S(1)}, u32[]{:S(2)}, u32[]{:S(2)}) %collective-permute-start.37) | collective-permute-done | bytes 147488 | tf_op jit(solution)/shard_map/ppermute | solution.py:554
  85.6 4.9 %shard_map.149 = (bf16[128,1152]{1,0:T(8,128)(2,1)S(1)}, bf16[128,1152]{1,0:T(8,128)(2,1)S(1)}, bf16[32,2,1152]{2,1,0:T(2,128)(2,1)}) custom-call(s32[4,8]{1,0:T(4,128)S(1)} %get-tuple-element.29.clips, bf16[32,2304]{1,0:T(8,128)(2,1)S(1)} %get-tuple-element.41.refs_0_, bf16[32,2304]{1,0:T(8,128)(2,1)S(1)} %collective-permute-done.35.refs_1_, ...), custom_call_target="tpu_custom_call" | custom-call | tf_op jit(solution)/shard_map/pallas_call | solution.py:365
  90.5 4.6 %all-to-all-start = ((bf16[32,2,1152]{2,1,0:T(2,128)(2,1)}), bf16[32,2,1152]{2,1,0:T(2,128)(2,1)S(1)}, u32[]{:S(2)}, u32[]{:S(2)}) async-start(bf16[32,2,1152]{2,1,0:T(2,128)(2,1)} %get-tuple-element.54), calls=%async_computation | async-start | bytes 294912 | tf_op jit(solution)/shard_map/all_to_all | solution.py:589
  95.2 2.5 %copy-done.1 = bf16[16,144,1152]{2,1,0:T(8,128)(2,1)S(1)} copy-done((bf16[16,144,1152]{2,1,0:T(8,128)(2,1)S(1)}, bf16[16,144,1152]{2,1,0:T(8,128)(2,1)}, u32[]{:S(2)}) %copy-start.1) | copy-done | bytes 5308440
  97.7 1.9 %shard_map.150 = (bf16[128,1152]{1,0:T(8,128)(2,1)}, bf16[128,1152]{1,0:T(8,128)(2,1)}) custom-call(bf16[32,2304]{1,0:T(8,128)(2,1)S(1)} %get-tuple-element.41.refs_0_, bf16[32,2304]{1,0:T(8,128)(2,1)S(1)} %collective-permute-done.35.refs_1_, bf16[32,2304]{1,0:T(8,128)(2,1)S(1)} %collective-permute-done.36.refs_2_, ...), custom_call_target="tpu_custom_call" | custom-call | tf_op jit(solution)/shard_map/pallas_call | solution.py:365
  99.6 4.0 %all-to-all-done = bf16[32,2,1152]{2,1,0:T(2,128)(2,1)S(1)} async-done(((bf16[32,2,1152]{2,1,0:T(2,128)(2,1)}), bf16[32,2,1152]{2,1,0:T(2,128)(2,1)S(1)}, u32[]{:S(2)}, u32[]{:S(2)}) %all-to-all-start) | async-done | bytes 147488 | tf_op jit(solution)/shard_map/all_to_all | solution.py:589
  (81 shorter events, 20.6 us)
Async XLA Ops:
  2.6 7.7 %collective-permute-start.4 = (bf16[144,1152]{1,0:T(8,128)(2,1)S(1)}, bf16[144,1152]{1,0:T(8,128)(2,1)S(1)}, u32[]{:S(2)}, u32[]{:S(2)}) collective-permute-start(bf16[144,1152]{1,0:T(8,128)(2,1)S(1)} %get-tuple-element.56.refs_0_), channel_id=1, source_target_pairs={{0,4},{1,3},{4,8},{5,1},{8,12},{9,5},{12,14},{13,9},{14,10},{15,13... | collective-permute-start | bytes 995336 | tf_op jit(solution)/shard_map/ppermute | solution.py:392
  5.2 8.6 %collective-permute-start.1 = (bf16[144,1152]{1,0:T(8,128)(2,1)S(1)}, bf16[144,1152]{1,0:T(8,128)(2,1)S(1)}, u32[]{:S(2)}, u32[]{:S(2)}) collective-permute-start(bf16[144,1152]{1,0:T(8,128)(2,1)S(1)} %collective-permute-done.refs_1_), channel_id=1, source_target_pairs={{0,4},{1,3},{4,8},{5,1},{8,12},{9,5},{12,14},{13,9},{14,10},{15,13... | collective-permute-start | bytes 995336 | tf_op jit(solution)/shard_map/ppermute | solution.py:392
  6.8 7.0 %collective-permute-start.7 = (bf16[144,1152]{1,0:T(8,128)(2,1)S(1)}, bf16[144,1152]{1,0:T(8,128)(2,1)S(1)}, u32[]{:S(2)}, u32[]{:S(2)}) collective-permute-start(bf16[144,1152]{1,0:T(8,128)(2,1)S(1)} %get-tuple-element.55.refs_16_), channel_id=1, source_target_pairs={{0,1},{1,0},{2,3},{3,2},{4,5},{5,4},{6,7},{7,6},{8,9},{9,8},{10,11... | collective-permute-start | bytes 995336 | tf_op jit(solution)/shard_map/ppermute | solution.py:398
  10.3 5.6 %collective-permute-start.6 = (bf16[144,1152]{1,0:T(8,128)(2,1)S(1)}, bf16[144,1152]{1,0:T(8,128)(2,1)S(1)}, u32[]{:S(2)}, u32[]{:S(2)}) collective-permute-start(bf16[144,1152]{1,0:T(8,128)(2,1)S(1)} %collective-permute-done.4.refs_2_), channel_id=1, source_target_pairs={{0,1},{1,0},{2,3},{3,2},{4,5},{5,4},{6,7},{7,6},{8,9},{9,8},{10,11... | collective-permute-start | bytes 995336 | tf_op jit(solution)/shard_map/ppermute | solution.py:398
  10.3 7.1 %collective-permute-start.5 = (bf16[144,1152]{1,0:T(8,128)(2,1)S(1)}, bf16[144,1152]{1,0:T(8,128)(2,1)S(1)}, u32[]{:S(2)}, u32[]{:S(2)}) collective-permute-start(bf16[144,1152]{1,0:T(8,128)(2,1)S(1)} %collective-permute-done.4.refs_2_), channel_id=1, source_target_pairs={{0,4},{1,3},{4,8},{5,1},{8,12},{9,5},{12,14},{13,9},{14,10},{15,13... | collective-permute-start | bytes 995336 | tf_op jit(solution)/shard_map/ppermute | solution.py:392
  12.4 10.1 %collective-permute-start.10 = (bf16[144,1152]{1,0:T(8,128)(2,1)S(1)}, bf16[144,1152]{1,0:T(8,128)(2,1)S(1)}, u32[]{:S(2)}, u32[]{:S(2)}) collective-permute-start(bf16[144,1152]{1,0:T(8,128)(2,1)S(1)} %collective-permute-done.4.refs_2_), channel_id=1, source_target_pairs={{0,16},{16,0},{1,17},{17,1},{2,18},{18,2},{3,19},{19,3},{4,20},{20... | collective-permute-start | bytes 995336 | tf_op jit(solution)/shard_map/ppermute | solution.py:395
  13.8 8.6 %collective-permute-start.8 = (bf16[144,1152]{1,0:T(8,128)(2,1)S(1)}, bf16[144,1152]{1,0:T(8,128)(2,1)S(1)}, u32[]{:S(2)}, u32[]{:S(2)}) collective-permute-start(bf16[144,1152]{1,0:T(8,128)(2,1)S(1)} %collective-permute-done.1.refs_1_.refs_6_), channel_id=1, source_target_pairs={{0,1},{1,0},{2,3},{3,2},{4,5},{5,4},{6,7},{7,6},{8,9},{9,8},{10,11... | collective-permute-start | bytes 995336 | tf_op jit(solution)/shard_map/ppermute | solution.py:398
  13.9 8.6 %collective-permute-start.3 = (bf16[144,1152]{1,0:T(8,128)(2,1)S(1)}, bf16[144,1152]{1,0:T(8,128)(2,1)S(1)}, u32[]{:S(2)}, u32[]{:S(2)}) collective-permute-start(bf16[144,1152]{1,0:T(8,128)(2,1)S(1)} %collective-permute-done.1.refs_1_.refs_6_), channel_id=1, source_target_pairs={{0,4},{1,3},{4,8},{5,1},{8,12},{9,5},{12,14},{13,9},{14,10},{15,13... | collective-permute-start | bytes 995336 | tf_op jit(solution)/shard_map/ppermute | solution.py:392
  17.4 7.2 %collective-permute-start.13 = (bf16[144,1152]{1,0:T(8,128)(2,1)S(1)}, bf16[144,1152]{1,0:T(8,128)(2,1)S(1)}, u32[]{:S(2)}, u32[]{:S(2)}) collective-permute-start(bf16[144,1152]{1,0:T(8,128)(2,1)S(1)} %shard_map.139.refs_1_.refs_3_), channel_id=1, source_target_pairs={{0,4},{1,3},{4,8},{5,1},{8,12},{9,5},{12,14},{13,9},{14,10},{15,13... | collective-permute-start | bytes 995336 | tf_op jit(solution)/shard_map/ppermute | solution.py:392
  20.9 9.1 %collective-permute-start.2 = (bf16[144,1152]{1,0:T(8,128)(2,1)S(1)}, bf16[144,1152]{1,0:T(8,128)(2,1)S(1)}, u32[]{:S(2)}, u32[]{:S(2)}) collective-permute-start(bf16[144,1152]{1,0:T(8,128)(2,1)S(1)} %collective-permute-done.1.refs_1_.refs_6_), channel_id=1, source_target_pairs={{0,16},{16,0},{1,17},{17,1},{2,18},{18,2},{3,19},{19,3},{4,20},{20... | collective-permute-start | bytes 995336 | tf_op jit(solution)/shard_map/ppermute | solution.py:395
  22.5 9.0 %collective-permute-start.12 = (bf16[144,1152]{1,0:T(8,128)(2,1)S(1)}, bf16[144,1152]{1,0:T(8,128)(2,1)S(1)}, u32[]{:S(2)}, u32[]{:S(2)}) collective-permute-start(bf16[144,1152]{1,0:T(8,128)(2,1)S(1)} %shard_map.140.refs_1_.refs_7_), channel_id=1, source_target_pairs={{0,1},{1,0},{2,3},{3,2},{4,5},{5,4},{6,7},{7,6},{8,9},{9,8},{10,11... | collective-permute-start | bytes 995336 | tf_op jit(solution)/shard_map/ppermute | solution.py:398
  23.0 8.5 %collective-permute-start.9 = (bf16[144,1152]{1,0:T(8,128)(2,1)S(1)}, bf16[144,1152]{1,0:T(8,128)(2,1)S(1)}, u32[]{:S(2)}, u32[]{:S(2)}) collective-permute-start(bf16[144,1152]{1,0:T(8,128)(2,1)S(1)} %shard_map.140.refs_1_.refs_7_), channel_id=1, source_target_pairs={{0,4},{1,3},{4,8},{5,1},{8,12},{9,5},{12,14},{13,9},{14,10},{15,13... | collective-permute-start | bytes 995336 | tf_op jit(solution)/shard_map/ppermute | solution.py:392
  24.6 9.1 %collective-permute-start.14 = (bf16[144,1152]{1,0:T(8,128)(2,1)S(1)}, bf16[144,1152]{1,0:T(8,128)(2,1)S(1)}, u32[]{:S(2)}, u32[]{:S(2)}) collective-permute-start(bf16[144,1152]{1,0:T(8,128)(2,1)S(1)} %shard_map.142.refs_4_), channel_id=1, source_target_pairs={{0,4},{1,3},{4,8},{5,1},{8,12},{9,5},{12,14},{13,9},{14,10},{15,13... | collective-permute-start | bytes 995336 | tf_op jit(solution)/shard_map/ppermute | solution.py:392
  26.7 10.5 %collective-permute-start.19 = (bf16[144,1152]{1,0:T(8,128)(2,1)S(1)}, bf16[144,1152]{1,0:T(8,128)(2,1)S(1)}, u32[]{:S(2)}, u32[]{:S(2)}) collective-permute-start(bf16[144,1152]{1,0:T(8,128)(2,1)S(1)} %collective-permute-done.10.refs_2_.refs_18_), channel_id=1, source_target_pairs={{0,4},{1,3},{4,8},{5,1},{8,12},{9,5},{12,14},{13,9},{14,10},{15,13... | collective-permute-start | bytes 995336 | tf_op jit(solution)/shard_map/ppermute | solution.py:392
  30.0 8.1 %collective-permute-start.20 = (bf16[144,1152]{1,0:T(8,128)(2,1)S(1)}, bf16[144,1152]{1,0:T(8,128)(2,1)S(1)}, u32[]{:S(2)}, u32[]{:S(2)}) collective-permute-start(bf16[144,1152]{1,0:T(8,128)(2,1)S(1)} %shard_map.142.refs_4_), channel_id=1, source_target_pairs={{0,16},{16,0},{1,17},{17,1},{2,18},{18,2},{3,19},{19,3},{4,20},{20... | collective-permute-start | bytes 995336 | tf_op jit(solution)/shard_map/ppermute | solution.py:395
  31.5 6.6 %collective-permute-start.18 = (bf16[144,1152]{1,0:T(8,128)(2,1)S(1)}, bf16[144,1152]{1,0:T(8,128)(2,1)S(1)}, u32[]{:S(2)}, u32[]{:S(2)}) collective-permute-start(bf16[144,1152]{1,0:T(8,128)(2,1)S(1)} %collective-permute-done.9.refs_4_.refs_2_.refs_8_), channel_id=1, source_target_pairs={{0,1},{1,0},{2,3},{3,2},{4,5},{5,4},{6,7},{7,6},{8,9},{9,8},{10,11... | collective-permute-start | bytes 995336 | tf_op jit(solution)/shard_map/ppermute | solution.py:398
  33.6 4.9 %collective-permute-start.17 = (bf16[144,1152]{1,0:T(8,128)(2,1)S(1)}, bf16[144,1152]{1,0:T(8,128)(2,1)S(1)}, u32[]{:S(2)}, u32[]{:S(2)}) collective-permute-start(bf16[144,1152]{1,0:T(8,128)(2,1)S(1)} %shard_map.143.refs_5_), channel_id=1, source_target_pairs={{0,1},{1,0},{2,3},{3,2},{4,5},{5,4},{6,7},{7,6},{8,9},{9,8},{10,11... | collective-permute-start | bytes 995336 | tf_op jit(solution)/shard_map/ppermute | solution.py:398
  33.6 7.1 %collective-permute-start.22 = (bf16[144,1152]{1,0:T(8,128)(2,1)S(1)}, bf16[144,1152]{1,0:T(8,128)(2,1)S(1)}, u32[]{:S(2)}, u32[]{:S(2)}) collective-permute-start(bf16[144,1152]{1,0:T(8,128)(2,1)S(1)} %get-tuple-element.32.refs_1_.refs_22_), channel_id=1, source_target_pairs={{0,4},{1,3},{4,8},{5,1},{8,12},{9,5},{12,14},{13,9},{14,10},{15,13... | collective-permute-start | bytes 995336 | tf_op jit(solution)/shard_map/ppermute | solution.py:392
  37.2 5.1 %collective-permute-start.15 = (bf16[144,1152]{1,0:T(8,128)(2,1)S(1)}, bf16[144,1152]{1,0:T(8,128)(2,1)S(1)}, u32[]{:S(2)}, u32[]{:S(2)}) collective-permute-start(bf16[144,1152]{1,0:T(8,128)(2,1)S(1)} %shard_map.139.refs_1_.refs_3_), channel_id=1, source_target_pairs={{0,1},{1,0},{2,3},{3,2},{4,5},{5,4},{6,7},{7,6},{8,9},{9,8},{10,11... | collective-permute-start | bytes 995336 | tf_op jit(solution)/shard_map/ppermute | solution.py:398
  38.1 4.8 %collective-permute-start.16 = (bf16[144,1152]{1,0:T(8,128)(2,1)S(1)}, bf16[144,1152]{1,0:T(8,128)(2,1)S(1)}, u32[]{:S(2)}, u32[]{:S(2)}) collective-permute-start(bf16[144,1152]{1,0:T(8,128)(2,1)S(1)} %shard_map.142.refs_4_), channel_id=1, source_target_pairs={{0,1},{1,0},{2,3},{3,2},{4,5},{5,4},{6,7},{7,6},{8,9},{9,8},{10,11... | collective-permute-start | bytes 995336 | tf_op jit(solution)/shard_map/ppermute | solution.py:398
  38.6 9.8 %collective-permute-start.21 = (bf16[144,1152]{1,0:T(8,128)(2,1)S(1)}, bf16[144,1152]{1,0:T(8,128)(2,1)S(1)}, u32[]{:S(2)}, u32[]{:S(2)}) collective-permute-start(bf16[144,1152]{1,0:T(8,128)(2,1)S(1)} %shard_map.143.refs_5_), channel_id=1, source_target_pairs={{0,16},{16,0},{1,17},{17,1},{2,18},{18,2},{3,19},{19,3},{4,20},{20... | collective-permute-start | bytes 995336 | tf_op jit(solution)/shard_map/ppermute | solution.py:395
  40.8 7.6 %collective-permute-start.23 = (bf16[144,1152]{1,0:T(8,128)(2,1)S(1)}, bf16[144,1152]{1,0:T(8,128)(2,1)S(1)}, u32[]{:S(2)}, u32[]{:S(2)}) collective-permute-start(bf16[144,1152]{1,0:T(8,128)(2,1)S(1)} %shard_map.144.refs_23_), channel_id=1, source_target_pairs={{0,4},{1,3},{4,8},{5,1},{8,12},{9,5},{12,14},{13,9},{14,10},{15,13... | collective-permute-start | bytes 995336 | tf_op jit(solution)/shard_map/ppermute | solution.py:392
  42.3 6.5 %collective-permute-start.27 = (bf16[144,1152]{1,0:T(8,128)(2,1)S(1)}, bf16[144,1152]{1,0:T(8,128)(2,1)S(1)}, u32[]{:S(2)}, u32[]{:S(2)}) collective-permute-start(bf16[144,1152]{1,0:T(8,128)(2,1)S(1)} %get-tuple-element.32.refs_1_.refs_22_), channel_id=1, source_target_pairs={{0,1},{1,0},{2,3},{3,2},{4,5},{5,4},{6,7},{7,6},{8,9},{9,8},{10,11... | collective-permute-start | bytes 995336 | tf_op jit(solution)/shard_map/ppermute | solution.py:398
  42.4 6.4 %collective-permute-start.25 = (bf16[144,1152]{1,0:T(8,128)(2,1)S(1)}, bf16[144,1152]{1,0:T(8,128)(2,1)S(1)}, u32[]{:S(2)}, u32[]{:S(2)}) collective-permute-start(bf16[144,1152]{1,0:T(8,128)(2,1)S(1)} %collective-permute-done.20.refs_3_.refs_20_), channel_id=1, source_target_pairs={{0,1},{1,0},{2,3},{3,2},{4,5},{5,4},{6,7},{7,6},{8,9},{9,8},{10,11... | collective-permute-start | bytes 995336 | tf_op jit(solution)/shard_map/ppermute | solution.py:398
  42.9 7.1 %collective-permute-start.28 = (bf16[144,1152]{1,0:T(8,128)(2,1)S(1)}, bf16[144,1152]{1,0:T(8,128)(2,1)S(1)}, u32[]{:S(2)}, u32[]{:S(2)}) collective-permute-start(bf16[144,1152]{1,0:T(8,128)(2,1)S(1)} %shard_map.144.refs_23_), channel_id=1, source_target_pairs={{0,1},{1,0},{2,3},{3,2},{4,5},{5,4},{6,7},{7,6},{8,9},{9,8},{10,11... | collective-permute-start | bytes 995336 | tf_op jit(solution)/shard_map/ppermute | solution.py:398
  59.6 7.5 %collective-permute-start.31 = (bf16[32,2304]{1,0:T(8,128)(2,1)S(1)}, bf16[32,2304]{1,0:T(8,128)(2,1)S(1)}, u32[]{:S(2)}, u32[]{:S(2)}) collective-permute-start(bf16[32,2304]{1,0:T(8,128)(2,1)S(1)} %get-tuple-element.36), channel_id=1, source_target_pairs={{0,2},{1,3},{2,0},{3,1},{4,6},{5,7},{6,4},{7,5},{8,10},{9,11},{10,... | collective-permute-start | bytes 442376 | tf_op jit(solution)/shard_map/ppermute | solution.py:554
  62.9 6.7 %collective-permute-start.32 = (bf16[32,2304]{1,0:T(8,128)(2,1)S(1)}, bf16[32,2304]{1,0:T(8,128)(2,1)S(1)}, u32[]{:S(2)}, u32[]{:S(2)}) collective-permute-start(bf16[32,2304]{1,0:T(8,128)(2,1)S(1)} %get-tuple-element.37), channel_id=1, source_target_pairs={{0,4},{1,5},{2,6},{3,7},{4,0},{5,1},{6,2},{7,3},{8,12},{9,13},{10,... | collective-permute-start | bytes 442376 | tf_op jit(solution)/shard_map/ppermute | solution.py:554
  64.1 7.4 %collective-permute-start.33 = (bf16[32,2304]{1,0:T(8,128)(2,1)S(1)}, bf16[32,2304]{1,0:T(8,128)(2,1)S(1)}, u32[]{:S(2)}, u32[]{:S(2)}) collective-permute-start(bf16[32,2304]{1,0:T(8,128)(2,1)S(1)} %get-tuple-element.38), channel_id=1, source_target_pairs={{0,6},{1,7},{2,4},{3,5},{4,2},{5,3},{6,0},{7,1},{8,14},{9,15},{10,... | collective-permute-start | bytes 442376 | tf_op jit(solution)/shard_map/ppermute | solution.py:554
  75.3 6.0 %collective-permute-start.35 = (bf16[32,2304]{1,0:T(8,128)(2,1)S(1)}, bf16[32,2304]{1,0:T(8,128)(2,1)S(1)}, u32[]{:S(2)}, u32[]{:S(2)}) collective-permute-start(bf16[32,2304]{1,0:T(8,128)(2,1)S(1)} %get-tuple-element.42), channel_id=1, source_target_pairs={{0,2},{1,3},{2,0},{3,1},{4,6},{5,7},{6,4},{7,5},{8,10},{9,11},{10,... | collective-permute-start | bytes 442376 | tf_op jit(solution)/shard_map/ppermute | solution.py:554
  77.1 6.7 %collective-permute-start.36 = (bf16[32,2304]{1,0:T(8,128)(2,1)S(1)}, bf16[32,2304]{1,0:T(8,128)(2,1)S(1)}, u32[]{:S(2)}, u32[]{:S(2)}) collective-permute-start(bf16[32,2304]{1,0:T(8,128)(2,1)S(1)} %get-tuple-element.43), channel_id=1, source_target_pairs={{0,4},{1,5},{2,6},{3,7},{4,0},{5,1},{6,2},{7,3},{8,12},{9,13},{10,... | collective-permute-start | bytes 442376 | tf_op jit(solution)/shard_map/ppermute | solution.py:554
  78.3 7.4 %collective-permute-start.37 = (bf16[32,2304]{1,0:T(8,128)(2,1)S(1)}, bf16[32,2304]{1,0:T(8,128)(2,1)S(1)}, u32[]{:S(2)}, u32[]{:S(2)}) collective-permute-start(bf16[32,2304]{1,0:T(8,128)(2,1)S(1)} %get-tuple-element.44), channel_id=1, source_target_pairs={{0,6},{1,7},{2,4},{3,5},{4,2},{5,3},{6,0},{7,1},{8,14},{9,15},{10,... | collective-permute-start | bytes 442376 | tf_op jit(solution)/shard_map/ppermute | solution.py:554
  90.5 13.0 %all-to-all-start = ((bf16[32,2,1152]{2,1,0:T(2,128)(2,1)}), bf16[32,2,1152]{2,1,0:T(2,128)(2,1)S(1)}, u32[]{:S(2)}, u32[]{:S(2)}) async-start(bf16[32,2,1152]{2,1,0:T(2,128)(2,1)} %get-tuple-element.54), calls=%async_computation | async-start | bytes 294912 | tf_op jit(solution)/shard_map/all_to_all | solution.py:589
  (15 other events, 209.7 us)
